TPU v7x, 128 devices: a whole 4x4x4 slice. The times are simulated.
128 devices in a mesh: dp: 16 (over y, x), segment: 4 (over z), mp: 2 (over core).
Axes of the slice: x: 4, y: 4, z: 4, core: 2. Of those that a mesh axis runs over, the one named last changes fastest.
Arguments:
- trunk_in: bfloat16 [4096, 2560], P('dp', 'mp'), may hold values from -6 to 6
- norm_gain: bfloat16 [4, 2560], P('segment'), may hold values from 0.5 to 1.5
- w_gate: bfloat16 [4, 2560, 3584], P('segment', 'dp', 'mp'), may hold values from -0.125 to 0.125
- w_up: bfloat16 [4, 2560, 3584], P('segment', 'dp', 'mp'), may hold values from -0.125 to 0.125
- w_down: bfloat16 [4, 3584, 2560], P('segment', 'mp', 'dp'), may hold values from -0.09375 to 0.09375
- w_cond: bfloat16 [2560, 512], P('mp'), may hold values from -0.125 to 0.125
- w_time: bfloat16 [256, 512], replicated, may hold values from -0.375 to 0.375
- w_in: bfloat16 [70, 256], replicated, may hold values from -0.75 to 0.75
- w_mid: bfloat16 [1280, 256], replicated, may hold values from -0.15625 to 0.15625
- w_res: bfloat16 [14, 256], replicated, may hold values from -1.5 to 1.5
- w_out: bfloat16 [256, 14], replicated, may hold values from -0.375 to 0.375
- tsteps: int32 [256, 8], P('dp'), may hold values from 0 to 99
- advantage: float32 [256, 8], P('dp'), may hold values from -4 to 4
- actions: bfloat16 [256, 64, 14], P('dp'), may hold values from -6 to 6
- noise: bfloat16 [256, 8, 64, 14], P('dp'), may hold values from -6 to 6
Outputs:
- grad_w_in: float32 [70, 256], P(None, 'segment')
- grad_w_mid: float32 [1280, 256], P(None, 'segment')
- grad_w_res: float32 [14, 256], P(None, 'segment')
- grad_w_out: float32 [256, 14], P('segment')
- grad_w_time: float32 [256, 512], P(None, 'segment')
- grad_w_cond: float32 [2560, 512], P('mp', 'segment')
- grad_cond: float32 [256, 2560], P(('dp', 'segment'), 'mp')
- loss: float32 [1], replicated
All inputs are finite; a program needn't handle non-finite values.
Results may differ from a plain program's by a relative error of at most 0.035.
Values may be sent and summed in bfloat16 or wider, within the bound.
A program may use at most 128 MiB of HBM per device.

v0:
```python
import math

import jax
import jax.numpy as jnp
from jax import lax
from jax.sharding import PartitionSpec as P

GROUPS = 8
TSTEPS = 100
TPS = 16
SPM = 4
SPD = 16
LEV = 8


def passed_along(block, axis, distance):
    devices = range(lax.axis_size(axis))
    route = [(i - distance, i) for i in devices if i - distance in devices]
    return lax.ppermute(block, axis, route)


def spread_2(value, axis, source):
    kept = jnp.where(lax.axis_index(axis) == source, value, 0).astype(value.dtype)
    return lax.psum(kept, axis)


def mish_value(values):
    return values * jnp.tanh(jax.nn.softplus(values))


def mish_slope(values):
    soft = jnp.tanh(jax.nn.softplus(values))
    return soft + values * jax.nn.sigmoid(values) * (1.0 - soft * soft)


def contract(form, left, right):
    return jnp.einsum(form, left, right, preferred_element_type=jnp.float32)


def alpha_table():
    grid = jnp.arange(TSTEPS + 1, dtype=jnp.float32) / TSTEPS
    curve = jnp.cos((grid + 0.008) / 1.008 * math.pi / 2.0) ** 2
    betas = jnp.minimum(1.0 - curve[1:] / curve[:-1], 0.999)
    return jnp.cumprod(1.0 - betas)


def norm_act(values):
    rows, steps, channels = values.shape
    grouped = values.reshape(rows, steps, GROUPS, channels // GROUPS)
    center = jnp.mean(grouped, axis=(1, 3), keepdims=True)
    spread = jnp.mean((grouped - center) ** 2, axis=(1, 3), keepdims=True)
    normed = (grouped - center) * lax.rsqrt(spread + 1e-05)
    return mish_value(normed.reshape(rows, steps, channels))


def columns(values):
    steps = values.shape[1]
    padded = jnp.pad(values, ((0, 0), (2, 2), (0, 0)))
    return jnp.concatenate([padded[:, tap : tap + steps] for tap in range(5)], axis=2)


def columns_adjoint(grads, width):
    total = 0.0
    for tap in range(5):
        piece = grads[:, :, tap * width : (tap + 1) * width]
        total = total + jnp.pad(piece, ((0, 0), (tap, 4 - tap), (0, 0)))
    return total[:, 2:-2]


def own_block(values, which, count, axis_number):
    width = values.shape[axis_number] // count
    return lax.dynamic_slice_in_dim(values, which * width, width, axis_number)


def denoise(
    film_cond, tsteps, advantage, actions, noise, w_in, w_mid, w_res, w_out, w_time, product
):
    row_count, levels = tsteps.shape
    horizon, action_dims = (actions.shape[1], actions.shape[2])
    channels = w_mid.shape[1]
    flat = row_count * levels
    matches = (tsteps[:, :, None] == jnp.arange(TSTEPS, dtype=jnp.int32)[None, None, :]).astype(
        jnp.float32
    )
    alpha = jnp.sum(matches * alpha_table()[None, None, :], axis=2)
    keep_root = jnp.sqrt(alpha)[:, :, None, None]
    noise_root = jnp.sqrt(1.0 - alpha)[:, :, None, None]
    noisy_act = (
        keep_root * actions.astype(jnp.float32)[:, None] + noise_root * noise.astype(jnp.float32)
    ).astype(jnp.bfloat16)
    noisy_act = noisy_act.reshape(flat, horizon, action_dims)
    half_dim = w_time.shape[0] // 2
    frequencies = jnp.exp(
        -math.log(10000.0) * jnp.arange(half_dim, dtype=jnp.float32) / (half_dim - 1)
    )
    angles = tsteps.astype(jnp.float32)[:, :, None] * frequencies[None, None, :]
    embedded = jnp.concatenate([jnp.sin(angles), jnp.cos(angles)], axis=2)
    time_act = mish_value(embedded).astype(jnp.bfloat16).reshape(flat, 2 * half_dim)
    film = film_cond[:, None, :] + product(
        "rld,dc->rlc", time_act.reshape(row_count, levels, -1), w_time
    )
    film = film.reshape(flat, 2 * channels)
    film_scale = film[:, None, :channels]
    film_shift = film[:, None, channels:]
    columns_in = columns(noisy_act)
    pre_first = product("mhk,kc->mhc", columns_in, w_in)
    act_first, first_back = jax.vjp(norm_act, pre_first)
    modulated = (film_scale * act_first + film_shift).astype(jnp.bfloat16)
    columns_mid = columns(modulated)
    pre_second = product("mhk,kc->mhc", columns_mid, w_mid)
    act_second, second_back = jax.vjp(norm_act, pre_second)
    block_out = (act_second + product("mha,ac->mhc", noisy_act, w_res)).astype(jnp.bfloat16)
    predicted = product("mhc,ca->mha", block_out, w_out)
    errors = predicted - noise.reshape(flat, horizon, action_dims).astype(jnp.float32)
    err_sum = jnp.sum(errors * errors) / (horizon * action_dims)
    weights = advantage.reshape(flat, 1, 1)
    d_pred = (2.0 * weights * errors / (horizon * action_dims)).astype(jnp.bfloat16)
    grad_out = product("mhc,mha->ca", block_out, d_pred)
    d_block = product("mha,ca->mhc", d_pred, w_out)
    grad_res = product("mha,mhc->ac", noisy_act, d_block.astype(jnp.bfloat16))
    d_second = second_back(d_block)[0].astype(jnp.bfloat16)
    grad_mid = product("mhk,mhc->kc", columns_mid, d_second)
    d_columns = product("mhc,kc->mhk", d_second, w_mid)
    d_modulated = columns_adjoint(d_columns, channels)
    d_film = jnp.concatenate(
        [jnp.sum(d_modulated * act_first, axis=1), jnp.sum(d_modulated, axis=1)], axis=1
    )
    d_first = first_back(film_scale * d_modulated)[0].astype(jnp.bfloat16)
    grad_in = product("mhk,mhc->kc", columns_in, d_first)
    grad_time = product("md,mc->dc", time_act, d_film.astype(jnp.bfloat16))
    d_film_cond = jnp.sum(d_film.reshape(row_count, levels, -1), axis=1)
    return (err_sum, grad_in, grad_mid, grad_res, grad_out, grad_time, d_film_cond)


def body(
    trunk_in,
    norm_gain,
    w_gate,
    w_up,
    w_down,
    w_cond,
    w_time,
    w_in,
    w_mid,
    w_res,
    w_out,
    tsteps,
    advantage,
    actions,
    noise,
):
    segments = lax.axis_size("segment")
    segment_index = lax.axis_index("segment")
    cores = lax.axis_size("mp")
    core_index = lax.axis_index("mp")
    gate_full, up_full, down_full = (
        lax.all_gather(w_gate, "dp", axis=1, tiled=True),
        lax.all_gather(w_up, "dp", axis=1, tiled=True),
        lax.all_gather(w_down, "dp", axis=2, tiled=True),
    )
    gate_weight = gate_full[0]
    up_weight = up_full[0]
    down_weight = down_full[0]
    norm_scale = norm_gain[0].astype(jnp.float32)
    micro_count = SPD // SPM
    batch_rows = SPM * TPS
    half_width = trunk_in.shape[1]
    inputs = trunk_in.reshape(micro_count, batch_rows, half_width)

    def trunk_layer(current):
        whole_rows = lax.all_gather(current, "mp", axis=1, tiled=True)
        widened = whole_rows.astype(jnp.float32)
        factor = lax.rsqrt(jnp.mean(widened * widened, axis=1, keepdims=True) + 1e-05)
        normed = (widened * factor * norm_scale).astype(jnp.bfloat16)
        gate_out = jnp.dot(normed, gate_weight, preferred_element_type=jnp.float32)
        up_out = jnp.dot(normed, up_weight, preferred_element_type=jnp.float32)
        hidden = (jax.nn.silu(gate_out) * up_out).astype(jnp.bfloat16)
        partial_out = jnp.dot(hidden, down_weight, preferred_element_type=jnp.float32)
        summed = lax.psum_scatter(
            partial_out.astype(jnp.bfloat16), "mp", scatter_dimension=1, tiled=True
        ).astype(jnp.float32)
        return (current.astype(jnp.float32) + summed).astype(jnp.bfloat16)

    def advance(step_index, loop_state):
        received, stored = loop_state
        fresh_rows = lax.dynamic_index_in_dim(
            inputs, jnp.minimum(step_index, micro_count - 1), 0, keepdims=False
        )
        fresh_rows = jnp.where(step_index < micro_count, fresh_rows, jnp.zeros_like(fresh_rows))
        current = jnp.where(segment_index == 0, fresh_rows, received)
        result = trunk_layer(current)
        slot_index = jnp.clip(step_index - (segments - 1), 0, micro_count - 1)
        previous = lax.dynamic_index_in_dim(stored, slot_index, 0, keepdims=False)
        kept_rows = jnp.where(step_index >= segments - 1, result, previous)
        stored = lax.dynamic_update_index_in_dim(stored, kept_rows, slot_index, 0)
        received = passed_along(result, "segment", 1)
        return (received, stored)

    start_state = (
        jnp.zeros((batch_rows, half_width), jnp.bfloat16),
        jnp.zeros((micro_count, batch_rows, half_width), jnp.bfloat16),
    )
    final_state = lax.fori_loop(0, micro_count + segments - 1, advance, start_state)
    trunk_out = final_state[1].reshape(SPD, TPS, half_width)
    cond = jnp.mean(trunk_out.astype(jnp.float32), axis=1).astype(jnp.bfloat16)
    is_last = (segment_index == segments - 1).astype(jnp.float32)
    row_total = cond.shape[0]
    own_rows = row_total // cores
    cond_act = mish_value(cond.astype(jnp.float32)).astype(jnp.bfloat16)
    film_cond = lax.psum_scatter(
        jnp.dot(cond_act, w_cond, preferred_element_type=jnp.float32).astype(jnp.bfloat16),
        "mp",
        scatter_dimension=0,
        tiled=True,
    ).astype(jnp.float32)
    begin_row = core_index * own_rows
    steps_own = lax.dynamic_slice_in_dim(tsteps, begin_row, own_rows, 0)
    advantage_own = lax.dynamic_slice_in_dim(advantage, begin_row, own_rows, 0)
    actions_own = lax.dynamic_slice_in_dim(actions, begin_row, own_rows, 0)
    noise_own = lax.dynamic_slice_in_dim(noise, begin_row, own_rows, 0)
    outcome = denoise(
        film_cond,
        steps_own,
        advantage_own,
        actions_own,
        noise_own,
        w_in,
        w_mid,
        w_res,
        w_out,
        w_time,
        contract,
    )
    err_sum, grad_in, grad_mid, grad_res, grad_out, grad_time, d_film_cond = outcome
    film_share = (d_film_cond * is_last).astype(jnp.bfloat16)
    film_all = lax.all_gather(film_share, "mp", axis=0, tiled=True)
    cond_grad_part = contract("sc,dc->sd", film_all, w_cond) * mish_slope(cond.astype(jnp.float32))
    grad_cond = lax.psum_scatter(
        cond_grad_part.astype(jnp.bfloat16), "segment", scatter_dimension=0, tiled=True
    ).astype(jnp.float32)
    local_sums = (
        lax.psum(grad_in.astype(jnp.bfloat16), ("dp", "mp")).astype(jnp.float32),
        lax.psum(grad_mid.astype(jnp.bfloat16), ("dp", "mp")).astype(jnp.float32),
        lax.psum(grad_res.astype(jnp.bfloat16), ("dp", "mp")).astype(jnp.float32),
        lax.psum(grad_out.astype(jnp.bfloat16), ("dp", "mp")).astype(jnp.float32),
        lax.psum(grad_time.astype(jnp.bfloat16), ("dp", "mp")).astype(jnp.float32),
        lax.psum(err_sum.astype(jnp.bfloat16), ("dp", "mp")).astype(jnp.float32),
    )
    cond_weight_part = contract("sd,sc->dc", cond_act, film_all)
    local_cond = lax.psum(cond_weight_part.astype(jnp.bfloat16), "dp").astype(jnp.float32)
    fanned = (
        spread_2(local_sums[0].astype(jnp.bfloat16), "segment", segments - 1).astype(jnp.float32),
        spread_2(local_sums[1].astype(jnp.bfloat16), "segment", segments - 1).astype(jnp.float32),
        spread_2(local_sums[2].astype(jnp.bfloat16), "segment", segments - 1).astype(jnp.float32),
        spread_2(local_sums[3].astype(jnp.bfloat16), "segment", segments - 1).astype(jnp.float32),
        spread_2(local_sums[4].astype(jnp.bfloat16), "segment", segments - 1).astype(jnp.float32),
        spread_2(local_sums[5].astype(jnp.bfloat16), "segment", segments - 1).astype(jnp.float32),
        spread_2(local_cond.astype(jnp.bfloat16), "segment", segments - 1).astype(local_cond.dtype),
    )
    summed_grads = fanned[:6]
    grad_w_cond = own_block(fanned[6], segment_index, segments, 1)
    replicas = lax.axis_size("dp")
    loss = (summed_grads[5] / (replicas * SPD * LEV)).reshape(1)
    return (
        own_block(summed_grads[0], segment_index, segments, 1),
        own_block(summed_grads[1], segment_index, segments, 1),
        own_block(summed_grads[2], segment_index, segments, 1),
        own_block(summed_grads[3], segment_index, segments, 0),
        own_block(summed_grads[4], segment_index, segments, 1),
        grad_w_cond,
        grad_cond,
        loss,
    )


def solution(mesh):
    in_specs = (
        P("dp", "mp"),
        P("segment", None),
        P("segment", "dp", "mp"),
        P("segment", "dp", "mp"),
        P("segment", "mp", "dp"),
        P("mp", None),
        P(),
        P(),
        P(),
        P(),
        P(),
        P("dp", None),
        P("dp", None),
        P("dp", None, None),
        P("dp", None, None, None),
    )
    out_specs = (
        P(None, "segment"),
        P(None, "segment"),
        P(None, "segment"),
        P("segment", None),
        P(None, "segment"),
        P("mp", "segment"),
        P(("dp", "segment"), "mp"),
        P(),
    )
    return jax.shard_map(body, mesh=mesh, in_specs=in_specs, out_specs=out_specs, check_vma=False)
```

profile of v0, /device:TPU:1, one launch (start us, length us, event | category | flops | bytes accessed | tf_op | source)
XLA Modules:
  0.0 996.6 jit_solution(12484185076508162451)
XLA Ops:
  16.7 6.4 concatenate.15
  23.1 4.0 fusion.92
  33.7 53.9 %all-gather.8.cloned.1.call-done = bf16[1,1792,2560]{1,2,0:T(8,128)(2,1)} async-done(((bf16[1,1792,160]{1,2,0:T(8,128)(2,1)}), bf16[1,1792,2560]{1,2,0:T(8,128)(2,1)}) %all-gather.8.cloned.1.call-update) | async-done | bytes 9175056 | tf_op jit(solution)/shard_map/all_gather | solution.py:159
  87.6 12.9 %copy.100 = bf16[1792,2560]{1,0:T(8,128)(2,1)} copy(bf16[1792,2560]{0,1:T(8,128)(2,1)} %bitcast.131) | data formatting | bytes 18350080 | tf_op jit(solution)/shard_map/while | solution.py:203
  100.5 63.2 %all-gather.4.cloned.1.call-done = bf16[1,2560,1792]{2,1,0:T(8,128)(2,1)} async-done(((bf16[1,160,1792]{2,1,0:T(8,128)(2,1)}), bf16[1,2560,1792]{2,1,0:T(8,128)(2,1)}) %all-gather.4.cloned.1.call-update) | async-done | bytes 9175056 | tf_op jit(solution)/shard_map/all_gather | solution.py:157
  163.7 76.1 %all-gather.6.cloned.1.call-done = bf16[1,2560,1792]{2,1,0:T(8,128)(2,1)} async-done(((bf16[1,160,1792]{2,1,0:T(8,128)(2,1)}), bf16[1,2560,1792]{2,1,0:T(8,128)(2,1)}) %all-gather.6.cloned.1.call-update) | async-done | bytes 9175056 | tf_op jit(solution)/shard_map/all_gather | solution.py:158
  240.7 282.4 %while.17 = (s32[]{:T(128)}, bf16[64,1280]{1,0:T(8,128)(2,1)S(1)}, bf16[4,64,1280]{2,1,0:T(8,128)(2,1)}, pred[]{:T(512)}, bf16[4,64,1280]{2,1,0:T(8,128)(2,1)}, ...) while((s32[]{:T(128)}, bf16[64,1280]{1,0:T(8,128)(2,1)S(1)}, ...), condition=%wide.region_5.6_spmd, body=%wide.region_2.5_spmd.sunk | while | flops 1764835328 | bytes 34035272 | solution.py:203
  244.2 5.4 fusion.125
  249.6 10.3 %convolution_convert_fusion.5 = bf16[64,2560]{1,0:T(8,128)(2,1)} fusion(bf16[1792,2560]{1,0:T(8,128)(2,1)} %get-tuple-element.426, bf16[2560,1792]{1,0:T(8,128)(2,1)} %get-tuple-element.425, f32[64,1792]{1,0:T(8,128)S(1)} %fusion.125, bf16[64,2560]{1,0:T(8,128)(2,1)S(1)} %all_gather.27, f32[2560]{0:T(1024)S(1)} %get-tuple-element.423, ...), kind=kOutput, calls=%fused_computation.clone.1 | convolution fusion | flops 1175912448 | bytes 19474688 | tf_op jit(solution)/shard_map/while/body/eval_jaxpr/dot_general | solution.py:178
  260.9 9.5 reduce-scatter.5.cloned.1.call-done
  275.3 3.4 collective-permute-done
  282.4 5.4 fusion.125
  287.8 10.3 %convolution_convert_fusion.5 = bf16[64,2560]{1,0:T(8,128)(2,1)} fusion(bf16[1792,2560]{1,0:T(8,128)(2,1)} %get-tuple-element.426, bf16[2560,1792]{1,0:T(8,128)(2,1)} %get-tuple-element.425, f32[64,1792]{1,0:T(8,128)S(1)} %fusion.125, bf16[64,2560]{1,0:T(8,128)(2,1)S(1)} %all_gather.27, f32[2560]{0:T(1024)S(1)} %get-tuple-element.423, ...), kind=kOutput, calls=%fused_computation.clone.1 | convolution fusion | flops 1175912448 | bytes 19474688 | tf_op jit(solution)/shard_map/while/body/eval_jaxpr/dot_general | solution.py:178
  299.1 12.0 %reduce-scatter.5.cloned.1.call-done = bf16[64,1280]{1,0:T(8,128)(2,1)} async-done(((bf16[64,2560]{1,0:T(8,128)(2,1)}), bf16[64,1280]{1,0:T(8,128)(2,1)}) %reduce-scatter.5.cloned.1.call-update) | async-done | bytes 163856 | tf_op jit(solution)/shard_map/while/body/eval_jaxpr/reduce_scatter | solution.py:179
  316.0 3.4 collective-permute-done
  323.2 5.4 fusion.125
  328.5 10.3 %convolution_convert_fusion.5 = bf16[64,2560]{1,0:T(8,128)(2,1)} fusion(bf16[1792,2560]{1,0:T(8,128)(2,1)} %get-tuple-element.426, bf16[2560,1792]{1,0:T(8,128)(2,1)} %get-tuple-element.425, f32[64,1792]{1,0:T(8,128)S(1)} %fusion.125, bf16[64,2560]{1,0:T(8,128)(2,1)S(1)} %all_gather.27, f32[2560]{0:T(1024)S(1)} %get-tuple-element.423, ...), kind=kOutput, calls=%fused_computation.clone.1 | convolution fusion | flops 1175912448 | bytes 19474688 | tf_op jit(solution)/shard_map/while/body/eval_jaxpr/dot_general | solution.py:178
  339.8 12.0 %reduce-scatter.5.cloned.1.call-done = bf16[64,1280]{1,0:T(8,128)(2,1)} async-done(((bf16[64,2560]{1,0:T(8,128)(2,1)}), bf16[64,1280]{1,0:T(8,128)(2,1)}) %reduce-scatter.5.cloned.1.call-update) | async-done | bytes 163856 | tf_op jit(solution)/shard_map/while/body/eval_jaxpr/reduce_scatter | solution.py:179
  356.7 3.4 collective-permute-done
  363.9 5.4 fusion.125
  369.3 10.3 %convolution_convert_fusion.5 = bf16[64,2560]{1,0:T(8,128)(2,1)} fusion(bf16[1792,2560]{1,0:T(8,128)(2,1)} %get-tuple-element.426, bf16[2560,1792]{1,0:T(8,128)(2,1)} %get-tuple-element.425, f32[64,1792]{1,0:T(8,128)S(1)} %fusion.125, bf16[64,2560]{1,0:T(8,128)(2,1)S(1)} %all_gather.27, f32[2560]{0:T(1024)S(1)} %get-tuple-element.423, ...), kind=kOutput, calls=%fused_computation.clone.1 | convolution fusion | flops 1175912448 | bytes 19474688 | tf_op jit(solution)/shard_map/while/body/eval_jaxpr/dot_general | solution.py:178
  380.6 12.0 %reduce-scatter.5.cloned.1.call-done = bf16[64,1280]{1,0:T(8,128)(2,1)} async-done(((bf16[64,2560]{1,0:T(8,128)(2,1)}), bf16[64,1280]{1,0:T(8,128)(2,1)}) %reduce-scatter.5.cloned.1.call-update) | async-done | bytes 163856 | tf_op jit(solution)/shard_map/while/body/eval_jaxpr/reduce_scatter | solution.py:179
  397.5 3.4 collective-permute-done
  404.7 5.4 fusion.125
  410.0 10.3 %convolution_convert_fusion.5 = bf16[64,2560]{1,0:T(8,128)(2,1)} fusion(bf16[1792,2560]{1,0:T(8,128)(2,1)} %get-tuple-element.426, bf16[2560,1792]{1,0:T(8,128)(2,1)} %get-tuple-element.425, f32[64,1792]{1,0:T(8,128)S(1)} %fusion.125, bf16[64,2560]{1,0:T(8,128)(2,1)S(1)} %all_gather.27, f32[2560]{0:T(1024)S(1)} %get-tuple-element.423, ...), kind=kOutput, calls=%fused_computation.clone.1 | convolution fusion | flops 1175912448 | bytes 19474688 | tf_op jit(solution)/shard_map/while/body/eval_jaxpr/dot_general | solution.py:178
  421.3 12.0 %reduce-scatter.5.cloned.1.call-done = bf16[64,1280]{1,0:T(8,128)(2,1)} async-done(((bf16[64,2560]{1,0:T(8,128)(2,1)}), bf16[64,1280]{1,0:T(8,128)(2,1)}) %reduce-scatter.5.cloned.1.call-update) | async-done | bytes 163856 | tf_op jit(solution)/shard_map/while/body/eval_jaxpr/reduce_scatter | solution.py:179
  445.4 5.4 fusion.125
  450.8 10.3 %convolution_convert_fusion.5 = bf16[64,2560]{1,0:T(8,128)(2,1)} fusion(bf16[1792,2560]{1,0:T(8,128)(2,1)} %get-tuple-element.426, bf16[2560,1792]{1,0:T(8,128)(2,1)} %get-tuple-element.425, f32[64,1792]{1,0:T(8,128)S(1)} %fusion.125, bf16[64,2560]{1,0:T(8,128)(2,1)S(1)} %all_gather.27, f32[2560]{0:T(1024)S(1)} %get-tuple-element.423, ...), kind=kOutput, calls=%fused_computation.clone.1 | convolution fusion | flops 1175912448 | bytes 19474688 | tf_op jit(solution)/shard_map/while/body/eval_jaxpr/dot_general | solution.py:178
  462.1 12.0 %reduce-scatter.5.cloned.1.call-done = bf16[64,1280]{1,0:T(8,128)(2,1)} async-done(((bf16[64,2560]{1,0:T(8,128)(2,1)}), bf16[64,1280]{1,0:T(8,128)(2,1)}) %reduce-scatter.5.cloned.1.call-update) | async-done | bytes 163856 | tf_op jit(solution)/shard_map/while/body/eval_jaxpr/reduce_scatter | solution.py:179
  486.1 5.4 fusion.125
  491.5 10.3 %convolution_convert_fusion.5 = bf16[64,2560]{1,0:T(8,128)(2,1)} fusion(bf16[1792,2560]{1,0:T(8,128)(2,1)} %get-tuple-element.426, bf16[2560,1792]{1,0:T(8,128)(2,1)} %get-tuple-element.425, f32[64,1792]{1,0:T(8,128)S(1)} %fusion.125, bf16[64,2560]{1,0:T(8,128)(2,1)S(1)} %all_gather.27, f32[2560]{0:T(1024)S(1)} %get-tuple-element.423, ...), kind=kOutput, calls=%fused_computation.clone.1 | convolution fusion | flops 1175912448 | bytes 19474688 | tf_op jit(solution)/shard_map/while/body/eval_jaxpr/dot_general | solution.py:178
  502.8 12.0 %reduce-scatter.5.cloned.1.call-done = bf16[64,1280]{1,0:T(8,128)(2,1)} async-done(((bf16[64,2560]{1,0:T(8,128)(2,1)}), bf16[64,1280]{1,0:T(8,128)(2,1)}) %reduce-scatter.5.cloned.1.call-update) | async-done | bytes 163856 | tf_op jit(solution)/shard_map/while/body/eval_jaxpr/reduce_scatter | solution.py:179
  530.3 9.5 reduce-scatter.3.cloned.1.call-done
  541.8 4.7 add_convert_fusion.3
  554.3 5.5 fusion.93
  563.4 5.3 fusion.28
  570.2 7.8 multiply_reduce_fusion.8
  582.0 5.0 add_convert_fusion.2
  587.1 7.8 fusion.29
  594.9 8.6 fusion.44
  603.5 12.6 %fusion.89 = (f32[64,64,256]{2,1,0:T(8,128)S(1)}, f32[64,64,256]{2,1,0:T(8,128)S(1)}, f32[64,64,256]{2,1,0:T(8,128)}, f32[64,64,256]{2,1,0:T(8,128)}, f32[64,64,256]{2,1,0:T(8,128)}) fusion(f32[64,64,1280]{2,1,0:T(8,128)} %fusion.44), kind=kLoop, calls=%fused_computation.189 | loop fusion | bytes 41943040 | tf_op jit(solution)/shard_map/slice | solution.py:65
  616.1 13.4 %multiply_reduce_fusion = (f32[64,256]{1,0:T(8,128)S(1)}, f32[64,256]{1,0:T(8,128)}, f32[64,256]{1,0:T(8,128)}, f32[64,256]{1,0:T(8,128)S(1)}, f32[64,64,256]{2,1,0:T(8,128)}) fusion(f32[64,256]{1,0:T(8,128)S(1)} %copy.106, f32[64,64,256]{2,1,0:T(8,128)S(1)} %copy-done.2, f32[64,256]{1,0:T(8,128)S(1)} %copy.104, f32[64,256]{1,0:T(8,128)} %copy-done.8, ...), kind=kLoop, calls=%fused_computation.42 | loop fusion | flops 35586048 | bytes 29818880 | tf_op jit(solution)/shard_map/reduce_sum | solution.py:126
  633.5 4.0 multiply_reduce_fusion.5
  648.0 98.0 %all-reduce.19.cloned.1.call-done = (bf16[1280,256]{0,1:T(8,128)(2,1)}, bf16[256,512]{1,0:T(8,128)(2,1)}) async-done(((bf16[1280,256]{0,1:T(8,128)(2,1)}, bf16[256,512]{1,0:T(8,128)(2,1)}), (bf16[1280,256]{0,1:T(8,128)(2,1)}, bf16[256,512]{1,0:T(8,128)(2,1)})) %all-reduce.19.cloned.1.call-update) | async-done | bytes 917520 | tf_op jit(solution)/shard_map/psum | solution.py:243
  747.6 87.4 %all-reduce.17.cloned.1.call-done = bf16[1280,512]{1,0:T(8,128)(2,1)} async-done(((bf16[1280,512]{1,0:T(8,128)(2,1)}), bf16[1280,512]{1,0:T(8,128)(2,1)}) %all-reduce.17.cloned.1.call-update) | async-done | bytes 1310736 | tf_op jit(solution)/shard_map/psum | solution.py:250
  837.0 4.7 fusion.36
  841.7 121.1 %all-reduce.8 = (bf16[70,256]{0,1:T(8,128)(2,1)S(1)}, bf16[14,256]{1,0:T(8,128)(2,1)S(1)}, bf16[256,14]{0,1:T(8,128)(2,1)S(1)}, bf16[]{:T(256)}) all-reduce(bf16[70,256]{0,1:T(8,128)(2,1)S(1)} %fusion.36, bf16[14,256]{1,0:T(8,128)(2,1)S(1)} %fusion.40, ...), channel_id=1, replica_groups=mesh['dp'=16,'segment'=4,'mp'=2] {'dp','mp'}, use_global_device_ids=true, to_apply=%region_28.30 | all-reduce | flops 25089 | bytes 100356 | tf_op jit(solution)/shard_map/psum | solution.py:242
  963.9 16.5 %all-reduce.22 = (bf16[70,256]{0,1:T(8,128)(2,1)S(1)}, bf16[14,256]{1,0:T(8,128)(2,1)S(1)}, bf16[256,14]{0,1:T(8,128)(2,1)S(1)}, bf16[16,1280]{1,0:T(8,128)(2,1)S(1)}, bf16[]{:T(256)}) all-reduce(bf16[70,256]{0,1:T(8,128)(2,1)S(1)} %broadcast_select_fusion.3, ...), channel_id=1, replica_groups=mesh['dp'=16,'segment'=4,'mp'=2] {'segment'}, use_global_device_ids=true, to_apply=%region_29.31 | all-reduce | flops 45569 | bytes 182276 | tf_op jit(solution)/shard_map/psum | solution.py:24
  (237 shorter events, 144.5 us)
Async XLA Ops:
  7.2 517.2 %copy-start = (bf16[1280,512]{1,0:T(8,128)(2,1)S(1)}, bf16[1280,512]{1,0:T(8,128)(2,1)}, u32[]{:S(2)}) copy-start(bf16[1280,512]{1,0:T(8,128)(2,1)} %param.23) | copy-start | bytes 3932164
  7.2 80.4 %all-gather.8.cloned.1.call-start = ((), (), s32[]{:S(2)}) async-start(), calls=%async_computation.4 | async-start | bytes 9748480 | tf_op jit(solution)/shard_map/all_gather | solution.py:159
  7.9 155.8 %all-gather.4.cloned.1.call-start = ((), (), s32[]{:S(2)}) async-start(), calls=%async_computation.2 | async-start | bytes 9748480 | tf_op jit(solution)/shard_map/all_gather | solution.py:157
  8.7 231.1 %all-gather.6.cloned.1.call-start = ((), (), s32[]{:S(2)}) async-start(), calls=%async_computation.3 | async-start | bytes 9748480 | tf_op jit(solution)/shard_map/all_gather | solution.py:158
  13.5 549.8 %copy-start.4 = (bf16[8,8,64,14]{3,2,1,0:T(8,128)(2,1)}, bf16[8,8,64,14]{3,2,1,0:T(8,128)(2,1)S(1)}, u32[]{:S(2)}) copy-start(bf16[8,8,64,14]{3,2,1,0:T(8,128)(2,1)S(1)} %copy.99) | copy-start | bytes 344068
  16.7 6.4 copy-start.19
  23.1 7.5 copy-start.20
  23.1 7.5 copy-start.15
  240.7 29.6 %reduce-scatter.5.cloned.1.call-start = ((), (), s32[]{:S(2)}) async-start(), calls=%async_computation.9 | async-start | bytes 491520 | tf_op jit(solution)/shard_map/while/body/eval_jaxpr/reduce_scatter | solution.py:179
  272.0 6.6 collective-permute-start
  278.6 32.4 %reduce-scatter.5.cloned.1.call-start = ((), (), s32[]{:S(2)}) async-start(), calls=%async_computation.9 | async-start | bytes 491520 | tf_op jit(solution)/shard_map/while/body/eval_jaxpr/reduce_scatter | solution.py:179
  312.7 6.6 collective-permute-start
  319.4 32.4 %reduce-scatter.5.cloned.1.call-start = ((), (), s32[]{:S(2)}) async-start(), calls=%async_computation.9 | async-start | bytes 491520 | tf_op jit(solution)/shard_map/while/body/eval_jaxpr/reduce_scatter | solution.py:179
  353.5 6.6 collective-permute-start
  360.1 32.4 %reduce-scatter.5.cloned.1.call-start = ((), (), s32[]{:S(2)}) async-start(), calls=%async_computation.9 | async-start | bytes 491520 | tf_op jit(solution)/shard_map/while/body/eval_jaxpr/reduce_scatter | solution.py:179
  394.2 6.6 collective-permute-start
  400.8 32.4 %reduce-scatter.5.cloned.1.call-start = ((), (), s32[]{:S(2)}) async-start(), calls=%async_computation.9 | async-start | bytes 491520 | tf_op jit(solution)/shard_map/while/body/eval_jaxpr/reduce_scatter | solution.py:179
  434.9 6.6 collective-permute-start
  441.6 32.4 %reduce-scatter.5.cloned.1.call-start = ((), (), s32[]{:S(2)}) async-start(), calls=%async_computation.9 | async-start | bytes 491520 | tf_op jit(solution)/shard_map/while/body/eval_jaxpr/reduce_scatter | solution.py:179
  475.7 6.6 collective-permute-start
  482.3 32.4 %reduce-scatter.5.cloned.1.call-start = ((), (), s32[]{:S(2)}) async-start(), calls=%async_computation.9 | async-start | bytes 491520 | tf_op jit(solution)/shard_map/while/body/eval_jaxpr/reduce_scatter | solution.py:179
  516.4 6.6 collective-permute-start
  523.1 16.8 %reduce-scatter.3.cloned.1.call-start = ((), (), s32[]{:S(2)}) async-start(), calls=%async_computation.5 | async-start | bytes 24576 | tf_op jit(solution)/shard_map/reduce_scatter | solution.py:210
  525.3 220.6 %all-reduce.19.cloned.1.call-start = ((), (), s32[]{:S(2)}) async-start(), calls=%async_computation.7 | async-start | bytes 1835008 | tf_op jit(solution)/shard_map/psum | solution.py:243
  526.5 43.7 %copy-start.22 = (f32[64]{0:T(128)}, f32[64]{0:T(128)S(1)}, u32[]{:S(2)}) copy-start(f32[64]{0:T(128)S(1)} %mul.384) | copy-start | bytes 772
  541.8 6.7 copy-start.8
  546.5 2.2 copy-start.1
  551.9 2.3 copy-start.9
  554.3 5.5 copy-start.16
  559.8 3.5 copy-start.24
  563.3 5.3 copy-start.21
  563.3 6.9 copy-start.3
  568.7 9.4 copy-start.7
  587.1 7.8 copy-start.10
  603.5 12.6 %copy-start.2 = (f32[64,64,256]{2,1,0:T(8,128)S(1)}, f32[64,64,256]{2,1,0:T(8,128)}, u32[]{:S(2)}) copy-start(f32[64,64,256]{2,1,0:T(8,128)} %get-tuple-element.319) | copy-start | bytes 12582916
  629.5 0.6 copy-start.11
  629.5 0.7 copy-start.13
  629.5 9.0 copy-start.17
  629.5 9.8 copy-start.18
  630.2 9.1 copy-start.12
  630.2 9.1 copy-start.14
  633.5 10.3 %copy-start.23 = (f32[64]{0:T(128)S(1)}, f32[64]{0:T(128)}, u32[]{:S(2)}) copy-start(f32[64]{0:T(128)} %copy-done.22) | copy-start | bytes 772
  637.5 8.4 copy-start.5
  641.1 193.9 %all-reduce.17.cloned.1.call-start = ((), (), s32[]{:S(2)}) async-start(), calls=%async_computation.6 | async-start | bytes 2621440 | tf_op jit(solution)/shard_map/psum | solution.py:250
  643.8 339.9 %all-reduce.21.cloned.1.call-start = ((), (), s32[]{:S(2)}) async-start(), calls=%async_computation.8 | async-start | bytes 4456448 | tf_op jit(solution)/shard_map/psum | solution.py:24
  647.9 189.0 %copy-start.6 = (bf16[64,64,70]{2,1,0:T(8,128)(2,1)S(1)}, bf16[64,64,70]{2,1,0:T(8,128)(2,1)}, u32[]{:S(2)}) copy-start(bf16[64,64,70]{2,1,0:T(8,128)(2,1)} %concatenate.15) | copy-start | bytes 1720324
Sparse Core Ops, SparseCore 0:
  10.2 77.4 all-gather.7
  89.7 73.9 all-gather.3
  165.9 73.9 all-gather.5
  260.0 10.2 reduce-scatter.4
  298.3 12.7 reduce-scatter.4
  339.0 12.7 reduce-scatter.4
  379.8 12.7 reduce-scatter.4
  420.5 12.7 reduce-scatter.4
  461.2 12.7 reduce-scatter.4
  502.0 12.7 reduce-scatter.4
  526.8 13.0 reduce-scatter.2
  641.2 104.7 all-reduce.18
  749.2 85.6 all-reduce.16
  838.0 62.2 all-reduce.20
where the time goes:
time: 1010 us; the launch traced here: 997 us
  waiting for transfers between devices  495 us (49%)
  matrix products  165 us (16%)
  blocking collectives  158 us (16%)
  other arithmetic  79.8 us (8%)
  local copies, waits for them, and re-layouts  55.8 us (6%)
  starting transfers between devices  23.3 us (2%)
  between operations  18.5 us (2%)
    psum x1, blocking collectives, body(): lax.psum(grad_in.astype(jnp.bfloat16), ('dp', 'mp')).astype(jnp.float32)  121 us
    psum x1, waiting for transfers between devices, body(): lax.psum(grad_mid.astype(jnp.bfloat16), ('dp', 'mp')).astype(jnp.float32)  98 us
    psum x1, waiting for transfers between devices, body(): lax.psum(cond_weight_part.astype(jnp.bfloat16), 'dp').astype(jnp.float32)  87.4 us
    reduce_scatter x7, waiting for transfers between devices, trunk_layer(): lax.psum_scatter(partial_out.astype(jnp.bfloat16), 'mp', scatter_dimensio...  81.3 us
    all_gather x1, waiting for transfers between devices, body(): lax.all_gather(w_up, 'dp', axis=1, tiled=True)  76.1 us
    dot_general x7, matrix products, trunk_layer(): jnp.dot(hidden, down_weight, preferred_element_type=jnp.float32)  72.3 us
    all_gather x1, waiting for transfers between devices, body(): lax.all_gather(w_gate, 'dp', axis=1, tiled=True)  63.2 us
    dot_general x14, matrix products, contract(): return jnp.einsum(form, left, right, preferred_element_type=jnp.float32)  54.5 us
  transfers between devices with their start and end apart: 21, of which 20 were waited for; matrix products, arithmetic and copies ran while one was open for 6% of the time, Pallas kernels for 0%

commit v1 on v0

v1 whole, which is shorter than its diff:
```python
import functools
import math

import jax
import jax.numpy as jnp
import numpy as np
from jax import lax
from jax.experimental import pallas as pl
from jax.experimental.pallas import tpu as pltpu
from jax.sharding import PartitionSpec as P

MESH = pl.DeviceIdType.MESH
GROUPS = 8
TSTEPS = 100
SIDE = 4
MICRO = 4
ROWS = 32
D = 2560
HALF = 1280
FH = 1792
SHARD = 160
CUT = 80
TILE = 256


def schedule():
    grid = np.arange(TSTEPS + 1, dtype=np.float64) / TSTEPS
    curve = np.cos((grid + 0.008) / 1.008 * math.pi / 2.0) ** 2
    betas = np.minimum(1.0 - curve[1:] / curve[:-1], 0.999)
    return np.cumprod(1.0 - betas)


def trunk_kernel(
    x_ref, gain_ref, wg_ref, wu_ref, wd_ref, wc_ref,
    cond_ref, wcond_ref,
    weights, first, arrived, leaving, normed, hidden, partial, share, other,
    own_sem, gs_sem, gr_sem, ms_sem, mr_sem, zs_sem, zr_sem, cs_sem, cr_sem,
):
    dp, seg, core = lax.axis_index("dp"), lax.axis_index("segment"), lax.axis_index("mp")
    y, x = dp // SIDE, dp % SIDE
    sibling = 1 - core

    def at(axis, delta):
        if axis == "x":
            return y * SIDE + (x + delta + SIDE) % SIDE
        return ((y + delta + SIDE) % SIDE) * SIDE + x

    barrier = pltpu.get_barrier_semaphore()
    for axis in ("x", "y"):
        for delta in (1, -1):
            pl.semaphore_signal(barrier, inc=1, device_id={"dp": at(axis, delta)}, device_id_type=MESH)
    pl.semaphore_signal(barrier, inc=1, device_id={"mp": sibling}, device_id_type=MESH)
    for step in range(1, 4):
        pl.semaphore_signal(barrier, inc=1, device_id={"segment": (seg + step) % 4}, device_id_type=MESH)
    pl.semaphore_wait(barrier, 8)

    sources = (wg_ref, wu_ref, wd_ref)
    chunks = [(which, part) for which in range(3) for part in range(2)]

    def spot(which, part, px, py, begin=0, size=CUT):
        row = (py * SIDE + px) * SHARD + part * CUT + begin
        return weights.at[which, pl.ds(pl.multiple_of(row, 16), size), :]

    def place(chunk, p_off, q_off, begin=0, size=CUT):
        which, part = chunk
        dx, dy = (p_off, q_off) if part == 0 else (q_off, p_off)
        return spot(which, part, (x + dx + SIDE) % SIDE, (y + dy + SIDE) % SIDE, begin, size)

    def axes(chunk):
        return ("x", "y") if chunk[1] == 0 else ("y", "x")

    def piece(chunk, kind):
        return (0, 48) if kind == 0 else (48, 32)

    def make(chunk, number, src, dst, axis, delta):
        q = chunks.index(chunk)
        return pltpu.make_async_remote_copy(
            src_ref=src, dst_ref=dst, send_sem=gs_sem.at[q, number], recv_sem=gr_sem.at[q, number],
            device_id={"dp": at(axis, delta)}, device_id_type=MESH,
        )

    OFF = (0, -1, 1, 2)

    def spec(chunk, number):
        p_axis, q_axis = axes(chunk)
        if number < 4:
            delta = 1 if number % 2 == 0 else -1
            if number < 2:
                return p_axis, delta, 0, 0, 0, CUT
            begin, size = piece(chunk, number - 2)
            return p_axis, delta, -delta, 0, begin, size
        slot, kind = divmod(number - 4, 4)
        delta = 1 if kind % 2 == 0 else -1
        if kind < 2:
            return q_axis, delta, OFF[slot], 0, 0, CUT
        begin, size = piece(chunk, kind - 2)
        return q_axis, delta, OFF[slot], -delta, begin, size

    def source_of(chunk, number):
        _, _, p_off, q_off, begin, size = spec(chunk, number)
        if p_off == 0 and q_off == 0:
            return sources[chunk[0]].at[pl.ds(chunk[1] * CUT + begin, size), :]
        return place(chunk, p_off, q_off, begin, size)

    def send(chunk, number):
        axis, delta, p_off, q_off, begin, size = spec(chunk, number)
        make(chunk, number, source_of(chunk, number), place(chunk, p_off, q_off, begin, size), axis, delta).start()

    def receive(chunk, number):
        axis, delta, p_off, q_off, begin, size = spec(chunk, number)
        if number < 4:
            p_off = p_off - delta
        else:
            q_off = q_off - delta
        spot_here = place(chunk, p_off, q_off, begin, size)
        make(chunk, number, spot_here, spot_here, axis, delta).wait_recv()

    def sent(chunk, number):
        axis, delta, p_off, q_off, begin, size = spec(chunk, number)
        make(chunk, number, source_of(chunk, number), place(chunk, p_off, q_off, begin, size), axis, delta).wait_send()

    own = []
    for chunk in chunks:
        for number in (0, 1, 4, 5):
            send(chunk, number)
    for which in range(3):
        keep = pltpu.make_async_copy(
            sources[which], weights.at[which, pl.ds(pl.multiple_of(dp * SHARD, 16), SHARD), :], own_sem.at[which]
        )
        keep.start()
        own.append(keep)

    def sibling_copy(number, src, dst):
        return pltpu.make_async_remote_copy(
            src_ref=src, dst_ref=dst, send_sem=ms_sem.at[number], recv_sem=mr_sem.at[number],
            device_id={"mp": sibling}, device_id_type=MESH,
        )

    here = pl.ds(pl.multiple_of(core * HALF, 128), HALF)
    there = pl.ds(pl.multiple_of(sibling * HALF, 128), HALF)
    for j in range(MICRO):
        src = x_ref.at[pl.ds(pl.multiple_of(64 * j + 32 * sibling, 16), ROWS), :]
        sibling_copy(j, src, first.at[j, :, here]).start()
        kept = pltpu.make_async_copy(
            x_ref.at[pl.ds(pl.multiple_of(64 * j + 32 * core, 16), ROWS), :], first.at[j, :, here], own_sem.at[3 + j]
        )
        kept.start()
        own.append(kept)
    here_rows = wcond_ref.at[pl.ds(pl.multiple_of(core * HALF, 16), HALF), :]
    there_rows = wcond_ref.at[pl.ds(pl.multiple_of(sibling * HALF, 16), HALF), :]
    sibling_copy(4, wc_ref, here_rows).start()
    kept = pltpu.make_async_copy(wc_ref, here_rows, own_sem.at[7])
    kept.start()
    own.append(kept)
    cond_ref[...] = jnp.zeros_like(cond_ref)

    for chunk in chunks:
        for number in (0, 1):
            receive(chunk, number)
            send(chunk, 2 + number)
            slot = 1 + number
            send(chunk, 4 + 4 * slot)
            send(chunk, 5 + 4 * slot)
        for kind in (0, 1):
            receive(chunk, 4 + kind)
            send(chunk, 6 + kind)
    for chunk in chunks:
        for number in (2, 3):
            receive(chunk, number)
        send(chunk, 16)
        send(chunk, 17)
        for slot in (1, 2):
            for kind in (0, 1):
                receive(chunk, 4 + 4 * slot + kind)
                send(chunk, 6 + 4 * slot + kind)
    for chunk in chunks:
        for kind in (0, 1):
            receive(chunk, 16 + kind)
            send(chunk, 18 + kind)
    for j in range(MICRO):
        sibling_copy(j, first.at[j, :, there], first.at[j, :, there]).wait_recv()
    for chunk in chunks:
        for slot in range(4):
            for kind in (2, 3):
                receive(chunk, 4 + 4 * slot + kind)
    for keep in own:
        keep.wait()

    def z_copy(j):
        return pltpu.make_async_remote_copy(
            src_ref=leaving.at[j], dst_ref=arrived.at[j], send_sem=zs_sem.at[j], recv_sem=zr_sem.at[j],
            device_id={"segment": (seg + 1) % 4}, device_id_type=MESH,
        )

    def cond_copy(j, target):
        return pltpu.make_async_remote_copy(
            src_ref=cond_ref.at[j], dst_ref=cond_ref.at[j], send_sem=cs_sem.at[j, target], recv_sem=cr_sem.at[j],
            device_id={"segment": target}, device_id_type=MESH,
        )

    gain = gain_ref[...].astype(jnp.float32)

    def micro(j, carry):
        @pl.when(seg == 0)
        def _():
            arrived[j] = first[j]

        @pl.when(seg > 0)
        def _():
            z_copy(j).wait_recv()

        state = arrived[j].astype(jnp.float32)
        factor = lax.rsqrt(jnp.mean(state * state, axis=1, keepdims=True) + 1e-05)
        normed[j, 0:ROWS] = (state * factor * gain).astype(jnp.bfloat16)
        swap = sibling_copy(5 + j, normed.at[j, pl.ds(0, ROWS)], normed.at[j, pl.ds(ROWS, ROWS)])
        swap.start()
        swap.wait_recv()

        def up(n, carry):
            cols = pl.ds(pl.multiple_of(n * TILE, TILE), TILE)
            rows = normed[j]
            gate = jnp.dot(rows, weights[0, :, cols], preferred_element_type=jnp.float32)
            lift = jnp.dot(rows, weights[1, :, cols], preferred_element_type=jnp.float32)
            hidden[:, cols] = (gate / (1.0 + jnp.exp(-gate)) * lift).astype(jnp.bfloat16)
            return carry

        lax.fori_loop(0, FH // TILE, up, 0)

        def down(n, carry):
            cols = pl.ds(pl.multiple_of(n * TILE, TILE), TILE)
            out = lax.dot_general(
                hidden[...], weights[2, cols, :], (((1,), (1,)), ((), ())), preferred_element_type=jnp.float32
            )
            partial[:, cols] = out[0:ROWS]
            share[j, :, cols] = out[ROWS:].astype(jnp.bfloat16)
            return carry

        lax.fori_loop(0, D // TILE, down, 0)
        back = sibling_copy(9 + j, share.at[j], other.at[j])
        back.start()
        back.wait_recv()
        result = (arrived[j].astype(jnp.float32) + (partial[...] + other[j].astype(jnp.float32))).astype(jnp.bfloat16)

        @pl.when(seg < 3)
        def _():
            leaving[j] = result
            z_copy(j).start()

        @pl.when(seg == 3)
        def _():
            mean = jnp.mean(result.astype(jnp.float32).reshape(2, 16, D), axis=1)
            cond_ref[j, 0:2] = mean.astype(jnp.bfloat16).astype(jnp.float32)
            for target in range(3):
                cond_copy(j, target).start()

        return carry

    lax.fori_loop(0, MICRO, micro, 0)

    for chunk in chunks:
        for number in range(20):
            sent(chunk, number)
    for j in range(MICRO):
        sibling_copy(j, x_ref.at[pl.ds(0, ROWS), :], first.at[j, :, there]).wait_send()
        sibling_copy(5 + j, normed.at[j, pl.ds(0, ROWS)], normed.at[j, pl.ds(ROWS, ROWS)]).wait_send()
        sibling_copy(9 + j, share.at[j], other.at[j]).wait_send()

        @pl.when(seg < 3)
        def _(j=j):
            z_copy(j).wait_send()
            cond_copy(j, 0).wait_recv()

        @pl.when(seg == 3)
        def _(j=j):
            for target in range(3):
                cond_copy(j, target).wait_send()

    last = sibling_copy(4, wc_ref, there_rows)
    last.wait_recv()
    last.wait_send()


def trunk(trunk_in, norm_gain, w_gate, w_up, w_down_t, w_cond):
    anywhere = pl.BlockSpec(memory_space=pl.ANY)
    vmem = pl.BlockSpec(memory_space=pltpu.VMEM)
    dma = pltpu.SemaphoreType.DMA
    bf16 = jnp.bfloat16
    return pl.pallas_call(
        trunk_kernel,
        out_shape=(
            jax.ShapeDtypeStruct((MICRO, 8, D), jnp.float32),
            jax.ShapeDtypeStruct((D, w_cond.shape[1]), bf16),
        ),
        in_specs=[anywhere, vmem, anywhere, anywhere, anywhere, anywhere],
        out_specs=(vmem, anywhere),
        scratch_shapes=[
            pltpu.VMEM((3, D, FH), bf16),
            pltpu.VMEM((MICRO, ROWS, D), bf16),
            pltpu.VMEM((MICRO, ROWS, D), bf16),
            pltpu.VMEM((MICRO, ROWS, D), bf16),
            pltpu.VMEM((MICRO, 2 * ROWS, D), bf16),
            pltpu.VMEM((2 * ROWS, FH), bf16),
            pltpu.VMEM((ROWS, D), jnp.float32),
            pltpu.VMEM((MICRO, ROWS, D), bf16),
            pltpu.VMEM((MICRO, ROWS, D), bf16),
            dma((8,)),
            dma((6, 20)),
            dma((6, 20)),
            dma((13,)),
            dma((13,)),
            dma((MICRO,)),
            dma((MICRO,)),
            dma((MICRO, 3)),
            dma((MICRO,)),
        ],
        compiler_params=pltpu.CompilerParams(
            collective_id=0, has_side_effects=True, vmem_limit_bytes=52 * 2**20
        ),
    )(trunk_in, norm_gain, w_gate, w_up, w_down_t, w_cond)


def mish_parts(values):
    small = jnp.exp(-jnp.abs(values))
    right = values > 0
    top = jnp.where(right, 1.0 + 2.0 * small, small * (small + 2.0))
    rest = jnp.where(right, 2.0 * small * small, 2.0)
    return small, right, top, rest


def mish_value(values):
    _, _, top, rest = mish_parts(values)
    return values * (top / (top + rest))


def mish_slope(values):
    small, right, top, rest = mish_parts(values)
    inverse = 1.0 / (top + rest)
    logistic = jnp.where(right, 1.0, small) / (1.0 + small)
    return top * inverse + values * logistic * (rest * (2.0 * top + rest)) * (inverse * inverse)


def collect_kernel(
    cond_ref, film_ref, grads_ref, wc_ref,
    total_ref, gwc_ref, gcond_ref,
    cond_sib, act_all, film_sib, film_out, film_z, film_all,
    mp_in, z_out, z_in, x_out, x_in, y_out, y_in, full,
    ms_sem, mr_sem, zs_sem, zr_sem, xs_sem, xr_sem, ys_sem, yr_sem,
):
    dp, seg, core = lax.axis_index("dp"), lax.axis_index("segment"), lax.axis_index("mp")
    y, x = dp // SIDE, dp % SIDE
    sibling = 1 - core

    def x_peer(step):
        return {"dp": y * SIDE + (x + step) % SIDE}

    def y_peer(step):
        return {"dp": ((y + step) % SIDE) * SIDE + x}

    def z_peer(step):
        return {"segment": (seg + step) % SIDE}

    barrier = pltpu.get_barrier_semaphore()
    pl.semaphore_signal(barrier, inc=1, device_id={"mp": sibling}, device_id_type=MESH)
    for step in range(1, SIDE):
        for peer in (x_peer, y_peer, z_peer):
            pl.semaphore_signal(barrier, inc=1, device_id=peer(step), device_id_type=MESH)
    pl.semaphore_wait(barrier, 10)

    def copy(src, dst, out_sem, in_sem, peer):
        return pltpu.make_async_remote_copy(
            src_ref=src, dst_ref=dst, send_sem=out_sem, recv_sem=in_sem, device_id=peer, device_id_type=MESH
        )

    started = []

    def launch(src, dst, out_sem, in_sem, peer):
        one = copy(src, dst, out_sem, in_sem, peer)
        one.start()
        started.append(one)

    def arrive(dst, in_sem):
        copy(dst, dst, ms_sem.at[0], in_sem, {"mp": sibling}).wait_recv()

    def to_sibling(number, src, dst):
        launch(src, dst, ms_sem.at[number], mr_sem.at[number], {"mp": sibling})

    def scatter(out_sem, in_sem, number, src, dst, me, peer):
        for step in range(1, SIDE):
            launch(
                src.at[(me + step) % SIDE], dst.at[me], out_sem.at[number, step - 1], in_sem.at[number, step - 1], peer(step)
            )

    def spread(out_sem, in_sem, number, slots, me, peer):
        for step in range(1, SIDE):
            launch(slots.at[me], slots.at[me], out_sem.at[number, step - 1], in_sem.at[number, step - 1], peer(step))

    def gathered(in_sem, number, slots, me):
        for step in range(1, SIDE):
            arrive(slots.at[(me - step + SIDE) % SIDE], in_sem.at[number, step - 1])

    def added(slots):
        pieces = [slots[k].astype(jnp.float32) for k in range(SIDE)]
        return (pieces[0] + pieces[1]) + (pieces[2] + pieces[3])

    here = pl.ds(pl.multiple_of(core * HALF, 128), HALF)
    there = pl.ds(pl.multiple_of(sibling * HALF, 128), HALF)
    mine = pl.ds(pl.multiple_of(core * 512, 128), 512)
    others = pl.ds(pl.multiple_of(sibling * 512, 128), 512)

    to_sibling(0, film_ref, film_sib)
    to_sibling(1, grads_ref.at[:, others, :], mp_in)
    to_sibling(2, cond_ref.at[:, :, there], cond_sib)

    arrive(film_sib, mr_sem.at[0])
    film_out[...] = jnp.zeros_like(film_out)
    for s in range(SIDE):
        film_out[s, 0:2] = film_ref[0:2, 128 * s : 128 * (s + 1)]
        film_out[s, 2:4] = film_sib[0:2, 128 * s : 128 * (s + 1)]
    scatter(zs_sem, zr_sem, 0, film_out, film_z, seg, z_peer)
    film_z[seg] = film_out[seg]

    arrive(mp_in, mr_sem.at[1])
    z_out[...] = (grads_ref[:, mine, :].astype(jnp.float32) + mp_in[...].astype(jnp.float32)).astype(jnp.bfloat16)
    scatter(zs_sem, zr_sem, 1, z_out, z_in, seg, z_peer)
    z_in[seg] = z_out[seg]

    arrive(cond_sib, mr_sem.at[2])
    rows = [cond_ref[j, 0:2, here] for j in range(MICRO)] + [cond_sib[j, 0:2] for j in range(MICRO)]
    act_all[y, x] = mish_value(jnp.concatenate(rows, axis=0)).astype(jnp.bfloat16)
    spread(xs_sem, xr_sem, 0, act_all.at[y], x, x_peer)

    gathered(zr_sem, 0, film_z, seg)
    rows = [film_z[j, 0:2] for j in range(MICRO)] + [film_z[j, 2:4] for j in range(MICRO)]
    film_all[y, x] = jnp.concatenate(rows, axis=0).astype(jnp.bfloat16)
    spread(xs_sem, xr_sem, 1, film_all.at[y], x, x_peer)

    low = jnp.where(core == 0, film_ref[0:2], film_sib[0:2])
    high = jnp.where(core == 0, film_sib[0:2], film_ref[0:2])
    film_rows = jnp.concatenate([low, high, jnp.zeros((12, 512), jnp.float32)], axis=0).astype(jnp.bfloat16)
    own_cond, sib_cond = cond_ref[seg, 0:2, here], cond_sib[seg, 0:2]
    cond_rows = jnp.concatenate(
        [jnp.where(core == 0, own_cond, sib_cond), jnp.where(core == 0, sib_cond, own_cond)], axis=0
    )
    back = lax.dot_general(film_rows, wc_ref[...], (((1,), (1,)), ((), ())), preferred_element_type=jnp.float32)
    gcond_ref[...] = back[0:4] * mish_slope(cond_rows)

    gathered(zr_sem, 1, z_in, seg)
    x_out[...] = added(z_in).astype(jnp.bfloat16).reshape(x_out.shape)
    scatter(xs_sem, xr_sem, 2, x_out, x_in, x, x_peer)
    x_in[x] = x_out[x]

    gathered(xr_sem, 0, act_all.at[y], x)
    spread(ys_sem, yr_sem, 0, act_all, y, y_peer)
    gathered(xr_sem, 1, film_all.at[y], x)
    spread(ys_sem, yr_sem, 1, film_all, y, y_peer)

    gathered(xr_sem, 2, x_in, x)
    y_out[...] = added(x_in).astype(jnp.bfloat16).reshape(y_out.shape)
    scatter(ys_sem, yr_sem, 2, y_out, y_in, y, y_peer)
    y_in[y] = y_out[y]
    gathered(yr_sem, 2, y_in, y)
    full[core, x, y] = added(y_in).astype(jnp.bfloat16)
    spread(ys_sem, yr_sem, 3, full.at[core, x], y, y_peer)
    gathered(yr_sem, 3, full.at[core, x], y)
    spread(xs_sem, xr_sem, 3, full.at[core], x, x_peer)

    gathered(yr_sem, 0, act_all, y)
    gathered(yr_sem, 1, film_all, y)

    gathered(xr_sem, 3, full.at[core], x)
    to_sibling(3, full.at[core], full.at[core])
    gwc_ref[...] = lax.dot_general(
        act_all[...].reshape(256, HALF), film_all[...].reshape(256, 128), (((0,), (0,)), ((), ())),
        preferred_element_type=jnp.float32,
    )
    arrive(full.at[sibling], mr_sem.at[3])
    total_ref[...] = full[...].astype(jnp.float32).reshape(total_ref.shape)
    for one in started:
        one.wait_send()


def collect(cond, film, grads, w_cond):
    vmem = pl.BlockSpec(memory_space=pltpu.VMEM)
    dma = pltpu.SemaphoreType.DMA
    bf16, f32 = jnp.bfloat16, jnp.float32
    return pl.pallas_call(
        collect_kernel,
        out_shape=(
            jax.ShapeDtypeStruct((1024, 128), f32),
            jax.ShapeDtypeStruct((HALF, 128), f32),
            jax.ShapeDtypeStruct((4, HALF), f32),
        ),
        in_specs=[vmem] * 4,
        out_specs=(vmem, vmem, vmem),
        scratch_shapes=[
            pltpu.VMEM((MICRO, 8, HALF), f32),
            pltpu.VMEM((SIDE, SIDE, 16, HALF), bf16),
            pltpu.VMEM((8, 512), f32),
            pltpu.VMEM((SIDE, 8, 128), f32),
            pltpu.VMEM((SIDE, 8, 128), f32),
            pltpu.VMEM((SIDE, SIDE, 16, 128), bf16),
            pltpu.VMEM((SIDE, 512, 128), bf16),
            pltpu.VMEM((SIDE, 512, 128), bf16),
            pltpu.VMEM((SIDE, 512, 128), bf16),
            pltpu.VMEM((SIDE, 128, 128), bf16),
            pltpu.VMEM((SIDE, 128, 128), bf16),
            pltpu.VMEM((SIDE, 32, 128), bf16),
            pltpu.VMEM((SIDE, 32, 128), bf16),
            pltpu.VMEM((2, SIDE, SIDE, 32, 128), bf16),
            dma((4,)), dma((4,)),
            dma((2, 3)), dma((2, 3)),
            dma((4, 3)), dma((4, 3)),
            dma((4, 3)), dma((4, 3)),
        ],
        compiler_params=pltpu.CompilerParams(
            collective_id=1, has_side_effects=True, vmem_limit_bytes=32 * 2**20
        ),
    )(cond, film, grads, w_cond)


def contract(form, left, right):
    return jnp.einsum(form, left, right, preferred_element_type=jnp.float32)


def norm_act(values):
    rows, steps, channels = values.shape
    grouped = values.reshape(rows, steps, GROUPS, channels // GROUPS)
    center = jnp.mean(grouped, axis=(1, 3), keepdims=True)
    spread = jnp.mean((grouped - center) ** 2, axis=(1, 3), keepdims=True)
    normed = (grouped - center) * lax.rsqrt(spread + 1e-05)
    return mish_value(normed.reshape(rows, steps, channels))


def columns(values):
    steps = values.shape[1]
    padded = jnp.pad(values, ((0, 0), (2, 2), (0, 0)))
    return jnp.concatenate([padded[:, tap : tap + steps] for tap in range(5)], axis=2)


def columns_adjoint(grads, width):
    total = 0.0
    for tap in range(5):
        piece = grads[:, :, tap * width : (tap + 1) * width]
        total = total + jnp.pad(piece, ((0, 0), (tap, 4 - tap), (0, 0)))
    return total[:, 2:-2]


def denoise(
    film_cond, tsteps, advantage, actions, noise, w_in, w_mid, w_res, w_out, w_time, product
):
    row_count, levels = tsteps.shape
    horizon, action_dims = (actions.shape[1], actions.shape[2])
    channels = w_mid.shape[1]
    flat = row_count * levels
    matches = (tsteps[:, :, None] == jnp.arange(TSTEPS, dtype=jnp.int32)[None, None, :]).astype(
        jnp.float32
    )
    alpha = jnp.sum(matches * jnp.asarray(schedule(), jnp.float32)[None, None, :], axis=2)
    keep_root = jnp.sqrt(alpha)[:, :, None, None]
    noise_root = jnp.sqrt(1.0 - alpha)[:, :, None, None]
    noisy_act = (
        keep_root * actions.astype(jnp.float32)[:, None] + noise_root * noise.astype(jnp.float32)
    ).astype(jnp.bfloat16)
    noisy_act = noisy_act.reshape(flat, horizon, action_dims)
    half_dim = w_time.shape[0] // 2
    frequencies = jnp.exp(
        -math.log(10000.0) * jnp.arange(half_dim, dtype=jnp.float32) / (half_dim - 1)
    )
    angles = tsteps.astype(jnp.float32)[:, :, None] * frequencies[None, None, :]
    embedded = jnp.concatenate([jnp.sin(angles), jnp.cos(angles)], axis=2)
    time_act = mish_value(embedded).astype(jnp.bfloat16).reshape(flat, 2 * half_dim)
    film = film_cond[:, None, :] + product(
        "rld,dc->rlc", time_act.reshape(row_count, levels, -1), w_time
    )
    film = film.reshape(flat, 2 * channels)
    film_scale = film[:, None, :channels]
    film_shift = film[:, None, channels:]
    columns_in = columns(noisy_act)
    pre_first = product("mhk,kc->mhc", columns_in, w_in)
    act_first, first_back = jax.vjp(norm_act, pre_first)
    modulated = (film_scale * act_first + film_shift).astype(jnp.bfloat16)
    columns_mid = columns(modulated)
    pre_second = product("mhk,kc->mhc", columns_mid, w_mid)
    act_second, second_back = jax.vjp(norm_act, pre_second)
    block_out = (act_second + product("mha,ac->mhc", noisy_act, w_res)).astype(jnp.bfloat16)
    predicted = product("mhc,ca->mha", block_out, w_out)
    errors = predicted - noise.reshape(flat, horizon, action_dims).astype(jnp.float32)
    err_sum = jnp.sum(errors * errors) / (horizon * action_dims)
    weights = advantage.reshape(flat, 1, 1)
    d_pred = (2.0 * weights * errors / (horizon * action_dims)).astype(jnp.bfloat16)
    grad_out = product("mhc,mha->ca", block_out, d_pred)
    d_block = product("mha,ca->mhc", d_pred, w_out)
    grad_res = product("mha,mhc->ac", noisy_act, d_block.astype(jnp.bfloat16))
    d_second = second_back(d_block)[0].astype(jnp.bfloat16)
    grad_mid = product("mhk,mhc->kc", columns_mid, d_second)
    d_columns = product("mhc,kc->mhk", d_second, w_mid)
    d_modulated = columns_adjoint(d_columns, channels)
    d_film = jnp.concatenate(
        [jnp.sum(d_modulated * act_first, axis=1), jnp.sum(d_modulated, axis=1)], axis=1
    )
    d_first = first_back(film_scale * d_modulated)[0].astype(jnp.bfloat16)
    grad_in = product("mhk,mhc->kc", columns_in, d_first)
    grad_time = product("md,mc->dc", time_act, d_film.astype(jnp.bfloat16))
    d_film_cond = jnp.sum(d_film.reshape(row_count, levels, -1), axis=1)
    return (err_sum, grad_in, grad_mid, grad_res, grad_out, grad_time, d_film_cond)


def body(
    trunk_in, norm_gain, w_gate, w_up, w_down, w_cond, w_time, w_in, w_mid, w_res, w_out,
    tsteps, advantage, actions, noise,
):
    seg, core = lax.axis_index("segment"), lax.axis_index("mp")
    cond_all, w_cond_full = trunk(trunk_in, norm_gain, w_gate[0], w_up[0], w_down[0].T, w_cond)
    cond = lax.dynamic_index_in_dim(cond_all, seg, 0, keepdims=False)[0:2]
    cond_act = mish_value(cond).astype(jnp.bfloat16)
    film_cond = jnp.dot(cond_act, w_cond_full, preferred_element_type=jnp.float32)
    begin = 4 * seg + 2 * core

    def own(values):
        return lax.dynamic_slice_in_dim(values, begin, 2, 0)

    err_sum, grad_in, grad_mid, grad_res, grad_out, grad_time, d_film_cond = denoise(
        film_cond, own(tsteps), own(advantage), own(actions), own(noise), w_in, w_mid, w_res, w_out, w_time, contract
    )
    blocks = []
    for s in range(4):
        part = slice(64 * s, 64 * (s + 1))
        upper = jnp.concatenate([grad_mid[:640, part], grad_mid[640:, part]], axis=1)
        low = jnp.concatenate(
            [grad_res[:, part], jnp.zeros((2, 64)), grad_out[part].T, jnp.zeros((2, 64)), jnp.full((48, 64), err_sum)], axis=0
        )
        middle = jnp.concatenate([jnp.pad(grad_in[:, part], ((0, 10), (0, 0))), low], axis=1)
        blocks.append(
            jnp.concatenate([upper, middle, grad_time[:, 128 * s : 128 * (s + 1)], jnp.zeros((48, 128))], axis=0)
        )
    packed = jnp.stack(blocks).astype(jnp.bfloat16)
    film_pad = jnp.pad(d_film_cond, ((0, 6), (0, 0)))
    total, grad_w_cond, grad_cond = collect(cond_all, film_pad, packed, w_cond)
    side = total[640:720, 64:]
    return (
        total[640:710, :64],
        jnp.concatenate([total[:640, :64], total[:640, 64:]], axis=0),
        side[0:14],
        side[16:30].T,
        total[720:976],
        grad_w_cond,
        grad_cond,
        side[32, 0:1] / 2048.0,
    )


def solution(mesh):
    in_specs = (
        P("dp", "mp"),
        P("segment", None),
        P("segment", "dp", "mp"),
        P("segment", "dp", "mp"),
        P("segment", "mp", "dp"),
        P("mp", None),
        P(),
        P(),
        P(),
        P(),
        P(),
        P("dp", None),
        P("dp", None),
        P("dp", None, None),
        P("dp", None, None, None),
    )
    out_specs = (
        P(None, "segment"),
        P(None, "segment"),
        P(None, "segment"),
        P("segment", None),
        P(None, "segment"),
        P("mp", "segment"),
        P(("dp", "segment"), "mp"),
        P(),
    )
    return jax.shard_map(body, mesh=mesh, in_specs=in_specs, out_specs=out_specs, check_vma=False)
```

time: 1010 us -> 356 us (0.35); the launches traced: 997 us -> 355 us
  waiting for transfers between devices: 495 us -> 0 us
  Pallas kernels: 0 us -> 286 us
  blocking collectives: 158 us -> 0 us
  matrix products: 165 us -> 16.1 us
  other arithmetic: 79.8 us -> 17.4 us
  local copies, waits for them, and re-layouts: 55.8 us -> 31.5 us
  starting transfers between devices: 23.3 us -> 0 us
  between operations: 18.5 us -> 3.75 us
    pallas_call x0 -> x2, Pallas kernels: none -> 286 us  [the longest x1 251 us: trunk(): pl.pallas_call(trunk_kernel, out_shape=(jax.ShapeDtypeStruct((MICRO, 8, D...]
    all_gather x3 -> x0, waiting for transfers between devices: 193 us -> none  [the longest x1 76.1 us: body(): lax.all_gather(w_up, 'dp', axis=1, tiled=True)]
    psum x3 -> x0, waiting for transfers between devices: 185 us -> none  [the longest x1 98 us: body(): lax.psum(grad_mid.astype(jnp.bfloat16), ('dp', 'mp')).astype(jnp.float32)]
    psum x2 -> x0, blocking collectives: 138 us -> none  [the longest x1 121 us: body(): lax.psum(grad_in.astype(jnp.bfloat16), ('dp', 'mp')).astype(jnp.float32)]
    dot_general x15 -> x1, matrix products: 111 us -> 2.19 us  [body(): jnp.dot(cond_act, w_cond_full, preferred_element_type=jnp.float32)]
    reduce_scatter x8 -> x0, waiting for transfers between devices: 90.8 us -> none  [the longest x7 81.3 us: trunk_layer(): lax.psum_scatter(partial_out.astype(jnp.bfloat16), 'mp', scatter_dimensio...]
    dot_general x14 -> x12, matrix products: 54.5 us -> 14 us  [contract(): return jnp.einsum(form, left, right, preferred_element_type=jnp.float32)]
    ppermute x7 -> x0, waiting for transfers between devices: 23.6 us -> none  [passed_along(): return lax.ppermute(block, axis, route)]
  transfers between devices with their start and end apart: 21 -> 0, of which waited for: 20 -> 0; matrix products, arithmetic and copies ran while one was open for 6% -> 0% of each run, Pallas kernels for 0% -> 0%
where the time goes in v1:
time: 356 us; the launch traced here: 355 us
  Pallas kernels  286 us (80%)
  local copies, waits for them, and re-layouts  31.5 us (9%)
  other arithmetic  17.4 us (5%)
  matrix products  16.1 us (5%)
  between operations  3.75 us (1%)
    pallas_call x1, Pallas kernels, trunk(): pl.pallas_call(trunk_kernel, out_shape=(jax.ShapeDtypeStruct((MICRO, 8, D...  251 us
    pallas_call x1, Pallas kernels, collect(): pl.pallas_call(collect_kernel, out_shape=(jax.ShapeDtypeStruct((1024, 128...  35 us
    concatenate x4, local copies, waits for them, and re-layouts, body(): jnp.concatenate([grad_res[:, part], jnp.zeros((2, 64)), grad_out[part].T,...  14.5 us
    dot_general x12, matrix products, contract(): return jnp.einsum(form, left, right, preferred_element_type=jnp.float32)  14 us

profile of v1, /device:TPU:1, one launch (start us, length us, event | category | flops | bytes accessed | tf_op | source)
XLA Modules:
  0.0 355.0 jit_solution(18184037988836886285)
XLA Ops:
  0.7 0.8 fusion.101
  1.6 0.8 select_reduce_fusion
  2.4 0.8 constant_dynamic-slice_fusion
  3.2 0.9 add_convert_fusion.4
  4.3 0.3 pad_slice_fusion
  4.7 0.6 concatenate.83
  5.3 0.3 fusion.110
  6.7 0.4 copy-done.18
  7.2 251.2 %shard_map.215 = (f32[4,8,2560]{2,1,0:T(8,128)S(1)}, bf16[2560,512]{1,0:T(8,128)(2,1)}) custom-call(bf16[256,1280]{1,0:T(8,128)(2,1)} %x_ref.1, bf16[1,2560]{1,0:T(2,128)(2,1)S(1)} %copy-done.4, bf16[160,1792]{1,0:T(8,128)(2,1)S(1)} %bitcast.92, bf16[160,1792]{1,0:T(8,128)(2,1)S(1)} %bitcast.93, bf16[160,1792]{1,0:T(8,128)(2,1)} %bitcast.98, ...), custom_call_target="tpu_custom_call" | custom-call | tf_op jit(solution)/shard_map/pallas_call | solution.py:288
  258.4 2.2 fusion.70
  260.7 0.7 add_convert_fusion.2
  261.7 0.7 constant_dynamic-update-slice_fusion
  262.8 0.9 fusion.111
  263.7 0.6 copy-done.12
  265.2 1.5 fusion.1
  266.7 0.8 dynamic-slice_convert_fusion
  267.6 2.6 multiply_reduce_fusion.9
  270.4 1.3 fusion.4
  271.8 0.7 slice_bitcast_fusion.4
  272.5 4.5 %multiply_reduce_fusion.8 = (f32[16,256]{1,0:T(8,128)S(1)}, f32[16,256]{1,0:T(8,128)}, f32[16,64,256]{2,1,0:T(8,128)}, bf16[16,64,256]{2,1,0:T(8,128)(2,1)S(1)}) fusion(f32[16,256]{1,0:T(8,128)S(1)} %mul.366, f32[16,64,256]{2,1,0:T(8,128)S(1)} %get-tuple-element.105, f32[16,256]{1,0:T(8,128)S(1)} %sub.58, bf16[256,14]{0,1:T(8,128)(2,1)S(1)} %copy-done.17, ...), kind=kOutput, calls=%fused_computation.64 | convolution fusion | flops 20219904 | bytes 2751552 | tf_op jit(solution)/shard_map/mha,ca->mhc/dot_general | solution.py:522
  277.2 0.7 fusion.108
  278.6 4.3 %concatenate.96 = bf16[80,64]{1,0:T(8,128)(2,1)} concatenate(bf16[14,64]{1,0:T(8,128)(2,1)S(1)} %get-tuple-element.91, bf16[2,64]{1,0:T(2,128)(2,1)S(1)} %broadcast.258, bf16[14,64]{1,0:T(8,128)(2,1)S(1)} %get-tuple-element.87, bf16[2,64]{1,0:T(2,128)(2,1)S(1)} %broadcast.258, bf16[48,64]{1,0:T(8,128)(2,1)S(1)} %broadcast_in_dim.56), dimensions={0} | concatenate | bytes 20480 | tf_op jit(solution)/shard_map/concatenate | solution.py:629
  282.9 4.4 %concatenate.92 = bf16[80,64]{1,0:T(8,128)(2,1)} concatenate(bf16[14,64]{1,0:T(8,128)(2,1)S(1)} %get-tuple-element.92, bf16[2,64]{1,0:T(2,128)(2,1)S(1)} %broadcast.258, bf16[14,64]{1,0:T(8,128)(2,1)S(1)} %get-tuple-element.88, bf16[2,64]{1,0:T(2,128)(2,1)S(1)} %broadcast.258, bf16[48,64]{1,0:T(8,128)(2,1)S(1)} %broadcast_in_dim.56), dimensions={0} | concatenate | bytes 20480 | tf_op jit(solution)/shard_map/concatenate | solution.py:629
  287.3 4.4 %concatenate.87 = bf16[80,64]{1,0:T(8,128)(2,1)} concatenate(bf16[14,64]{1,0:T(8,128)(2,1)S(1)} %get-tuple-element.89, bf16[2,64]{1,0:T(2,128)(2,1)S(1)} %broadcast.258, bf16[14,64]{1,0:T(8,128)(2,1)S(1)} %get-tuple-element.85, bf16[2,64]{1,0:T(2,128)(2,1)S(1)} %broadcast.258, bf16[48,64]{1,0:T(8,128)(2,1)S(1)} %broadcast_in_dim.56), dimensions={0} | concatenate | bytes 20480 | tf_op jit(solution)/shard_map/concatenate | solution.py:629
  291.6 0.8 reduce_sum.235
  293.4 1.7 add_convert_fusion.1
  295.1 0.3 copy-done.13
  295.5 0.9 fusion
  296.4 1.3 fusion.103
  297.7 0.9 fusion.26
  298.5 0.7 fusion.102
  299.2 3.3 multiply_reduce_fusion.6
  302.9 2.1 multiply_reduce_fusion.5
  305.1 0.7 multiply_sine_fusion
  305.9 0.3 convolution_convert_fusion
  306.1 0.7 fusion.105
  307.4 0.4 fusion.2
  308.3 1.7 fusion.52
  310.0 1.5 concatenate.100
  311.5 1.3 fusion.40
  312.9 35.0 %shard_map.216 = (f32[1024,128]{1,0:T(8,128)S(1)}, f32[1280,128]{1,0:T(8,128)S(1)}, f32[4,1280]{1,0:T(4,128)S(1)}) custom-call(f32[4,8,2560]{2,1,0:T(8,128)S(1)} %get-tuple-element.13.cond_ref, f32[8,512]{1,0:T(8,128)S(1)} %pad.56.film_ref, bf16[4,1024,128]{2,1,0:T(8,128)(2,1)S(1)} %pad_maximum_fusion.grads_ref, bf16[1280,512]{1,0:T(8,128)(2,1)S(1)} %copy-done.1), custom_call_target="tpu_custom_call" | custom-call | tf_op jit(solution)/shard_map/pallas_call | solution.py:486
  348.2 0.9 copy.59
  349.1 0.7 slice.224
  349.8 0.7 copy.58
  350.5 0.7 slice_bitcast_fusion
  351.1 0.6 slice.225
  352.4 0.8 copy.72
  353.2 0.6 copy.73
  (119 shorter events, 6.3 us)
Async XLA Ops:
  0.6 262.1 %copy-start = (bf16[1280,256]{1,0:T(8,128)(2,1)S(1)}, bf16[1280,256]{1,0:T(8,128)(2,1)}, u32[]{:S(2)}) copy-start(bf16[1280,256]{1,0:T(8,128)(2,1)} %param.24) | copy-start | bytes 1966084
  0.6 4.7 %copy-start.14 = (bf16[70,256]{1,0:T(8,128)(2,1)S(1)}, bf16[70,256]{1,0:T(8,128)(2,1)}, u32[]{:S(2)}) copy-start(bf16[70,256]{1,0:T(8,128)(2,1)} %param.23) | copy-start | bytes 107524
  4.6 2.5 copy-start.2
  4.7 2.5 copy-start.3
  4.7 2.5 copy-start.4
  5.3 1.4 copy-start.6
  6.6 0.6 copy-start.18
  6.6 0.6 copy-start.21
  7.2 253.4 %copy-start.8 = (bf16[256,512]{1,0:T(8,128)(2,1)S(1)}, bf16[256,512]{1,0:T(8,128)(2,1)}, u32[]{:S(2)}) copy-start(bf16[256,512]{1,0:T(8,128)(2,1)} %param.22) | copy-start | bytes 786436
  262.8 1.5 copy-start.12
  262.8 2.4 copy-start.22
  265.2 2.4 copy-start.17
  265.2 5.0 %copy-start.20 = (f32[16,8]{0,1:T(8,128)S(1)}, f32[16,8]{0,1:T(8,128)}, u32[]{:S(2)}) copy-start(f32[16,8]{0,1:T(8,128)} %param.28) | copy-start | bytes 1540
  278.6 13.0 %copy-start.15 = (bf16[2,64]{1,0:T(2,128)(2,1)}, bf16[2,64]{1,0:T(2,128)(2,1)S(1)}, u32[]{:S(2)}) copy-start(bf16[2,64]{1,0:T(2,128)(2,1)S(1)} %broadcast.258) | copy-start | bytes 772
  293.4 2.1 copy-start.13
  299.2 5.8 %copy-start.19 = (f32[2,8]{1,0:T(2,128)S(1)}, f32[2,8]{1,0:T(2,128)}, u32[]{:S(2)}) copy-start(f32[2,8]{1,0:T(2,128)} %copy-done.18) | copy-start | bytes 196
  302.5 4.9 %copy-start.5 = (f32[16,64,256]{2,1,0:T(8,128)S(1)}, f32[16,64,256]{2,1,0:T(8,128)}, u32[]{:S(2)}) copy-start(f32[16,64,256]{2,1,0:T(8,128)} %get-tuple-element.49) | copy-start | bytes 3145732
  302.5 4.9 %copy-start.7 = (bf16[16,64,70]{2,1,0:T(8,128)(2,1)S(1)}, bf16[16,64,70]{2,1,0:T(8,128)(2,1)}, u32[]{:S(2)}) copy-start(bf16[16,64,70]{2,1,0:T(8,128)(2,1)} %copy-done.6) | copy-start | bytes 430084
  306.8 3.2 copy-start.16
  307.4 0.8 copy-start.9
  307.4 0.9 copy-start.10
  307.4 0.9 copy-start.11
  307.8 5.1 %copy-start.1 = (bf16[1280,512]{1,0:T(8,128)(2,1)S(1)}, bf16[1280,512]{1,0:T(8,128)(2,1)}, u32[]{:S(2)}) copy-start(bf16[1280,512]{1,0:T(8,128)(2,1)} %wc_ref.3) | copy-start | bytes 3932164

commit v2 on v1

--- a/solution.py
+++ b/solution.py
@@ -10,7 +10,6 @@
 from jax.sharding import PartitionSpec as P
 
 MESH = pl.DeviceIdType.MESH
-GROUPS = 8
 TSTEPS = 100
 SIDE = 4
 MICRO = 4
@@ -518,91 +517,258 @@
     )(cond, film, grads, w_cond)
 
 
-def contract(form, left, right):
-    return jnp.einsum(form, left, right, preferred_element_type=jnp.float32)
-
-
-def norm_act(values):
-    rows, steps, channels = values.shape
-    grouped = values.reshape(rows, steps, GROUPS, channels // GROUPS)
-    center = jnp.mean(grouped, axis=(1, 3), keepdims=True)
-    spread = jnp.mean((grouped - center) ** 2, axis=(1, 3), keepdims=True)
-    normed = (grouped - center) * lax.rsqrt(spread + 1e-05)
-    return mish_value(normed.reshape(rows, steps, channels))
-
-
-def columns(values):
-    steps = values.shape[1]
-    padded = jnp.pad(values, ((0, 0), (2, 2), (0, 0)))
-    return jnp.concatenate([padded[:, tap : tap + steps] for tap in range(5)], axis=2)
-
-
-def columns_adjoint(grads, width):
-    total = 0.0
+FLATS = 16
+STEPS = 64
+C = 256
+BLOCK = 256
+
+
+def denoise_kernel(
+    film_cond_ref, noise_ref, actions_ref, keep_ref, blend_ref, adv_ref, time_ref,
+    win_ref, wres_ref, wmid_ref, wmid_t_ref, wout_ref, wout_t_ref, wtime_ref,
+    packed_ref, film_ref,
+    npad, cols, pad, mid, back, pre, res, unit1, act1, slope1, unit2, slope2, block, d_block, d_pred,
+    d_second, d_first, film, d_film, sum1, sum2, inv1, inv2, mean1, mean2,
+):
+    bf16, f32 = jnp.bfloat16, jnp.float32
+
+    def rows_of(f, size=STEPS):
+        return pl.ds(pl.multiple_of(f * size, size), size)
+
+    def one(f):
+        return pl.ds(f, 1)
+
+    def each(body, count=FLATS):
+        def step(f, carry):
+            body(f)
+            return carry
+
+        lax.fori_loop(0, count, step, 0)
+
+    lanes = lax.broadcasted_iota(jnp.int32, (C, C), 1)
+    row_ids = lax.broadcasted_iota(jnp.int32, (C, C), 0)
+    same = jnp.where(lanes // 32 == row_ids // 32, 1.0 / 2048.0, 0.0).astype(f32)
+
+    def group_mean(values):
+        return jnp.dot(values, same, preferred_element_type=f32, precision=lax.Precision.HIGHEST)
+
+    def dot(left, right):
+        return jnp.dot(left, right, preferred_element_type=f32)
+
+    npad[...] = jnp.zeros_like(npad)
+    pad[...] = jnp.zeros_like(pad)
+
+    def make_cols(f):
+        sample = rows_of(f // 8)
+        noisy = keep_ref[one(f)] * actions_ref[sample].astype(f32) + blend_ref[one(f)] * noise_ref[rows_of(f)].astype(f32)
+        noisy = noisy.astype(bf16).astype(f32)
+        npad[f, 8:72] = noisy
+        total = pltpu.roll(noisy, 114, 1)
+        for tap in range(5):
+            total = total + pltpu.roll(npad[f, 6 + tap : 70 + tap], 44 + 14 * tap, 1)
+        cols[rows_of(f)] = total.astype(bf16)
+
+    each(make_cols)
+
+    time_film = dot(time_ref[...], wtime_ref[...])
+    top = jnp.broadcast_to(film_cond_ref[0:1], (8, 2 * C))
+    low = jnp.broadcast_to(film_cond_ref[1:2], (8, 2 * C))
+    film[...] = jnp.concatenate([top, low], axis=0) + time_film
+
+    def first_conv(b):
+        rows = rows_of(b, BLOCK)
+        out = dot(cols[rows], win_ref[...])
+        pre[rows] = out
+        res[rows] = dot(cols[rows], wres_ref[...])
+
+    each(first_conv, 4)
+
+    def centre(inverse):
+        def total(f):
+            sum1[one(f)] = jnp.sum(pre[rows_of(f)], axis=0, keepdims=True)
+
+        each(total)
+        mean1[...] = group_mean(sum1[...])
+
+        def moved(f):
+            left = pre[rows_of(f)] - mean1[one(f)]
+            pre[rows_of(f)] = left
+            sum1[one(f)] = jnp.sum(left * left, axis=0, keepdims=True)
+
+        each(moved)
+        inverse[...] = lax.rsqrt(group_mean(sum1[...]) + 1e-05)
+
+    def mish_both(values):
+        small, right, above, rest = mish_parts(values)
+        inverse = 1.0 / (above + rest)
+        logistic = jnp.where(right, 1.0, small) / (1.0 + small)
+        ratio = above * inverse
+        value = values * ratio
+        return value, ratio + values * logistic * (rest * (2.0 * above + rest)) * (inverse * inverse)
+
+    centre(inv1)
+
+    def first_act(f):
+        unit = pre[rows_of(f)] * inv1[one(f)]
+        value, slope = mish_both(unit)
+        unit1[rows_of(f)] = unit
+        act1[rows_of(f)] = value
+        slope1[rows_of(f)] = slope
+        changed = film[one(f), 0:C] * value + film[one(f), C:]
+        pad[f, 8:72] = changed.astype(bf16).astype(f32)
+        for tap in range(5):
+            mid[rows_of(f), C * tap : C * (tap + 1)] = pad[f, 6 + tap : 70 + tap].astype(bf16)
+
+    each(first_act)
+
+    def second_conv(b):
+        rows = rows_of(b, BLOCK)
+        pre[rows] = dot(mid[rows], wmid_ref[...])
+
+    each(second_conv, 4)
+    centre(inv2)
+
+    def second_act(f):
+        unit = pre[rows_of(f)] * inv2[one(f)]
+        value, slope = mish_both(unit)
+        unit2[rows_of(f)] = unit
+        slope2[rows_of(f)] = slope
+        block[rows_of(f)] = (value + res[rows_of(f)]).astype(bf16)
+
+    each(second_act)
+
+    def errors(f, total):
+        rows = rows_of(f)
+        error = dot(block[rows], wout_ref[...]) - noise_ref[rows].astype(f32)
+        d_pred[rows] = (adv_ref[one(f)] * error * (2.0 / 896.0)).astype(bf16)
+        return total + error * error
+
+    err = lax.fori_loop(0, FLATS, errors, jnp.zeros((STEPS, 128), f32))
+    err_sum = jnp.sum(err) * (1.0 / 896.0)
+
+    def from_pred(b):
+        rows = rows_of(b, BLOCK)
+        out = dot(d_pred[rows], wout_t_ref[...])
+        pre[rows] = out
+        d_block[rows] = out.astype(bf16)
+
+    each(from_pred, 4)
+
+    def act_back(scale, unit, slope):
+        def totals(f):
+            grad = scale(f) * slope[rows_of(f)]
+            pre[rows_of(f)] = grad
+            sum1[one(f)] = jnp.sum(grad, axis=0, keepdims=True)
+            sum2[one(f)] = jnp.sum(grad * unit[rows_of(f)], axis=0, keepdims=True)
+
+        each(totals)
+        mean1[...] = group_mean(sum1[...])
+        mean2[...] = group_mean(sum2[...])
+
+    act_back(lambda f: pre[rows_of(f)], unit2, slope2)
+
+    def second_back(f):
+        grad = inv2[one(f)] * (pre[rows_of(f)] - mean1[one(f)] - unit2[rows_of(f)] * mean2[one(f)])
+        rounded = grad.astype(bf16)
+        d_second[rows_of(f)] = rounded
+        pad[f, 8:72] = rounded.astype(f32)
+        for tap in range(5):
+            back[rows_of(f), C * tap : C * (tap + 1)] = pad[f, 10 - tap : 74 - tap].astype(bf16)
+
+    each(second_back)
+
+    def mid_back(b):
+        rows = rows_of(b, BLOCK)
+        pre[rows] = dot(back[rows], wmid_t_ref[...])
+
+    each(mid_back, 4)
+
+    def film_back(f):
+        grad = pre[rows_of(f)]
+        d_film[one(f), 0:C] = jnp.sum(grad * act1[rows_of(f)], axis=0, keepdims=True)
+        d_film[one(f), C:] = jnp.sum(grad, axis=0, keepdims=True)
+
+    each(film_back)
+    film_ref[...] = jnp.zeros_like(film_ref)
+    film_ref[0:1] = jnp.sum(d_film[0:8], axis=0, keepdims=True)
+    film_ref[1:2] = jnp.sum(d_film[8:16], axis=0, keepdims=True)
+
+    act_back(lambda f: pre[rows_of(f)] * film[one(f), 0:C], unit1, slope1)
+
+    def first_back(f):
+        grad = inv1[one(f)] * (pre[rows_of(f)] - mean1[one(f)] - unit1[rows_of(f)] * mean2[one(f)])
+        d_first[rows_of(f)] = grad.astype(bf16)
+
+    each(first_back)
+
+    def over_rows(left, right):
+        return lax.dot_general(left, right, (((0,), (0,)), ((), ())), preferred_element_type=f32)
+
     for tap in range(5):
-        piece = grads[:, :, tap * width : (tap + 1) * width]
-        total = total + jnp.pad(piece, ((0, 0), (tap, 4 - tap), (0, 0)))
-    return total[:, 2:-2]
-
-
-def denoise(
-    film_cond, tsteps, advantage, actions, noise, w_in, w_mid, w_res, w_out, w_time, product
-):
-    row_count, levels = tsteps.shape
-    horizon, action_dims = (actions.shape[1], actions.shape[2])
-    channels = w_mid.shape[1]
-    flat = row_count * levels
-    matches = (tsteps[:, :, None] == jnp.arange(TSTEPS, dtype=jnp.int32)[None, None, :]).astype(
-        jnp.float32
+        grad = over_rows(d_second[...], mid[:, C * tap : C * (tap + 1)]).astype(bf16)
+        for s in range(4):
+            for half in range(2):
+                begin = 64 * (2 * tap + half)
+                packed_ref[s, begin : begin + 64] = grad[64 * s : 64 * (s + 1), 128 * half : 128 * (half + 1)]
+    lane = lax.broadcasted_iota(jnp.int32, (C, 128), 1)
+    inner = over_rows(d_first[...], cols[...])
+    skip = over_rows(d_block[...], cols[...])
+    out = over_rows(block[...], d_pred[...])
+    joined = jnp.where(lane < 70, inner, jnp.where(lane < 84, skip, jnp.where(lane < 98, out, err_sum))).astype(bf16)
+    timed = over_rows(time_ref[...], d_film[...].astype(bf16)).astype(bf16)
+    for s in range(4):
+        packed_ref[s, 640:704] = joined[64 * s : 64 * (s + 1)]
+        packed_ref[s, 704:960] = timed[:, 128 * s : 128 * (s + 1)]
+        packed_ref[s, 960:1024] = jnp.zeros((64, 128), bf16)
+
+
+def denoise(film_cond, tsteps, advantage, actions, noise, w_time, w_in, w_mid, w_res, w_out):
+    bf16, f32 = jnp.bfloat16, jnp.float32
+    flat = tsteps.reshape(FLATS, 1)
+    table = schedule()
+    picked = (flat == jnp.arange(TSTEPS, dtype=jnp.int32)[None]).astype(f32)
+    keep = jnp.sum(picked * jnp.asarray(np.sqrt(table), f32)[None], axis=1, keepdims=True)
+    blend = jnp.sum(picked * jnp.asarray(np.sqrt(1.0 - table), f32)[None], axis=1, keepdims=True)
+
+    def wide(values):
+        return jnp.broadcast_to(values, (FLATS, 128))
+
+    half_dim = w_time.shape[0] // 2
+    frequencies = jnp.exp(-math.log(10000.0) * jnp.arange(half_dim, dtype=f32) / (half_dim - 1))
+    angles = flat.astype(f32) * frequencies[None]
+    time_act = mish_value(jnp.concatenate([jnp.sin(angles), jnp.cos(angles)], axis=1)).astype(bf16)
+    noise_lanes = jnp.pad(noise.reshape(FLATS * STEPS, 14), ((0, 0), (84, 30)))
+    action_lanes = jnp.pad(actions.reshape(2 * STEPS, 14), ((0, 0), (84, 30)))
+    w_mid_t = w_mid.reshape(5, C, C).transpose(0, 2, 1).reshape(5 * C, C)
+    vmem = pl.BlockSpec(memory_space=pltpu.VMEM)
+    flat_rows = FLATS * STEPS
+    big, small = pltpu.VMEM((flat_rows, C), f32), pltpu.VMEM((FLATS, C), f32)
+    big16 = pltpu.VMEM((flat_rows, C), bf16)
+    return pl.pallas_call(
+        denoise_kernel,
+        out_shape=(jax.ShapeDtypeStruct((4, 1024, 128), bf16), jax.ShapeDtypeStruct((8, 2 * C), f32)),
+        in_specs=[vmem] * 14,
+        out_specs=(vmem, vmem),
+        scratch_shapes=[
+            pltpu.VMEM((FLATS, 80, 128), f32),
+            pltpu.VMEM((flat_rows, 128), bf16),
+            pltpu.VMEM((FLATS, 80, C), f32),
+            pltpu.VMEM((flat_rows, 5 * C), bf16),
+            pltpu.VMEM((flat_rows, 5 * C), bf16),
+            big, big, big, big, big, big, big,
+            big16, big16,
+            pltpu.VMEM((flat_rows, 128), bf16),
+            big16, big16,
+            pltpu.VMEM((FLATS, 2 * C), f32),
+            pltpu.VMEM((FLATS, 2 * C), f32),
+            small, small, small, small, small, small,
+        ],
+        compiler_params=pltpu.CompilerParams(vmem_limit_bytes=48 * 2**20),
+    )(
+        film_cond, noise_lanes, action_lanes, wide(keep), wide(blend), wide(advantage.reshape(FLATS, 1)), time_act,
+        jnp.pad(w_in, ((0, 58), (0, 0))), jnp.pad(w_res, ((70, 44), (0, 0))), w_mid, w_mid_t,
+        jnp.pad(w_out, ((0, 0), (84, 30))), jnp.pad(w_out.T, ((84, 30), (0, 0))), w_time,
     )
-    alpha = jnp.sum(matches * jnp.asarray(schedule(), jnp.float32)[None, None, :], axis=2)
-    keep_root = jnp.sqrt(alpha)[:, :, None, None]
-    noise_root = jnp.sqrt(1.0 - alpha)[:, :, None, None]
-    noisy_act = (
-        keep_root * actions.astype(jnp.float32)[:, None] + noise_root * noise.astype(jnp.float32)
-    ).astype(jnp.bfloat16)
-    noisy_act = noisy_act.reshape(flat, horizon, action_dims)
-    half_dim = w_time.shape[0] // 2
-    frequencies = jnp.exp(
-        -math.log(10000.0) * jnp.arange(half_dim, dtype=jnp.float32) / (half_dim - 1)
-    )
-    angles = tsteps.astype(jnp.float32)[:, :, None] * frequencies[None, None, :]
-    embedded = jnp.concatenate([jnp.sin(angles), jnp.cos(angles)], axis=2)
-    time_act = mish_value(embedded).astype(jnp.bfloat16).reshape(flat, 2 * half_dim)
-    film = film_cond[:, None, :] + product(
-        "rld,dc->rlc", time_act.reshape(row_count, levels, -1), w_time
-    )
-    film = film.reshape(flat, 2 * channels)
-    film_scale = film[:, None, :channels]
-    film_shift = film[:, None, channels:]
-    columns_in = columns(noisy_act)
-    pre_first = product("mhk,kc->mhc", columns_in, w_in)
-    act_first, first_back = jax.vjp(norm_act, pre_first)
-    modulated = (film_scale * act_first + film_shift).astype(jnp.bfloat16)
-    columns_mid = columns(modulated)
-    pre_second = product("mhk,kc->mhc", columns_mid, w_mid)
-    act_second, second_back = jax.vjp(norm_act, pre_second)
-    block_out = (act_second + product("mha,ac->mhc", noisy_act, w_res)).astype(jnp.bfloat16)
-    predicted = product("mhc,ca->mha", block_out, w_out)
-    errors = predicted - noise.reshape(flat, horizon, action_dims).astype(jnp.float32)
-    err_sum = jnp.sum(errors * errors) / (horizon * action_dims)
-    weights = advantage.reshape(flat, 1, 1)
-    d_pred = (2.0 * weights * errors / (horizon * action_dims)).astype(jnp.bfloat16)
-    grad_out = product("mhc,mha->ca", block_out, d_pred)
-    d_block = product("mha,ca->mhc", d_pred, w_out)
-    grad_res = product("mha,mhc->ac", noisy_act, d_block.astype(jnp.bfloat16))
-    d_second = second_back(d_block)[0].astype(jnp.bfloat16)
-    grad_mid = product("mhk,mhc->kc", columns_mid, d_second)
-    d_columns = product("mhc,kc->mhk", d_second, w_mid)
-    d_modulated = columns_adjoint(d_columns, channels)
-    d_film = jnp.concatenate(
-        [jnp.sum(d_modulated * act_first, axis=1), jnp.sum(d_modulated, axis=1)], axis=1
-    )
-    d_first = first_back(film_scale * d_modulated)[0].astype(jnp.bfloat16)
-    grad_in = product("mhk,mhc->kc", columns_in, d_first)
-    grad_time = product("md,mc->dc", time_act, d_film.astype(jnp.bfloat16))
-    d_film_cond = jnp.sum(d_film.reshape(row_count, levels, -1), axis=1)
-    return (err_sum, grad_in, grad_mid, grad_res, grad_out, grad_time, d_film_cond)
 
 
 def body(
@@ -619,33 +785,20 @@
     def own(values):
         return lax.dynamic_slice_in_dim(values, begin, 2, 0)
 
-    err_sum, grad_in, grad_mid, grad_res, grad_out, grad_time, d_film_cond = denoise(
-        film_cond, own(tsteps), own(advantage), own(actions), own(noise), w_in, w_mid, w_res, w_out, w_time, contract
+    packed, d_film_cond = denoise(
+        film_cond, own(tsteps), own(advantage), own(actions), own(noise), w_time, w_in, w_mid, w_res, w_out
     )
-    blocks = []
-    for s in range(4):
-        part = slice(64 * s, 64 * (s + 1))
-        upper = jnp.concatenate([grad_mid[:640, part], grad_mid[640:, part]], axis=1)
-        low = jnp.concatenate(
-            [grad_res[:, part], jnp.zeros((2, 64)), grad_out[part].T, jnp.zeros((2, 64)), jnp.full((48, 64), err_sum)], axis=0
-        )
-        middle = jnp.concatenate([jnp.pad(grad_in[:, part], ((0, 10), (0, 0))), low], axis=1)
-        blocks.append(
-            jnp.concatenate([upper, middle, grad_time[:, 128 * s : 128 * (s + 1)], jnp.zeros((48, 128))], axis=0)
-        )
-    packed = jnp.stack(blocks).astype(jnp.bfloat16)
-    film_pad = jnp.pad(d_film_cond, ((0, 6), (0, 0)))
-    total, grad_w_cond, grad_cond = collect(cond_all, film_pad, packed, w_cond)
-    side = total[640:720, 64:]
+    total, grad_w_cond, grad_cond = collect(cond_all, d_film_cond, packed, w_cond)
+    joined = total[640:704]
     return (
-        total[640:710, :64],
-        jnp.concatenate([total[:640, :64], total[:640, 64:]], axis=0),
-        side[0:14],
-        side[16:30].T,
-        total[720:976],
+        joined[:, 0:70].T,
+        total[0:640].reshape(10, 64, 128).transpose(0, 2, 1).reshape(1280, 64),
+        joined[:, 70:84].T,
+        joined[:, 84:98],
+        total[704:960],
         grad_w_cond,
         grad_cond,
-        side[32, 0:1] / 2048.0,
+        joined[0, 98:99] / 2048.0,
     )
 
 

time: 356 us -> 326 us (0.916)
  Pallas kernels: 286 us -> 305 us
  other arithmetic: 17.4 us -> 0.34 us
  local copies, waits for them, and re-layouts: 31.5 us -> 15.4 us
  matrix products: 16.1 us -> 2.25 us
    pallas_call x0 -> x1, Pallas kernels: none -> 18.7 us  [denoise(): pl.pallas_call(denoise_kernel, out_shape=(jax.ShapeDtypeStruct((4, 1024,...]
    concatenate x7 -> x0, local copies, waits for them, and re-layouts: 15.4 us -> none  [the longest x4 14.5 us: body(): jnp.concatenate([grad_res[:, part], jnp.zeros((2, 64)), grad_out[part].T,...]
    dot_general x12 -> x0, matrix products: 14 us -> none  [contract(): return jnp.einsum(form, left, right, preferred_element_type=jnp.float32)]
    reduce_sum x17 -> x1, other arithmetic: 7.65 us -> 0.18 us  [denoise(): jnp.sum(picked * jnp.asarray(np.sqrt(1.0 - table), f32)[None], axis=1, ke...]
    convert_element_type x6 -> x2, other arithmetic: 4.95 us -> 0.03 us  [the longest x1 0.02 us: denoise(): mish_value(jnp.concatenate([jnp.sin(angles), jnp.cos(angles)], axis=1))]
    unnamed x53 -> x38, local copies, waits for them, and re-layouts: 5.37 us -> 9.96 us
    slice x11 -> x4, local copies, waits for them, and re-layouts: 5.14 us -> 1.34 us  [the longest x1 0.66 us: body(): total[704:960]]
where the time goes in v2:
time: 326 us; the launch traced here: 325 us
  Pallas kernels  305 us (94%)
  local copies, waits for them, and re-layouts  15.4 us (5%)
    pallas_call x1, Pallas kernels, trunk(): pl.pallas_call(trunk_kernel, out_shape=(jax.ShapeDtypeStruct((MICRO, 8, D...  251 us
    pallas_call x1, Pallas kernels, collect(): pl.pallas_call(collect_kernel, out_shape=(jax.ShapeDtypeStruct((1024, 128...  34.9 us
    pallas_call x1, Pallas kernels, denoise(): pl.pallas_call(denoise_kernel, out_shape=(jax.ShapeDtypeStruct((4, 1024,...  18.7 us
    unnamed x38, local copies, waits for them, and re-layouts  9.96 us

profile of v2, /device:TPU:1, one launch (start us, length us, event | category | flops | bytes accessed | tf_op | source)
XLA Modules:
  0.0 325.2 jit_solution(12306915501142767853)
XLA Ops:
  0.6 0.0 copy-start
  0.7 1.1 copy-done.3
  1.8 1.1 copy-done.4
  2.8 0.7 copy-done.8
  3.5 251.0 %shard_map.224 = (f32[4,8,2560]{2,1,0:T(8,128)S(1)}, bf16[2560,512]{1,0:T(8,128)(2,1)}) custom-call(bf16[256,1280]{1,0:T(8,128)(2,1)} %x_ref.1, bf16[1,2560]{1,0:T(2,128)(2,1)S(1)} %copy-done.8, bf16[160,1792]{1,0:T(8,128)(2,1)S(1)} %bitcast.35, bf16[160,1792]{1,0:T(8,128)(2,1)S(1)} %bitcast.36, bf16[160,1792]{1,0:T(8,128)(2,1)} %bitcast.40, ...), custom_call_target="tpu_custom_call" | custom-call | tf_op jit(solution)/shard_map/pallas_call | solution.py:287
  254.6 0.0 copy-start.12
  254.6 0.0 copy-start.14
  254.6 0.0 copy-start.15
  254.6 0.0 copy-start.13
  254.6 0.0 copy-start.9
  254.6 0.0 copy-start.11
  254.6 0.0 copy-start.10
  254.7 2.3 fusion.8.film_cond_ref
  256.9 0.7 copy-done.5
  257.7 0.2 copy.43
  257.9 0.1 pad.24.noise_ref
  258.0 0.8 constant_dynamic-slice_fusion.2
  258.8 0.1 copy.44
  258.9 0.1 pad.25.actions_ref
  259.0 0.1 constant_dynamic-slice_fusion.1
  259.1 0.1 copy.45
  259.2 0.1 eq.15
  259.3 0.2 select_reduce_fusion
  259.5 0.1 broadcast_in_dim.12.keep_ref
  259.5 0.1 broadcast_in_dim.13.blend_ref
  259.6 0.1 constant_dynamic-slice_fusion
  259.7 0.1 copy.46
  259.8 0.1 broadcast_in_dim.14
  259.8 0.1 broadcast_in_dim.15.adv_ref
  259.9 0.1 multiply_sine_fusion
  260.2 0.2 copy.47
  260.4 0.7 copy.48
  261.2 0.9 pad.28.wout_ref
  262.1 0.0 copy-start.7
  262.1 0.9 copy-done.7
  263.1 18.7 %shard_map.225 = (bf16[4,1024,128]{2,1,0:T(8,128)(2,1)S(1)}, f32[8,512]{1,0:T(8,128)S(1)}) custom-call(f32[2,512]{1,0:T(2,128)S(1)} %fusion.8.film_cond_ref, bf16[1024,128]{1,0:T(8,128)(2,1)S(1)} %pad.24.noise_ref, bf16[128,128]{1,0:T(8,128)(2,1)S(1)} %pad.25.actions_ref, f32[16,128]{1,0:T(8,128)S(1)} %broadcast_in_dim.12.keep_ref, ...), custom_call_target="tpu_custom_call" | custom-call | tf_op jit(solution)/shard_map/pallas_call | solution.py:747
  281.7 1.0 copy-done.6
  282.7 34.9 %shard_map.226 = (f32[1024,128]{1,0:T(8,128)S(1)}, f32[1280,128]{1,0:T(8,128)S(1)}, f32[4,1280]{1,0:T(4,128)S(1)}) custom-call(f32[4,8,2560]{2,1,0:T(8,128)S(1)} %copy-done.6, f32[8,512]{1,0:T(8,128)S(1)} %get-tuple-element.17.film_ref, bf16[4,1024,128]{2,1,0:T(8,128)(2,1)S(1)} %get-tuple-element.18.grads_ref, bf16[1280,512]{1,0:T(8,128)(2,1)S(1)} %copy-done.1), custom_call_target="tpu_custom_call" | custom-call | tf_op jit(solution)/shard_map/pallas_call | solution.py:485
  317.6 0.6 slice_bitcast_fusion.1
  318.2 0.2 copy.49
  318.5 0.8 copy.54
  319.3 0.1 fusion.17
  319.4 0.7 copy.50
  320.0 0.7 copy.51
  320.7 0.7 slice.35
  321.4 0.6 slice.36
  322.6 0.8 copy.57
  323.5 0.6 copy.58
  (25 shorter events, 0.1 us)
Async XLA Ops:
  0.6 257.0 %copy-start = (bf16[16,8,64,14]{2,1,3,0:T(8,128)(2,1)S(1)}, bf16[16,8,64,14]{2,1,3,0:T(8,128)(2,1)}, u32[]{:S(2)}) copy-start(bf16[16,8,64,14]{2,1,3,0:T(8,128)(2,1)} %param.31) | copy-start | bytes 688132
  0.6 1.1 copy-start.3
  1.8 1.1 copy-start.4
  2.8 0.7 copy-start.8
  254.6 4.5 %copy-start.12 = (s32[16,8]{0,1:T(8,128)S(1)}, s32[16,8]{0,1:T(8,128)}, u32[]{:S(2)}) copy-start(s32[16,8]{0,1:T(8,128)} %param.28) | copy-start | bytes 1540
  254.6 4.7 %copy-start.14 = (f32[100]{0:T(128)S(1)}, f32[100]{0:T(128)}, u32[]{:S(2)}) copy-start(f32[100]{0:T(128)} %constant.49.clone) | copy-start | bytes 1204
  254.6 4.7 %copy-start.15 = (f32[100]{0:T(128)S(1)}, f32[100]{0:T(128)}, u32[]{:S(2)}) copy-start(f32[100]{0:T(128)} %constant.48.clone) | copy-start | bytes 1204
  254.6 5.0 %copy-start.13 = (f32[16,8]{0,1:T(8,128)S(1)}, f32[16,8]{0,1:T(8,128)}, u32[]{:S(2)}) copy-start(f32[16,8]{0,1:T(8,128)} %param.29) | copy-start | bytes 1540
  254.6 5.5 %copy-start.9 = (bf16[70,256]{1,0:T(8,128)(2,1)S(1)}, bf16[70,256]{1,0:T(8,128)(2,1)}, u32[]{:S(2)}) copy-start(bf16[70,256]{1,0:T(8,128)(2,1)} %param.24) | copy-start | bytes 107524
  254.6 5.5 %copy-start.11 = (bf16[14,256]{1,0:T(8,128)(2,1)S(1)}, bf16[14,256]{1,0:T(8,128)(2,1)}, u32[]{:S(2)}) copy-start(bf16[14,256]{1,0:T(8,128)(2,1)} %param.26) | copy-start | bytes 21508
  254.6 5.5 %copy-start.2 = (bf16[1280,256]{1,0:T(8,128)(2,1)S(1)}, bf16[1280,256]{1,0:T(8,128)(2,1)}, u32[]{:S(2)}) copy-start(bf16[1280,256]{1,0:T(8,128)(2,1)} %wmid_ref.1) | copy-start | bytes 1966084
  254.6 5.8 %copy-start.10 = (bf16[256,14]{0,1:T(8,128)(2,1)S(1)}, bf16[256,14]{0,1:T(8,128)(2,1)}, u32[]{:S(2)}) copy-start(bf16[256,14]{0,1:T(8,128)(2,1)} %param.27) | copy-start | bytes 21508
  256.9 0.7 copy-start.5
  257.6 24.1 %copy-start.1 = (bf16[1280,512]{1,0:T(8,128)(2,1)S(1)}, bf16[1280,512]{1,0:T(8,128)(2,1)}, u32[]{:S(2)}) copy-start(bf16[1280,512]{1,0:T(8,128)(2,1)} %wc_ref.3) | copy-start | bytes 3932164
  262.1 1.0 copy-start.7
  281.7 1.0 copy-start.6

commit v3 on v2

--- a/solution.py
+++ b/solution.py
@@ -14,6 +14,10 @@
 SIDE = 4
 MICRO = 4
 ROWS = 32
+BATCHES = 2
+OWN = 64
+PART = 512
+PARTS = 5
 D = 2560
 HALF = 1280
 FH = 1792
@@ -33,7 +37,7 @@
     x_ref, gain_ref, wg_ref, wu_ref, wd_ref, wc_ref,
     cond_ref, wcond_ref,
     weights, first, arrived, leaving, normed, hidden, partial, share, other,
-    own_sem, gs_sem, gr_sem, ms_sem, mr_sem, zs_sem, zr_sem, cs_sem, cr_sem,
+    own_sem, gs_sem, gr_sem, ms_sem, mr_sem, ps_sem, pr_sem, zs_sem, zr_sem, cs_sem, cr_sem,
 ):
     dp, seg, core = lax.axis_index("dp"), lax.axis_index("segment"), lax.axis_index("mp")
     y, x = dp // SIDE, dp % SIDE
@@ -137,11 +141,14 @@
 
     here = pl.ds(pl.multiple_of(core * HALF, 128), HALF)
     there = pl.ds(pl.multiple_of(sibling * HALF, 128), HALF)
+    def slot_of(j, features):
+        return first.at[j // 2, pl.ds(32 * (j % 2), ROWS), features]
+
     for j in range(MICRO):
         src = x_ref.at[pl.ds(pl.multiple_of(64 * j + 32 * sibling, 16), ROWS), :]
-        sibling_copy(j, src, first.at[j, :, here]).start()
+        sibling_copy(j, src, slot_of(j, here)).start()
         kept = pltpu.make_async_copy(
-            x_ref.at[pl.ds(pl.multiple_of(64 * j + 32 * core, 16), ROWS), :], first.at[j, :, here], own_sem.at[3 + j]
+            x_ref.at[pl.ds(pl.multiple_of(64 * j + 32 * core, 16), ROWS), :], slot_of(j, here), own_sem.at[3 + j]
         )
         kept.start()
         own.append(kept)
@@ -177,19 +184,32 @@
             receive(chunk, 16 + kind)
             send(chunk, 18 + kind)
     for j in range(MICRO):
-        sibling_copy(j, first.at[j, :, there], first.at[j, :, there]).wait_recv()
-    for chunk in chunks:
-        for slot in range(4):
-            for kind in (2, 3):
-                receive(chunk, 4 + 4 * slot + kind)
-    for keep in own:
+        sibling_copy(j, slot_of(j, there), slot_of(j, there)).wait_recv()
+    for keep in own[3:7]:
         keep.wait()
 
-    def z_copy(j):
+    def finish_gather():
+        for chunk in chunks:
+            for slot in range(4):
+                for kind in (2, 3):
+                    receive(chunk, 4 + 4 * slot + kind)
+        for keep in own[:3] + own[7:]:
+            keep.wait()
+
+    def z_copy(b, g):
         return pltpu.make_async_remote_copy(
-            src_ref=leaving.at[j], dst_ref=arrived.at[j], send_sem=zs_sem.at[j], recv_sem=zr_sem.at[j],
+            src_ref=leaving.at[b, g], dst_ref=arrived.at[b, g], send_sem=zs_sem.at[b, g], recv_sem=zr_sem.at[b, g],
             device_id={"segment": (seg + 1) % 4}, device_id_type=MESH,
         )
+
+    def share_copy(b, g):
+        return pltpu.make_async_remote_copy(
+            src_ref=share.at[b, g], dst_ref=other.at[b, g], send_sem=ps_sem.at[b, g], recv_sem=pr_sem.at[b, g],
+            device_id={"mp": sibling}, device_id_type=MESH,
+        )
+
+    def normed_copy(b):
+        return sibling_copy(5 + b, normed.at[b, pl.ds(0, OWN)], normed.at[b, pl.ds(OWN, OWN)])
 
     def cond_copy(j, target):
         return pltpu.make_async_remote_copy(
@@ -197,76 +217,97 @@
             device_id={"segment": target}, device_id_type=MESH,
         )
 
-    gain = gain_ref[...].astype(jnp.float32)
-
-    def micro(j, carry):
-        @pl.when(seg == 0)
-        def _():
-            arrived[j] = first[j]
-
+    def columns_of(g):
+        return slice(PART * g, PART * (g + 1))
+
+    def normalize(b):
+        states = [arrived[b, g].astype(jnp.float32) for g in range(PARTS)]
+        total = sum(jnp.sum(state * state, axis=1, keepdims=True) for state in states)
+        factor = lax.rsqrt(total * (1.0 / D) + 1e-05)
+        for g in range(PARTS):
+            gain = gain_ref[:, columns_of(g)].astype(jnp.float32)
+            normed[b, 0:OWN, columns_of(g)] = (states[g] * factor * gain).astype(jnp.bfloat16)
+        normed_copy(b).start()
+
+    def batch(b, carry):
         @pl.when(seg > 0)
         def _():
-            z_copy(j).wait_recv()
-
-        state = arrived[j].astype(jnp.float32)
-        factor = lax.rsqrt(jnp.mean(state * state, axis=1, keepdims=True) + 1e-05)
-        normed[j, 0:ROWS] = (state * factor * gain).astype(jnp.bfloat16)
-        swap = sibling_copy(5 + j, normed.at[j, pl.ds(0, ROWS)], normed.at[j, pl.ds(ROWS, ROWS)])
-        swap.start()
-        swap.wait_recv()
-
-        def up(n, carry):
-            cols = pl.ds(pl.multiple_of(n * TILE, TILE), TILE)
-            rows = normed[j]
+            for g in range(PARTS):
+                z_copy(b, g).wait_recv()
+            normalize(b)
+
+        normed_copy(b).wait_recv()
+        for n in range(FH // TILE):
+            cols = slice(n * TILE, (n + 1) * TILE)
+            rows = normed[b]
             gate = jnp.dot(rows, weights[0, :, cols], preferred_element_type=jnp.float32)
             lift = jnp.dot(rows, weights[1, :, cols], preferred_element_type=jnp.float32)
             hidden[:, cols] = (gate / (1.0 + jnp.exp(-gate)) * lift).astype(jnp.bfloat16)
-            return carry
-
-        lax.fori_loop(0, FH // TILE, up, 0)
-
-        def down(n, carry):
-            cols = pl.ds(pl.multiple_of(n * TILE, TILE), TILE)
-            out = lax.dot_general(
-                hidden[...], weights[2, cols, :], (((1,), (1,)), ((), ())), preferred_element_type=jnp.float32
-            )
-            partial[:, cols] = out[0:ROWS]
-            share[j, :, cols] = out[ROWS:].astype(jnp.bfloat16)
-            return carry
-
-        lax.fori_loop(0, D // TILE, down, 0)
-        back = sibling_copy(9 + j, share.at[j], other.at[j])
-        back.start()
-        back.wait_recv()
-        result = (arrived[j].astype(jnp.float32) + (partial[...] + other[j].astype(jnp.float32))).astype(jnp.bfloat16)
-
-        @pl.when(seg < 3)
-        def _():
-            leaving[j] = result
-            z_copy(j).start()
+
+        def finish(g):
+            share_copy(b, g).wait_recv()
+            whole = partial[g] + other[b, g].astype(jnp.float32)
+            leaving[b, g] = (arrived[b, g].astype(jnp.float32) + whole).astype(jnp.bfloat16)
+
+            @pl.when(seg < 3)
+            def _():
+                z_copy(b, g).start()
+
+        for g in range(PARTS):
+            for half in range(2):
+                part = slice(TILE * half, TILE * (half + 1))
+                out = lax.dot_general(
+                    hidden[...], weights[2, PART * g + TILE * half : PART * g + TILE * (half + 1), :],
+                    (((1,), (1,)), ((), ())), preferred_element_type=jnp.float32,
+                )
+                partial[g, :, part] = out[0:OWN]
+                share[b, g, :, part] = out[OWN:].astype(jnp.bfloat16)
+            share_copy(b, g).start()
+            if g > 0:
+                finish(g - 1)
+        finish(PARTS - 1)
 
         @pl.when(seg == 3)
         def _():
-            mean = jnp.mean(result.astype(jnp.float32).reshape(2, 16, D), axis=1)
-            cond_ref[j, 0:2] = mean.astype(jnp.bfloat16).astype(jnp.float32)
-            for target in range(3):
-                cond_copy(j, target).start()
+            for half in range(2):
+                for g in range(PARTS):
+                    rows = leaving[b, g, ROWS * half : ROWS * (half + 1)].astype(jnp.float32)
+                    mean = jnp.mean(rows.reshape(2, 16, PART), axis=1)
+                    cond_ref[2 * b + half, 0:2, columns_of(g)] = mean.astype(jnp.bfloat16).astype(jnp.float32)
+                for target in range(3):
+                    cond_copy(2 * b + half, target).start()
 
         return carry
 
-    lax.fori_loop(0, MICRO, micro, 0)
+    @pl.when(seg == 0)
+    def _():
+        for b in range(BATCHES):
+            for g in range(PARTS):
+                arrived[b, g] = first[b, :, columns_of(g)]
+            normalize(b)
+
+    finish_gather()
+    lax.fori_loop(0, BATCHES, batch, 0)
 
     for chunk in chunks:
         for number in range(20):
             sent(chunk, number)
+    for b in range(BATCHES):
+        normed_copy(b).wait_send()
+        for g in range(PARTS):
+            share_copy(b, g).wait_send()
+
+    @pl.when(seg < 3)
+    def _():
+        for b in range(BATCHES):
+            for g in range(PARTS):
+                z_copy(b, g).wait_send()
+
     for j in range(MICRO):
-        sibling_copy(j, x_ref.at[pl.ds(0, ROWS), :], first.at[j, :, there]).wait_send()
-        sibling_copy(5 + j, normed.at[j, pl.ds(0, ROWS)], normed.at[j, pl.ds(ROWS, ROWS)]).wait_send()
-        sibling_copy(9 + j, share.at[j], other.at[j]).wait_send()
+        sibling_copy(j, x_ref.at[pl.ds(0, ROWS), :], slot_of(j, there)).wait_send()
 
         @pl.when(seg < 3)
         def _(j=j):
-            z_copy(j).wait_send()
             cond_copy(j, 0).wait_recv()
 
         @pl.when(seg == 3)
@@ -294,21 +335,23 @@
         out_specs=(vmem, anywhere),
         scratch_shapes=[
             pltpu.VMEM((3, D, FH), bf16),
-            pltpu.VMEM((MICRO, ROWS, D), bf16),
-            pltpu.VMEM((MICRO, ROWS, D), bf16),
-            pltpu.VMEM((MICRO, ROWS, D), bf16),
-            pltpu.VMEM((MICRO, 2 * ROWS, D), bf16),
-            pltpu.VMEM((2 * ROWS, FH), bf16),
-            pltpu.VMEM((ROWS, D), jnp.float32),
-            pltpu.VMEM((MICRO, ROWS, D), bf16),
-            pltpu.VMEM((MICRO, ROWS, D), bf16),
+            pltpu.VMEM((BATCHES, OWN, D), bf16),
+            pltpu.VMEM((BATCHES, PARTS, OWN, PART), bf16),
+            pltpu.VMEM((BATCHES, PARTS, OWN, PART), bf16),
+            pltpu.VMEM((BATCHES, 2 * OWN, D), bf16),
+            pltpu.VMEM((2 * OWN, FH), bf16),
+            pltpu.VMEM((PARTS, OWN, PART), jnp.float32),
+            pltpu.VMEM((BATCHES, PARTS, OWN, PART), bf16),
+            pltpu.VMEM((BATCHES, PARTS, OWN, PART), bf16),
             dma((8,)),
             dma((6, 20)),
             dma((6, 20)),
-            dma((13,)),
-            dma((13,)),
-            dma((MICRO,)),
-            dma((MICRO,)),
+            dma((7,)),
+            dma((7,)),
+            dma((BATCHES, PARTS)),
+            dma((BATCHES, PARTS)),
+            dma((BATCHES, PARTS)),
+            dma((BATCHES, PARTS)),
             dma((MICRO, 3)),
             dma((MICRO,)),
         ],

time: 326 us -> 301 us (0.923)
  Pallas kernels: 305 us -> 280 us
    pallas_call x1, Pallas kernels: 251 us -> 225 us  [trunk(): pl.pallas_call(trunk_kernel, out_shape=(jax.ShapeDtypeStruct((MICRO, 8, D...]
where the time goes in v3:
time: 301 us
  Pallas kernels  280 us (93%)
  local copies, waits for them, and re-layouts  15.4 us (5%)
    pallas_call x1, Pallas kernels, trunk(): pl.pallas_call(trunk_kernel, out_shape=(jax.ShapeDtypeStruct((MICRO, 8, D...  225 us
    pallas_call x1, Pallas kernels, collect(): pl.pallas_call(collect_kernel, out_shape=(jax.ShapeDtypeStruct((1024, 128...  36.1 us
    pallas_call x1, Pallas kernels, denoise(): pl.pallas_call(denoise_kernel, out_shape=(jax.ShapeDtypeStruct((4, 1024,...  18.8 us
    unnamed x38, local copies, waits for them, and re-layouts  9.96 us

profile of v3, /device:TPU:1, one launch (start us, length us, event | category | flops | bytes accessed | tf_op | source)
XLA Modules:
  0.0 301.0 jit_solution(10974835748746173008)
XLA Ops:
  0.6 0.0 copy-start
  0.7 1.1 copy-done.3
  1.8 1.1 copy-done.4
  2.8 0.7 copy-done.8
  3.5 225.4 %shard_map.224 = (f32[4,8,2560]{2,1,0:T(8,128)S(1)}, bf16[2560,512]{1,0:T(8,128)(2,1)}) custom-call(bf16[256,1280]{1,0:T(8,128)(2,1)} %x_ref.1, bf16[1,2560]{1,0:T(2,128)(2,1)S(1)} %copy-done.8, bf16[160,1792]{1,0:T(8,128)(2,1)S(1)} %bitcast.35, bf16[160,1792]{1,0:T(8,128)(2,1)S(1)} %bitcast.36, bf16[160,1792]{1,0:T(8,128)(2,1)} %bitcast.40, ...), custom_call_target="tpu_custom_call" | custom-call | tf_op jit(solution)/shard_map/pallas_call | solution.py:328
  228.9 0.0 copy-start.12
  228.9 0.0 copy-start.14
  228.9 0.0 copy-start.15
  228.9 0.0 copy-start.13
  229.0 0.0 copy-start.9
  229.0 0.0 copy-start.11
  229.0 0.0 copy-start.2
  229.0 2.3 fusion.8.film_cond_ref
  231.3 0.7 copy-done.5
  232.0 0.2 copy.43
  232.2 0.1 pad.24.noise_ref
  232.4 0.8 constant_dynamic-slice_fusion.2
  233.2 0.1 copy.44
  233.3 0.1 pad.25.actions_ref
  233.4 0.1 constant_dynamic-slice_fusion.1
  233.5 0.1 copy.45
  233.5 0.1 eq.15
  233.6 0.2 select_reduce_fusion
  233.8 0.1 broadcast_in_dim.12.keep_ref
  233.9 0.1 broadcast_in_dim.13.blend_ref
  234.0 0.1 constant_dynamic-slice_fusion
  234.0 0.1 copy.46
  234.1 0.1 broadcast_in_dim.14
  234.2 0.1 broadcast_in_dim.15.adv_ref
  234.3 0.1 multiply_sine_fusion
  234.5 0.2 copy.47
  234.8 0.7 copy.48
  235.5 0.9 pad.28.wout_ref
  236.5 0.9 copy-done.7
  237.4 18.8 %shard_map.225 = (bf16[4,1024,128]{2,1,0:T(8,128)(2,1)S(1)}, f32[8,512]{1,0:T(8,128)S(1)}) custom-call(f32[2,512]{1,0:T(2,128)S(1)} %fusion.8.film_cond_ref, bf16[1024,128]{1,0:T(8,128)(2,1)S(1)} %pad.24.noise_ref, bf16[128,128]{1,0:T(8,128)(2,1)S(1)} %pad.25.actions_ref, f32[16,128]{1,0:T(8,128)S(1)} %broadcast_in_dim.12.keep_ref, ...), custom_call_target="tpu_custom_call" | custom-call | tf_op jit(solution)/shard_map/pallas_call | solution.py:790
  256.3 0.0 copy-start.6
  256.3 1.0 copy-done.6
  257.2 36.1 %shard_map.226 = (f32[1024,128]{1,0:T(8,128)S(1)}, f32[1280,128]{1,0:T(8,128)S(1)}, f32[4,1280]{1,0:T(4,128)S(1)}) custom-call(f32[4,8,2560]{2,1,0:T(8,128)S(1)} %copy-done.6, f32[8,512]{1,0:T(8,128)S(1)} %get-tuple-element.17.film_ref, bf16[4,1024,128]{2,1,0:T(8,128)(2,1)S(1)} %get-tuple-element.18.grads_ref, bf16[1280,512]{1,0:T(8,128)(2,1)S(1)} %copy-done.1), custom_call_target="tpu_custom_call" | custom-call | tf_op jit(solution)/shard_map/pallas_call | solution.py:528
  293.4 0.6 slice_bitcast_fusion.1
  294.0 0.2 copy.49
  294.2 0.8 copy.54
  295.1 0.1 fusion.17
  295.1 0.7 copy.50
  295.8 0.7 copy.51
  296.5 0.7 slice.35
  297.2 0.6 slice.36
  298.4 0.8 copy.57
  299.2 0.6 copy.58
  (25 shorter events, 0.1 us)
Async XLA Ops:
  0.6 231.4 %copy-start = (bf16[16,8,64,14]{2,1,3,0:T(8,128)(2,1)S(1)}, bf16[16,8,64,14]{2,1,3,0:T(8,128)(2,1)}, u32[]{:S(2)}) copy-start(bf16[16,8,64,14]{2,1,3,0:T(8,128)(2,1)} %param.31) | copy-start | bytes 688132
  0.6 1.1 copy-start.3
  1.8 1.1 copy-start.4
  2.8 0.7 copy-start.8
  228.9 4.5 %copy-start.12 = (s32[16,8]{0,1:T(8,128)S(1)}, s32[16,8]{0,1:T(8,128)}, u32[]{:S(2)}) copy-start(s32[16,8]{0,1:T(8,128)} %param.28) | copy-start | bytes 1540
  228.9 4.7 %copy-start.14 = (f32[100]{0:T(128)S(1)}, f32[100]{0:T(128)}, u32[]{:S(2)}) copy-start(f32[100]{0:T(128)} %constant.49.clone) | copy-start | bytes 1204
  228.9 4.7 %copy-start.15 = (f32[100]{0:T(128)S(1)}, f32[100]{0:T(128)}, u32[]{:S(2)}) copy-start(f32[100]{0:T(128)} %constant.48.clone) | copy-start | bytes 1204
  228.9 5.0 %copy-start.13 = (f32[16,8]{0,1:T(8,128)S(1)}, f32[16,8]{0,1:T(8,128)}, u32[]{:S(2)}) copy-start(f32[16,8]{0,1:T(8,128)} %param.29) | copy-start | bytes 1540
  229.0 5.5 %copy-start.9 = (bf16[70,256]{1,0:T(8,128)(2,1)S(1)}, bf16[70,256]{1,0:T(8,128)(2,1)}, u32[]{:S(2)}) copy-start(bf16[70,256]{1,0:T(8,128)(2,1)} %param.24) | copy-start | bytes 107524
  229.0 5.5 %copy-start.11 = (bf16[14,256]{1,0:T(8,128)(2,1)S(1)}, bf16[14,256]{1,0:T(8,128)(2,1)}, u32[]{:S(2)}) copy-start(bf16[14,256]{1,0:T(8,128)(2,1)} %param.26) | copy-start | bytes 21508
  229.0 5.5 %copy-start.2 = (bf16[1280,256]{1,0:T(8,128)(2,1)S(1)}, bf16[1280,256]{1,0:T(8,128)(2,1)}, u32[]{:S(2)}) copy-start(bf16[1280,256]{1,0:T(8,128)(2,1)} %wmid_ref.1) | copy-start | bytes 1966084
  229.0 5.8 %copy-start.10 = (bf16[256,14]{0,1:T(8,128)(2,1)S(1)}, bf16[256,14]{0,1:T(8,128)(2,1)}, u32[]{:S(2)}) copy-start(bf16[256,14]{0,1:T(8,128)(2,1)} %param.27) | copy-start | bytes 21508
  231.3 0.7 copy-start.5
  232.0 24.3 %copy-start.1 = (bf16[1280,512]{1,0:T(8,128)(2,1)S(1)}, bf16[1280,512]{1,0:T(8,128)(2,1)}, u32[]{:S(2)}) copy-start(bf16[1280,512]{1,0:T(8,128)(2,1)} %wc_ref.3) | copy-start | bytes 3932164
  236.5 1.0 copy-start.7
  256.3 1.0 copy-start.6

commit v4 on v3

--- a/solution.py
+++ b/solution.py
@@ -381,11 +381,23 @@
     return top * inverse + values * logistic * (rest * (2.0 * top + rest)) * (inverse * inverse)
 
 
-def collect_kernel(
-    cond_ref, film_ref, grads_ref, wc_ref,
-    total_ref, gwc_ref, gcond_ref,
-    cond_sib, act_all, film_sib, film_out, film_z, film_all,
-    mp_in, z_out, z_in, x_out, x_in, y_out, y_in, full,
+FLATS = 16
+STEPS = 64
+C = 256
+BLOCK = 256
+ROWS_A = 320
+ROWS_B = 192
+
+
+def finish_kernel(
+    cond_ref, wcond_ref, wc_ref, noise_in, actions_in, tsteps_ref, advantage_ref, roots_ref, table_ref,
+    win_in, wres_in, wmid_ref, wout_in, wtime_ref,
+    full_a, full_b, act_all, film_all, gcond_ref,
+    noise_ref, actions_ref, keep_ref, blend_ref, adv_ref, time_ref, wide_in, wide_res, wide_out, win_ref, wres_ref,
+    wout_ref, wout_t_ref, npad, cols, pad, mid, back, pre, res, unit1, act1, slope1, unit2, slope2, block, d_block, d_pred,
+    d_second, d_first, film, d_film, sum1, sum2, inv1, inv2, mean1, mean2,
+    cond_sib, film_ref, film_sib, film_out, film_z,
+    grads_a, grads_b, mp_a, mp_b, zo_a, zo_b, zi_a, zi_b, xo_a, xo_b, xi_a, xi_b, yi_a, yi_b,
     ms_sem, mr_sem, zs_sem, zr_sem, xs_sem, xr_sem, ys_sem, yr_sem,
 ):
     dp, seg, core = lax.axis_index("dp"), lax.axis_index("segment"), lax.axis_index("mp")
@@ -406,7 +418,6 @@
     for step in range(1, SIDE):
         for peer in (x_peer, y_peer, z_peer):
             pl.semaphore_signal(barrier, inc=1, device_id=peer(step), device_id_type=MESH)
-    pl.semaphore_wait(barrier, 10)
 
     def copy(src, dst, out_sem, in_sem, peer):
         return pltpu.make_async_remote_copy(
@@ -446,133 +457,6 @@
 
     here = pl.ds(pl.multiple_of(core * HALF, 128), HALF)
     there = pl.ds(pl.multiple_of(sibling * HALF, 128), HALF)
-    mine = pl.ds(pl.multiple_of(core * 512, 128), 512)
-    others = pl.ds(pl.multiple_of(sibling * 512, 128), 512)
-
-    to_sibling(0, film_ref, film_sib)
-    to_sibling(1, grads_ref.at[:, others, :], mp_in)
-    to_sibling(2, cond_ref.at[:, :, there], cond_sib)
-
-    arrive(film_sib, mr_sem.at[0])
-    film_out[...] = jnp.zeros_like(film_out)
-    for s in range(SIDE):
-        film_out[s, 0:2] = film_ref[0:2, 128 * s : 128 * (s + 1)]
-        film_out[s, 2:4] = film_sib[0:2, 128 * s : 128 * (s + 1)]
-    scatter(zs_sem, zr_sem, 0, film_out, film_z, seg, z_peer)
-    film_z[seg] = film_out[seg]
-
-    arrive(mp_in, mr_sem.at[1])
-    z_out[...] = (grads_ref[:, mine, :].astype(jnp.float32) + mp_in[...].astype(jnp.float32)).astype(jnp.bfloat16)
-    scatter(zs_sem, zr_sem, 1, z_out, z_in, seg, z_peer)
-    z_in[seg] = z_out[seg]
-
-    arrive(cond_sib, mr_sem.at[2])
-    rows = [cond_ref[j, 0:2, here] for j in range(MICRO)] + [cond_sib[j, 0:2] for j in range(MICRO)]
-    act_all[y, x] = mish_value(jnp.concatenate(rows, axis=0)).astype(jnp.bfloat16)
-    spread(xs_sem, xr_sem, 0, act_all.at[y], x, x_peer)
-
-    gathered(zr_sem, 0, film_z, seg)
-    rows = [film_z[j, 0:2] for j in range(MICRO)] + [film_z[j, 2:4] for j in range(MICRO)]
-    film_all[y, x] = jnp.concatenate(rows, axis=0).astype(jnp.bfloat16)
-    spread(xs_sem, xr_sem, 1, film_all.at[y], x, x_peer)
-
-    low = jnp.where(core == 0, film_ref[0:2], film_sib[0:2])
-    high = jnp.where(core == 0, film_sib[0:2], film_ref[0:2])
-    film_rows = jnp.concatenate([low, high, jnp.zeros((12, 512), jnp.float32)], axis=0).astype(jnp.bfloat16)
-    own_cond, sib_cond = cond_ref[seg, 0:2, here], cond_sib[seg, 0:2]
-    cond_rows = jnp.concatenate(
-        [jnp.where(core == 0, own_cond, sib_cond), jnp.where(core == 0, sib_cond, own_cond)], axis=0
-    )
-    back = lax.dot_general(film_rows, wc_ref[...], (((1,), (1,)), ((), ())), preferred_element_type=jnp.float32)
-    gcond_ref[...] = back[0:4] * mish_slope(cond_rows)
-
-    gathered(zr_sem, 1, z_in, seg)
-    x_out[...] = added(z_in).astype(jnp.bfloat16).reshape(x_out.shape)
-    scatter(xs_sem, xr_sem, 2, x_out, x_in, x, x_peer)
-    x_in[x] = x_out[x]
-
-    gathered(xr_sem, 0, act_all.at[y], x)
-    spread(ys_sem, yr_sem, 0, act_all, y, y_peer)
-    gathered(xr_sem, 1, film_all.at[y], x)
-    spread(ys_sem, yr_sem, 1, film_all, y, y_peer)
-
-    gathered(xr_sem, 2, x_in, x)
-    y_out[...] = added(x_in).astype(jnp.bfloat16).reshape(y_out.shape)
-    scatter(ys_sem, yr_sem, 2, y_out, y_in, y, y_peer)
-    y_in[y] = y_out[y]
-    gathered(yr_sem, 2, y_in, y)
-    full[core, x, y] = added(y_in).astype(jnp.bfloat16)
-    spread(ys_sem, yr_sem, 3, full.at[core, x], y, y_peer)
-    gathered(yr_sem, 3, full.at[core, x], y)
-    spread(xs_sem, xr_sem, 3, full.at[core], x, x_peer)
-
-    gathered(yr_sem, 0, act_all, y)
-    gathered(yr_sem, 1, film_all, y)
-
-    gathered(xr_sem, 3, full.at[core], x)
-    to_sibling(3, full.at[core], full.at[core])
-    gwc_ref[...] = lax.dot_general(
-        act_all[...].reshape(256, HALF), film_all[...].reshape(256, 128), (((0,), (0,)), ((), ())),
-        preferred_element_type=jnp.float32,
-    )
-    arrive(full.at[sibling], mr_sem.at[3])
-    total_ref[...] = full[...].astype(jnp.float32).reshape(total_ref.shape)
-    for one in started:
-        one.wait_send()
-
-
-def collect(cond, film, grads, w_cond):
-    vmem = pl.BlockSpec(memory_space=pltpu.VMEM)
-    dma = pltpu.SemaphoreType.DMA
-    bf16, f32 = jnp.bfloat16, jnp.float32
-    return pl.pallas_call(
-        collect_kernel,
-        out_shape=(
-            jax.ShapeDtypeStruct((1024, 128), f32),
-            jax.ShapeDtypeStruct((HALF, 128), f32),
-            jax.ShapeDtypeStruct((4, HALF), f32),
-        ),
-        in_specs=[vmem] * 4,
-        out_specs=(vmem, vmem, vmem),
-        scratch_shapes=[
-            pltpu.VMEM((MICRO, 8, HALF), f32),
-            pltpu.VMEM((SIDE, SIDE, 16, HALF), bf16),
-            pltpu.VMEM((8, 512), f32),
-            pltpu.VMEM((SIDE, 8, 128), f32),
-            pltpu.VMEM((SIDE, 8, 128), f32),
-            pltpu.VMEM((SIDE, SIDE, 16, 128), bf16),
-            pltpu.VMEM((SIDE, 512, 128), bf16),
-            pltpu.VMEM((SIDE, 512, 128), bf16),
-            pltpu.VMEM((SIDE, 512, 128), bf16),
-            pltpu.VMEM((SIDE, 128, 128), bf16),
-            pltpu.VMEM((SIDE, 128, 128), bf16),
-            pltpu.VMEM((SIDE, 32, 128), bf16),
-            pltpu.VMEM((SIDE, 32, 128), bf16),
-            pltpu.VMEM((2, SIDE, SIDE, 32, 128), bf16),
-            dma((4,)), dma((4,)),
-            dma((2, 3)), dma((2, 3)),
-            dma((4, 3)), dma((4, 3)),
-            dma((4, 3)), dma((4, 3)),
-        ],
-        compiler_params=pltpu.CompilerParams(
-            collective_id=1, has_side_effects=True, vmem_limit_bytes=32 * 2**20
-        ),
-    )(cond, film, grads, w_cond)
-
-
-FLATS = 16
-STEPS = 64
-C = 256
-BLOCK = 256
-
-
-def denoise_kernel(
-    film_cond_ref, noise_ref, actions_ref, keep_ref, blend_ref, adv_ref, time_ref,
-    win_ref, wres_ref, wmid_ref, wmid_t_ref, wout_ref, wout_t_ref, wtime_ref,
-    packed_ref, film_ref,
-    npad, cols, pad, mid, back, pre, res, unit1, act1, slope1, unit2, slope2, block, d_block, d_pred,
-    d_second, d_first, film, d_film, sum1, sum2, inv1, inv2, mean1, mean2,
-):
     bf16, f32 = jnp.bfloat16, jnp.float32
 
     def rows_of(f, size=STEPS):
@@ -598,24 +482,64 @@
     def dot(left, right):
         return jnp.dot(left, right, preferred_element_type=f32)
 
+    begin = 4 * seg + 2 * core
+    sample_at = lax.broadcasted_iota(jnp.int32, (8, 16), 1)
+
+    def column(ref):
+        pieces = []
+        for sample in range(2):
+            chosen = jnp.where(sample_at == begin + sample, ref[...].astype(f32), 0.0)
+            pieces.append(jnp.sum(chosen, axis=1, keepdims=True))
+        return jnp.broadcast_to(jnp.concatenate(pieces, axis=0), (FLATS, 128))
+
+    steps_at = column(tsteps_ref)
+    lane_at = lax.broadcasted_iota(jnp.int32, (FLATS, 128), 1).astype(f32)
+    picked = jnp.where(steps_at == lane_at, 1.0, 0.0)
+    keep_ref[...] = jnp.broadcast_to(jnp.sum(picked * roots_ref[0:1], axis=1, keepdims=True), (FLATS, 128))
+    blend_ref[...] = jnp.broadcast_to(jnp.sum(picked * roots_ref[1:2], axis=1, keepdims=True), (FLATS, 128))
+    adv_ref[...] = column(advantage_ref)
+    time_ref[...] = dot(picked.astype(bf16), table_ref[...]).astype(bf16)
+    for sample in range(2):
+        actions_ref[sample] = jnp.zeros((STEPS, 128), f32)
+        actions_ref[sample, :, 0:14] = actions_in[sample].astype(f32)
+
+    def widen(f):
+        noise_ref[rows_of(f)] = jnp.zeros((STEPS, 128), f32)
+        noise_ref[rows_of(f), 0:14] = noise_in[rows_of(f)].astype(f32)
+
+    each(widen)
+    wide_in[...] = jnp.zeros_like(wide_in)
+    wide_in[0:70] = win_in[...].astype(f32)
+    win_ref[...] = wide_in[...].astype(bf16)
+    wide_res[...] = jnp.zeros_like(wide_res)
+    wide_res[70:84] = wres_in[...].astype(f32)
+    wres_ref[...] = wide_res[...].astype(bf16)
+    wide_out[...] = jnp.zeros_like(wide_out)
+    wide_out[0:14] = wout_in[...].astype(f32)
+    wout_t_ref[...] = wide_out[...].astype(bf16)
+    wout_ref[...] = wide_out[...].T.astype(bf16)
+
     npad[...] = jnp.zeros_like(npad)
     pad[...] = jnp.zeros_like(pad)
 
     def make_cols(f):
-        sample = rows_of(f // 8)
-        noisy = keep_ref[one(f)] * actions_ref[sample].astype(f32) + blend_ref[one(f)] * noise_ref[rows_of(f)].astype(f32)
+        noisy = keep_ref[one(f)] * actions_ref[f // 8] + blend_ref[one(f)] * noise_ref[rows_of(f)]
         noisy = noisy.astype(bf16).astype(f32)
         npad[f, 8:72] = noisy
-        total = pltpu.roll(noisy, 114, 1)
+        total = pltpu.roll(noisy, 70, 1)
         for tap in range(5):
-            total = total + pltpu.roll(npad[f, 6 + tap : 70 + tap], 44 + 14 * tap, 1)
+            total = total + pltpu.roll(npad[f, 6 + tap : 70 + tap], 14 * tap, 1)
         cols[rows_of(f)] = total.astype(bf16)
 
     each(make_cols)
 
+    pl.semaphore_wait(barrier, 10)
+    to_sibling(3, cond_ref.at[:, :, there], cond_sib)
+
     time_film = dot(time_ref[...], wtime_ref[...])
-    top = jnp.broadcast_to(film_cond_ref[0:1], (8, 2 * C))
-    low = jnp.broadcast_to(film_cond_ref[1:2], (8, 2 * C))
+    film_cond = dot(mish_value(cond_ref[seg]).astype(bf16), wcond_ref[...])
+    top = jnp.broadcast_to(film_cond[0:1], (8, 2 * C))
+    low = jnp.broadcast_to(film_cond[1:2], (8, 2 * C))
     film[...] = jnp.concatenate([top, low], axis=0) + time_film
 
     def first_conv(b):
@@ -625,6 +549,11 @@
         res[rows] = dot(cols[rows], wres_ref[...])
 
     each(first_conv, 4)
+
+    arrive(cond_sib, mr_sem.at[3])
+    pairs = [cond_ref[j, 0:2, here] for j in range(MICRO)] + [cond_sib[j, 0:2] for j in range(MICRO)]
+    act_all[y, x] = mish_value(jnp.concatenate(pairs, axis=0)).astype(bf16)
+    spread(xs_sem, xr_sem, 0, act_all.at[y], x, x_peer)
 
     def centre(inverse):
         def total(f):
@@ -664,6 +593,9 @@
 
     each(first_act)
 
+    gathered(xr_sem, 0, act_all.at[y], x)
+    spread(ys_sem, yr_sem, 0, act_all, y, y_peer)
+
     def second_conv(b):
         rows = rows_of(b, BLOCK)
         pre[rows] = dot(mid[rows], wmid_ref[...])
@@ -682,7 +614,7 @@
 
     def errors(f, total):
         rows = rows_of(f)
-        error = dot(block[rows], wout_ref[...]) - noise_ref[rows].astype(f32)
+        error = dot(block[rows], wout_ref[...]) - noise_ref[rows]
         d_pred[rows] = (adv_ref[one(f)] * error * (2.0 / 896.0)).astype(bf16)
         return total + error * error
 
@@ -720,30 +652,6 @@
 
     each(second_back)
 
-    def mid_back(b):
-        rows = rows_of(b, BLOCK)
-        pre[rows] = dot(back[rows], wmid_t_ref[...])
-
-    each(mid_back, 4)
-
-    def film_back(f):
-        grad = pre[rows_of(f)]
-        d_film[one(f), 0:C] = jnp.sum(grad * act1[rows_of(f)], axis=0, keepdims=True)
-        d_film[one(f), C:] = jnp.sum(grad, axis=0, keepdims=True)
-
-    each(film_back)
-    film_ref[...] = jnp.zeros_like(film_ref)
-    film_ref[0:1] = jnp.sum(d_film[0:8], axis=0, keepdims=True)
-    film_ref[1:2] = jnp.sum(d_film[8:16], axis=0, keepdims=True)
-
-    act_back(lambda f: pre[rows_of(f)] * film[one(f), 0:C], unit1, slope1)
-
-    def first_back(f):
-        grad = inv1[one(f)] * (pre[rows_of(f)] - mean1[one(f)] - unit1[rows_of(f)] * mean2[one(f)])
-        d_first[rows_of(f)] = grad.astype(bf16)
-
-    each(first_back)
-
     def over_rows(left, right):
         return lax.dot_general(left, right, (((0,), (0,)), ((), ())), preferred_element_type=f32)
 
@@ -752,47 +660,199 @@
         for s in range(4):
             for half in range(2):
                 begin = 64 * (2 * tap + half)
-                packed_ref[s, begin : begin + 64] = grad[64 * s : 64 * (s + 1), 128 * half : 128 * (half + 1)]
+                grads_a[s, begin : begin + 64] = grad[64 * s : 64 * (s + 1), 128 * half : 128 * (half + 1)]
+
+    def ours(rows):
+        return pl.ds(pl.multiple_of(core * rows, 16), rows)
+
+    def theirs(rows):
+        return pl.ds(pl.multiple_of(sibling * rows, 16), rows)
+
+    def to_segments(number, grads, landed, out, slots, rows):
+        out[...] = (grads[:, ours(rows), :].astype(f32) + landed[...].astype(f32)).astype(bf16)
+        scatter(zs_sem, zr_sem, number, out, slots, seg, z_peer)
+        slots[seg] = out[seg]
+
+    def to_row(number, got, out, slots):
+        out[...] = added(got).astype(bf16).reshape(out.shape)
+        scatter(xs_sem, xr_sem, number, out, slots, x, x_peer)
+        slots[x] = out[x]
+
+    def to_column(number, got, slots):
+        slots[y] = added(got).astype(bf16)
+        spread(ys_sem, yr_sem, number, slots, y, y_peer)
+
+    to_sibling(1, grads_a.at[:, theirs(ROWS_A), :], mp_a)
+
+    def mid_back(b):
+        rows = rows_of(b, BLOCK)
+        pre[rows] = sum(
+            lax.dot_general(
+                back[rows, C * tap : C * (tap + 1)], wmid_ref[C * tap : C * (tap + 1)], (((1,), (1,)), ((), ())),
+                preferred_element_type=f32,
+            )
+            for tap in range(5)
+        )
+
+    each(mid_back, 4)
+
+    arrive(mp_a, mr_sem.at[1])
+    to_segments(1, grads_a, mp_a, zo_a, zi_a, ROWS_A)
+
+    def film_back(f):
+        grad = pre[rows_of(f)]
+        d_film[one(f), 0:C] = jnp.sum(grad * act1[rows_of(f)], axis=0, keepdims=True)
+        d_film[one(f), C:] = jnp.sum(grad, axis=0, keepdims=True)
+
+    each(film_back)
+    film_ref[...] = jnp.zeros_like(film_ref)
+    film_ref[0:1] = jnp.sum(d_film[0:8], axis=0, keepdims=True)
+    film_ref[1:2] = jnp.sum(d_film[8:16], axis=0, keepdims=True)
+
+    to_sibling(0, film_ref, film_sib)
+
+    act_back(lambda f: pre[rows_of(f)] * film[one(f), 0:C], unit1, slope1)
+
+    arrive(film_sib, mr_sem.at[0])
+    film_out[...] = jnp.zeros_like(film_out)
+    for s in range(SIDE):
+        film_out[s, 0:2] = film_ref[0:2, 128 * s : 128 * (s + 1)]
+        film_out[s, 2:4] = film_sib[0:2, 128 * s : 128 * (s + 1)]
+    scatter(zs_sem, zr_sem, 0, film_out, film_z, seg, z_peer)
+    film_z[seg] = film_out[seg]
+
+    def first_back(f):
+        grad = inv1[one(f)] * (pre[rows_of(f)] - mean1[one(f)] - unit1[rows_of(f)] * mean2[one(f)])
+        d_first[rows_of(f)] = grad.astype(bf16)
+
+    each(first_back)
+
     lane = lax.broadcasted_iota(jnp.int32, (C, 128), 1)
     inner = over_rows(d_first[...], cols[...])
     skip = over_rows(d_block[...], cols[...])
-    out = over_rows(block[...], d_pred[...])
+    out = pltpu.roll(over_rows(block[...], d_pred[...]), 84, 1)
     joined = jnp.where(lane < 70, inner, jnp.where(lane < 84, skip, jnp.where(lane < 98, out, err_sum))).astype(bf16)
     timed = over_rows(time_ref[...], d_film[...].astype(bf16)).astype(bf16)
     for s in range(4):
-        packed_ref[s, 640:704] = joined[64 * s : 64 * (s + 1)]
-        packed_ref[s, 704:960] = timed[:, 128 * s : 128 * (s + 1)]
-        packed_ref[s, 960:1024] = jnp.zeros((64, 128), bf16)
-
-
-def denoise(film_cond, tsteps, advantage, actions, noise, w_time, w_in, w_mid, w_res, w_out):
+        grads_b[s, 0:64] = joined[64 * s : 64 * (s + 1)]
+        grads_b[s, 64:320] = timed[:, 128 * s : 128 * (s + 1)]
+        grads_b[s, 320:384] = jnp.zeros((64, 128), bf16)
+    to_sibling(2, grads_b.at[:, theirs(ROWS_B), :], mp_b)
+
+    gathered(zr_sem, 1, zi_a, seg)
+    to_row(2, zi_a, xo_a, xi_a)
+    arrive(mp_b, mr_sem.at[2])
+    to_segments(2, grads_b, mp_b, zo_b, zi_b, ROWS_B)
+
+    gathered(zr_sem, 0, film_z, seg)
+    pairs = [film_z[j, 0:2] for j in range(MICRO)] + [film_z[j, 2:4] for j in range(MICRO)]
+    film_all[y, x] = jnp.concatenate(pairs, axis=0).astype(bf16)
+    spread(xs_sem, xr_sem, 1, film_all.at[y], x, x_peer)
+
+    gathered(xr_sem, 2, xi_a, x)
+    to_column(2, xi_a, yi_a)
+    gathered(zr_sem, 2, zi_b, seg)
+    to_row(3, zi_b, xo_b, xi_b)
+    gathered(xr_sem, 1, film_all.at[y], x)
+    spread(ys_sem, yr_sem, 1, film_all, y, y_peer)
+    gathered(yr_sem, 2, yi_a, y)
+    full_a[core, x] = added(yi_a).astype(bf16)
+    spread(xs_sem, xr_sem, 4, full_a.at[core], x, x_peer)
+    gathered(xr_sem, 3, xi_b, x)
+    to_column(3, xi_b, yi_b)
+
+    low = jnp.where(core == 0, film_ref[0:2], film_sib[0:2])
+    high = jnp.where(core == 0, film_sib[0:2], film_ref[0:2])
+    film_rows = jnp.concatenate([low, high, jnp.zeros((12, 512), jnp.float32)], axis=0).astype(jnp.bfloat16)
+    own_cond, sib_cond = cond_ref[seg, 0:2, here], cond_sib[seg, 0:2]
+    cond_rows = jnp.concatenate(
+        [jnp.where(core == 0, own_cond, sib_cond), jnp.where(core == 0, sib_cond, own_cond)], axis=0
+    )
+    back = lax.dot_general(film_rows, wc_ref[...], (((1,), (1,)), ((), ())), preferred_element_type=jnp.float32)
+    gcond_ref[...] = back[0:4] * mish_slope(cond_rows)
+
+    gathered(xr_sem, 4, full_a.at[core], x)
+    to_sibling(4, full_a.at[core], full_a.at[core])
+    gathered(yr_sem, 3, yi_b, y)
+    full_b[core, x] = added(yi_b).astype(bf16)
+    spread(xs_sem, xr_sem, 5, full_b.at[core], x, x_peer)
+    gathered(yr_sem, 0, act_all, y)
+    gathered(yr_sem, 1, film_all, y)
+    gathered(xr_sem, 5, full_b.at[core], x)
+    to_sibling(5, full_b.at[core], full_b.at[core])
+    arrive(full_a.at[sibling], mr_sem.at[4])
+    arrive(full_b.at[sibling], mr_sem.at[5])
+    for sent_copy in started:
+        sent_copy.wait_send()
+
+
+def unpack_kernel(full_a, full_b, act_all, film_all, back_ref, gin, gmid, gres, gout, gtime, gwc, gcond, loss):
+    f32 = jnp.float32
+    flat_a = full_a[...].astype(f32).reshape(640, 128)
+    for q in range(10):
+        gmid[:, 128 * q : 128 * (q + 1)] = flat_a[64 * q : 64 * (q + 1)]
+    flat_b = full_b[...].astype(f32).reshape(384, 128)
+    joined = flat_b[0:64]
+    turned = joined.T
+    gin[...] = joined[:, 0:70]
+    gres[...] = turned[70:84]
+    gout[...] = turned[84:98]
+    loss[...] = joined[0:1, 98:99] * (1.0 / 2048.0)
+    gtime[...] = flat_b[64:320]
+    gcond[...] = back_ref[...]
+    gwc[...] = lax.dot_general(
+        act_all[...].reshape(256, HALF), film_all[...].reshape(256, 128), (((0,), (0,)), ((), ())),
+        preferred_element_type=f32,
+    )
+
+
+def step_tables():
+    table = schedule()
+    roots = np.zeros((8, 128))
+    roots[0, :TSTEPS], roots[1, :TSTEPS] = np.sqrt(table), np.sqrt(1.0 - table)
+    half = C // 2
+    angles = np.arange(TSTEPS)[:, None] * np.exp(-math.log(10000.0) * np.arange(half) / (half - 1))[None]
+    embedded = np.concatenate([np.sin(angles), np.cos(angles)], axis=1)
+    times = np.zeros((128, C))
+    times[:TSTEPS] = embedded * np.tanh(np.log1p(np.exp(embedded)))
+    return jnp.asarray(roots, jnp.float32), jnp.asarray(times, jnp.float32).astype(jnp.bfloat16)
+
+
+def finish(cond, w_cond_full, w_cond, noise, actions, tsteps, advantage, w_in, w_res, w_mid, w_out, w_time):
     bf16, f32 = jnp.bfloat16, jnp.float32
-    flat = tsteps.reshape(FLATS, 1)
-    table = schedule()
-    picked = (flat == jnp.arange(TSTEPS, dtype=jnp.int32)[None]).astype(f32)
-    keep = jnp.sum(picked * jnp.asarray(np.sqrt(table), f32)[None], axis=1, keepdims=True)
-    blend = jnp.sum(picked * jnp.asarray(np.sqrt(1.0 - table), f32)[None], axis=1, keepdims=True)
-
-    def wide(values):
-        return jnp.broadcast_to(values, (FLATS, 128))
-
-    half_dim = w_time.shape[0] // 2
-    frequencies = jnp.exp(-math.log(10000.0) * jnp.arange(half_dim, dtype=f32) / (half_dim - 1))
-    angles = flat.astype(f32) * frequencies[None]
-    time_act = mish_value(jnp.concatenate([jnp.sin(angles), jnp.cos(angles)], axis=1)).astype(bf16)
-    noise_lanes = jnp.pad(noise.reshape(FLATS * STEPS, 14), ((0, 0), (84, 30)))
-    action_lanes = jnp.pad(actions.reshape(2 * STEPS, 14), ((0, 0), (84, 30)))
-    w_mid_t = w_mid.reshape(5, C, C).transpose(0, 2, 1).reshape(5 * C, C)
+    roots, times = step_tables()
     vmem = pl.BlockSpec(memory_space=pltpu.VMEM)
     flat_rows = FLATS * STEPS
     big, small = pltpu.VMEM((flat_rows, C), f32), pltpu.VMEM((FLATS, C), f32)
     big16 = pltpu.VMEM((flat_rows, C), bf16)
+    rows_a, rows_b = pltpu.VMEM((SIDE, ROWS_A, 128), bf16), pltpu.VMEM((SIDE, ROWS_B, 128), bf16)
+    part_a, part_b = pltpu.VMEM((SIDE, ROWS_A // SIDE, 128), bf16), pltpu.VMEM((SIDE, ROWS_B // SIDE, 128), bf16)
+    dma = pltpu.SemaphoreType.DMA
     return pl.pallas_call(
-        denoise_kernel,
-        out_shape=(jax.ShapeDtypeStruct((4, 1024, 128), bf16), jax.ShapeDtypeStruct((8, 2 * C), f32)),
+        finish_kernel,
+        out_shape=(
+            jax.ShapeDtypeStruct((2, SIDE, ROWS_A // SIDE, 128), bf16),
+            jax.ShapeDtypeStruct((2, SIDE, ROWS_B // SIDE, 128), bf16),
+            jax.ShapeDtypeStruct((SIDE, SIDE, 16, HALF), bf16),
+            jax.ShapeDtypeStruct((SIDE, SIDE, 16, 128), bf16),
+            jax.ShapeDtypeStruct((4, HALF), f32),
+        ),
         in_specs=[vmem] * 14,
-        out_specs=(vmem, vmem),
+        out_specs=(vmem,) * 5,
         scratch_shapes=[
+            pltpu.VMEM((flat_rows, 128), f32),
+            pltpu.VMEM((2, STEPS, 128), f32),
+            pltpu.VMEM((FLATS, 128), f32),
+            pltpu.VMEM((FLATS, 128), f32),
+            pltpu.VMEM((FLATS, 128), f32),
+            pltpu.VMEM((FLATS, C), bf16),
+            pltpu.VMEM((128, C), f32),
+            pltpu.VMEM((128, C), f32),
+            pltpu.VMEM((128, C), f32),
+            pltpu.VMEM((128, C), bf16),
+            pltpu.VMEM((128, C), bf16),
+            pltpu.VMEM((C, 128), bf16),
+            pltpu.VMEM((128, C), bf16),
             pltpu.VMEM((FLATS, 80, 128), f32),
             pltpu.VMEM((flat_rows, 128), bf16),
             pltpu.VMEM((FLATS, 80, C), f32),
@@ -805,44 +865,57 @@
             pltpu.VMEM((FLATS, 2 * C), f32),
             pltpu.VMEM((FLATS, 2 * C), f32),
             small, small, small, small, small, small,
+            pltpu.VMEM((MICRO, 8, HALF), f32),
+            pltpu.VMEM((8, 512), f32),
+            pltpu.VMEM((8, 512), f32),
+            pltpu.VMEM((SIDE, 8, 128), f32),
+            pltpu.VMEM((SIDE, 8, 128), f32),
+            pltpu.VMEM((SIDE, 2 * ROWS_A, 128), bf16),
+            pltpu.VMEM((SIDE, 2 * ROWS_B, 128), bf16),
+            rows_a, rows_b, rows_a, rows_b, rows_a, rows_b,
+            part_a, part_b, part_a, part_b, part_a, part_b,
+            dma((6,)), dma((6,)),
+            dma((3, 3)), dma((3, 3)),
+            dma((6, 3)), dma((6, 3)),
+            dma((4, 3)), dma((4, 3)),
         ],
-        compiler_params=pltpu.CompilerParams(vmem_limit_bytes=48 * 2**20),
+        compiler_params=pltpu.CompilerParams(
+            collective_id=1, has_side_effects=True, vmem_limit_bytes=48 * 2**20
+        ),
     )(
-        film_cond, noise_lanes, action_lanes, wide(keep), wide(blend), wide(advantage.reshape(FLATS, 1)), time_act,
-        jnp.pad(w_in, ((0, 58), (0, 0))), jnp.pad(w_res, ((70, 44), (0, 0))), w_mid, w_mid_t,
-        jnp.pad(w_out, ((0, 0), (84, 30))), jnp.pad(w_out.T, ((84, 30), (0, 0))), w_time,
+        cond, w_cond_full, w_cond, noise, actions, tsteps, advantage, roots, times, w_in, w_res, w_mid, w_out, w_time
     )
+
+
+def unpack(*arrays):
+    f32 = jnp.float32
+    vmem = pl.BlockSpec(memory_space=pltpu.VMEM)
+    shapes = ((64, 70), (64, 1280), (14, 64), (14, 64), (256, 128), (HALF, 128), (4, HALF), (1, 1))
+    return pl.pallas_call(
+        unpack_kernel,
+        out_shape=tuple(jax.ShapeDtypeStruct(shape, f32) for shape in shapes),
+        in_specs=[vmem] * 5,
+        out_specs=(vmem,) * 8,
+        compiler_params=pltpu.CompilerParams(vmem_limit_bytes=32 * 2**20),
+    )(*arrays)
 
 
 def body(
     trunk_in, norm_gain, w_gate, w_up, w_down, w_cond, w_time, w_in, w_mid, w_res, w_out,
     tsteps, advantage, actions, noise,
 ):
-    seg, core = lax.axis_index("segment"), lax.axis_index("mp")
     cond_all, w_cond_full = trunk(trunk_in, norm_gain, w_gate[0], w_up[0], w_down[0].T, w_cond)
-    cond = lax.dynamic_index_in_dim(cond_all, seg, 0, keepdims=False)[0:2]
-    cond_act = mish_value(cond).astype(jnp.bfloat16)
-    film_cond = jnp.dot(cond_act, w_cond_full, preferred_element_type=jnp.float32)
-    begin = 4 * seg + 2 * core
+    begin = 4 * lax.axis_index("segment") + 2 * lax.axis_index("mp")
 
     def own(values):
         return lax.dynamic_slice_in_dim(values, begin, 2, 0)
 
-    packed, d_film_cond = denoise(
-        film_cond, own(tsteps), own(advantage), own(actions), own(noise), w_time, w_in, w_mid, w_res, w_out
+    parts = finish(
+        cond_all, w_cond_full, w_cond, own(noise).reshape(FLATS * STEPS, 14), own(actions), tsteps.T, advantage.T,
+        w_in, w_res, w_mid, w_out.T, w_time,
     )
-    total, grad_w_cond, grad_cond = collect(cond_all, d_film_cond, packed, w_cond)
-    joined = total[640:704]
-    return (
-        joined[:, 0:70].T,
-        total[0:640].reshape(10, 64, 128).transpose(0, 2, 1).reshape(1280, 64),
-        joined[:, 70:84].T,
-        joined[:, 84:98],
-        total[704:960],
-        grad_w_cond,
-        grad_cond,
-        joined[0, 98:99] / 2048.0,
-    )
+    gin, gmid, gres, gout, gtime, gwc, gcond, loss = unpack(*parts)
+    return gin.T, gmid.T, gres, gout.T, gtime, gwc, gcond, loss.reshape(1)
 
 
 def solution(mesh):

time: 301 us -> 281 us (0.934)
  local copies, waits for them, and re-layouts: 15.4 us -> 4.15 us
  Pallas kernels: 280 us -> 276 us
    unnamed x38 -> x29, local copies, waits for them, and re-layouts: 9.96 us -> 3 us
    pallas_call x2, Pallas kernels: 54.9 us -> 50.6 us  [the longest x1 49.2 us: finish(): pl.pallas_call(finish_kernel, out_shape=(jax.ShapeDtypeStruct((2, SIDE, R...]
where the time goes in v4:
time: 281 us
  Pallas kernels  276 us (98%)
  local copies, waits for them, and re-layouts  4.15 us (1%)
    pallas_call x1, Pallas kernels, trunk(): pl.pallas_call(trunk_kernel, out_shape=(jax.ShapeDtypeStruct((MICRO, 8, D...  226 us
    pallas_call x1, Pallas kernels, finish(): pl.pallas_call(finish_kernel, out_shape=(jax.ShapeDtypeStruct((2, SIDE, R...  49.2 us

profile of v4, /device:TPU:1, one launch (start us, length us, event | category | flops | bytes accessed | tf_op | source)
XLA Modules:
  0.0 281.1 jit_solution(18396325867321231340)
XLA Ops:
  0.6 0.0 copy-start
  0.6 0.0 copy-start.1
  0.7 0.0 copy-start.2
  0.7 0.9 constant_dynamic-slice_fusion
  1.6 0.1 copy.27.actions_in
  1.7 0.0 copy-done
  1.7 0.2 copy.25
  2.0 0.0 copy-start.3
  2.0 1.1 copy-done.3
  3.0 0.0 copy-start.4
  3.0 1.1 copy-done.4
  4.1 0.0 copy-start.8
  4.1 0.7 copy-done.8
  4.8 0.0 copy-start.5
  4.8 0.0 copy-start.6
  4.8 0.0 copy-start.7
  4.8 0.0 copy-start.9
  4.8 0.0 copy-start.10
  4.8 0.0 copy-start.11
  4.8 0.0 copy-start.12
  4.8 0.0 copy-start.13
  4.8 225.5 %shard_map.224 = (f32[4,8,2560]{2,1,0:T(8,128)S(1)}, bf16[2560,512]{1,0:T(8,128)(2,1)}) custom-call(bf16[256,1280]{1,0:T(8,128)(2,1)} %x_ref.1, bf16[1,2560]{1,0:T(2,128)(2,1)S(1)} %copy-done.8, bf16[160,1792]{1,0:T(8,128)(2,1)S(1)} %bitcast.14, bf16[160,1792]{1,0:T(8,128)(2,1)S(1)} %bitcast.15, bf16[160,1792]{1,0:T(8,128)(2,1)} %bitcast.19, ...), custom_call_target="tpu_custom_call" | custom-call | tf_op jit(solution)/shard_map/pallas_call | solution.py:328
  230.4 0.0 copy-done.1
  230.4 0.0 copy-done.2
  230.4 0.0 copy-done.5
  230.4 0.0 copy-done.6
  230.4 0.0 copy-done.7
  230.4 0.0 copy-done.9
  230.5 0.0 copy-done.10
  230.5 0.0 copy-done.11
  230.5 0.0 copy-done.12
  230.5 0.0 copy-done.13
  230.5 49.2 %shard_map.225 = (bf16[2,4,80,128]{3,2,1,0:T(8,128)(2,1)S(1)}, bf16[2,4,48,128]{3,2,1,0:T(8,128)(2,1)S(1)}, bf16[4,4,16,1280]{3,2,1,0:T(8,128)(2,1)S(1)}, bf16[4...) custom-call(f32[4,8,2560]{2,1,0:T(8,128)S(1)} %get-tuple-element.23.cond_ref, bf16[2560,512]{1,0:T(8,128)(2,1)} %get-tuple-element.24.wcond_ref, ...), custom_call_target="tpu_custom_call" | custom-call | tf_op jit(solution)/shard_map/pallas_call | solution.py:831
  279.7 1.3 shard_map.226
  (1 shorter events, 0.0 us)
Async XLA Ops:
  0.6 1.1 copy-start
  0.6 229.7 %copy-start.1 = (bf16[1280,512]{1,0:T(8,128)(2,1)S(1)}, bf16[1280,512]{1,0:T(8,128)(2,1)}, u32[]{:S(2)}) copy-start(bf16[1280,512]{1,0:T(8,128)(2,1)} %wc_ref.3) | copy-start | bytes 3932164
  0.7 229.7 %copy-start.2 = (bf16[1280,256]{1,0:T(8,128)(2,1)S(1)}, bf16[1280,256]{1,0:T(8,128)(2,1)}, u32[]{:S(2)}) copy-start(bf16[1280,256]{1,0:T(8,128)(2,1)} %wmid_ref.1) | copy-start | bytes 1966084
  2.0 1.1 copy-start.3
  3.0 1.1 copy-start.4
  4.1 0.7 copy-start.8
  4.8 225.6 %copy-start.5 = (bf16[256,512]{1,0:T(8,128)(2,1)S(1)}, bf16[256,512]{1,0:T(8,128)(2,1)}, u32[]{:S(2)}) copy-start(bf16[256,512]{1,0:T(8,128)(2,1)} %wtime_ref.1) | copy-start | bytes 786436
  4.8 225.6 %copy-start.6 = (bf16[128,256]{1,0:T(8,128)(2,1)S(1)}, bf16[128,256]{1,0:T(8,128)(2,1)}, u32[]{:S(2)}) copy-start(bf16[128,256]{1,0:T(8,128)(2,1)} %constant.26.table_ref) | copy-start | bytes 196612
  4.8 225.6 %copy-start.7 = (bf16[70,256]{1,0:T(8,128)(2,1)S(1)}, bf16[70,256]{1,0:T(8,128)(2,1)}, u32[]{:S(2)}) copy-start(bf16[70,256]{1,0:T(8,128)(2,1)} %win_in.1) | copy-start | bytes 107524
  4.8 225.7 %copy-start.9 = (bf16[14,256]{1,0:T(8,128)(2,1)S(1)}, bf16[14,256]{1,0:T(8,128)(2,1)}, u32[]{:S(2)}) copy-start(bf16[14,256]{1,0:T(8,128)(2,1)} %wres_in.1) | copy-start | bytes 21508
  4.8 225.7 %copy-start.10 = (bf16[256,14]{0,1:T(8,128)(2,1)S(1)}, bf16[256,14]{0,1:T(8,128)(2,1)}, u32[]{:S(2)}) copy-start(bf16[256,14]{0,1:T(8,128)(2,1)} %param.27) | copy-start | bytes 21508
  4.8 225.7 %copy-start.11 = (s32[16,8]{0,1:T(8,128)S(1)}, s32[16,8]{0,1:T(8,128)}, u32[]{:S(2)}) copy-start(s32[16,8]{0,1:T(8,128)} %param.28) | copy-start | bytes 1540
  4.8 225.7 %copy-start.12 = (f32[16,8]{0,1:T(8,128)S(1)}, f32[16,8]{0,1:T(8,128)}, u32[]{:S(2)}) copy-start(f32[16,8]{0,1:T(8,128)} %param.29) | copy-start | bytes 1540
  4.8 225.7 %copy-start.13 = (f32[8,128]{1,0:T(8,128)S(1)}, f32[8,128]{1,0:T(8,128)}, u32[]{:S(2)}) copy-start(f32[8,128]{1,0:T(8,128)} %constant.20.clone.roots_ref) | copy-start | bytes 12292

commit v5 on v4

--- a/solution.py
+++ b/solution.py
@@ -397,7 +397,7 @@
     wout_ref, wout_t_ref, npad, cols, pad, mid, back, pre, res, unit1, act1, slope1, unit2, slope2, block, d_block, d_pred,
     d_second, d_first, film, d_film, sum1, sum2, inv1, inv2, mean1, mean2,
     cond_sib, film_ref, film_sib, film_out, film_z,
-    grads_a, grads_b, mp_a, mp_b, zo_a, zo_b, zi_a, zi_b, xo_a, xo_b, xi_a, xi_b, yi_a, yi_b,
+    grads_a, grads_b, mp_a, mp_b, zo_a, zo_b, zi_a, zi_b, xo_a, xi_a, yi_a, xi_b, yi_b,
     ms_sem, mr_sem, zs_sem, zr_sem, xs_sem, xr_sem, ys_sem, yr_sem,
 ):
     dp, seg, core = lax.axis_index("dp"), lax.axis_index("segment"), lax.axis_index("mp")
@@ -470,14 +470,20 @@
             body(f)
             return carry
 
-        lax.fori_loop(0, count, step, 0)
+        lax.fori_loop(0, count, step, 0, unroll=4 if count == FLATS else 2)
 
     lanes = lax.broadcasted_iota(jnp.int32, (C, C), 1)
     row_ids = lax.broadcasted_iota(jnp.int32, (C, C), 0)
-    same = jnp.where(lanes // 32 == row_ids // 32, 1.0 / 2048.0, 0.0).astype(f32)
+    same = jnp.where(lanes // 32 == row_ids // 32, 1.0 / 2048.0, 0.0).astype(bf16)
 
     def group_mean(values):
-        return jnp.dot(values, same, preferred_element_type=f32, precision=lax.Precision.HIGHEST)
+        high = values.astype(bf16)
+        rest = values - high.astype(f32)
+        middle = rest.astype(bf16)
+        low = (rest - middle.astype(f32)).astype(bf16)
+        count = values.shape[0]
+        sums = jnp.dot(jnp.concatenate([high, middle, low], axis=0), same, preferred_element_type=f32)
+        return sums[0:count] + (sums[count : 2 * count] + sums[2 * count : 3 * count])
 
     def dot(left, right):
         return jnp.dot(left, right, preferred_element_type=f32)
@@ -618,7 +624,7 @@
         d_pred[rows] = (adv_ref[one(f)] * error * (2.0 / 896.0)).astype(bf16)
         return total + error * error
 
-    err = lax.fori_loop(0, FLATS, errors, jnp.zeros((STEPS, 128), f32))
+    err = lax.fori_loop(0, FLATS, errors, jnp.zeros((STEPS, 128), f32), unroll=4)
     err_sum = jnp.sum(err) * (1.0 / 896.0)
 
     def from_pred(b):
@@ -637,8 +643,9 @@
             sum2[one(f)] = jnp.sum(grad * unit[rows_of(f)], axis=0, keepdims=True)
 
         each(totals)
-        mean1[...] = group_mean(sum1[...])
-        mean2[...] = group_mean(sum2[...])
+        means = group_mean(jnp.concatenate([sum1[...], sum2[...]], axis=0))
+        mean1[...] = means[0:FLATS]
+        mean2[...] = means[FLATS:]
 
     act_back(lambda f: pre[rows_of(f)], unit2, slope2)
 
@@ -752,7 +759,8 @@
     gathered(xr_sem, 2, xi_a, x)
     to_column(2, xi_a, yi_a)
     gathered(zr_sem, 2, zi_b, seg)
-    to_row(3, zi_b, xo_b, xi_b)
+    xi_b[x] = added(zi_b).astype(bf16)
+    spread(xs_sem, xr_sem, 3, xi_b, x, x_peer)
     gathered(xr_sem, 1, film_all.at[y], x)
     spread(ys_sem, yr_sem, 1, film_all, y, y_peer)
     gathered(yr_sem, 2, yi_a, y)
@@ -774,12 +782,10 @@
     gathered(xr_sem, 4, full_a.at[core], x)
     to_sibling(4, full_a.at[core], full_a.at[core])
     gathered(yr_sem, 3, yi_b, y)
-    full_b[core, x] = added(yi_b).astype(bf16)
-    spread(xs_sem, xr_sem, 5, full_b.at[core], x, x_peer)
+    full_b[core] = added(yi_b).astype(bf16)
+    to_sibling(5, full_b.at[core], full_b.at[core])
     gathered(yr_sem, 0, act_all, y)
     gathered(yr_sem, 1, film_all, y)
-    gathered(xr_sem, 5, full_b.at[core], x)
-    to_sibling(5, full_b.at[core], full_b.at[core])
     arrive(full_a.at[sibling], mr_sem.at[4])
     arrive(full_b.at[sibling], mr_sem.at[5])
     for sent_copy in started:
@@ -826,13 +832,13 @@
     big, small = pltpu.VMEM((flat_rows, C), f32), pltpu.VMEM((FLATS, C), f32)
     big16 = pltpu.VMEM((flat_rows, C), bf16)
     rows_a, rows_b = pltpu.VMEM((SIDE, ROWS_A, 128), bf16), pltpu.VMEM((SIDE, ROWS_B, 128), bf16)
-    part_a, part_b = pltpu.VMEM((SIDE, ROWS_A // SIDE, 128), bf16), pltpu.VMEM((SIDE, ROWS_B // SIDE, 128), bf16)
+    part_a = pltpu.VMEM((SIDE, ROWS_A // SIDE, 128), bf16)
     dma = pltpu.SemaphoreType.DMA
     return pl.pallas_call(
         finish_kernel,
         out_shape=(
             jax.ShapeDtypeStruct((2, SIDE, ROWS_A // SIDE, 128), bf16),
-            jax.ShapeDtypeStruct((2, SIDE, ROWS_B // SIDE, 128), bf16),
+            jax.ShapeDtypeStruct((2, ROWS_B, 128), bf16),
             jax.ShapeDtypeStruct((SIDE, SIDE, 16, HALF), bf16),
             jax.ShapeDtypeStruct((SIDE, SIDE, 16, 128), bf16),
             jax.ShapeDtypeStruct((4, HALF), f32),
@@ -873,10 +879,10 @@
             pltpu.VMEM((SIDE, 2 * ROWS_A, 128), bf16),
             pltpu.VMEM((SIDE, 2 * ROWS_B, 128), bf16),
             rows_a, rows_b, rows_a, rows_b, rows_a, rows_b,
-            part_a, part_b, part_a, part_b, part_a, part_b,
+            part_a, part_a, part_a, rows_b, rows_b,
             dma((6,)), dma((6,)),
             dma((3, 3)), dma((3, 3)),
-            dma((6, 3)), dma((6, 3)),
+            dma((5, 3)), dma((5, 3)),
             dma((4, 3)), dma((4, 3)),
         ],
         compiler_params=pltpu.CompilerParams(

time: 281 us -> 277 us (0.986)
  Pallas kernels: 276 us -> 271 us
    pallas_call x1, Pallas kernels: 49.2 us -> 44.5 us  [finish(): pl.pallas_call(finish_kernel, out_shape=(jax.ShapeDtypeStruct((2, SIDE, R...]
where the time goes in v5:
time: 277 us; the launch traced here: 276 us
  Pallas kernels  271 us (98%)
  local copies, waits for them, and re-layouts  4.15 us (1%)
    pallas_call x1, Pallas kernels, trunk(): pl.pallas_call(trunk_kernel, out_shape=(jax.ShapeDtypeStruct((MICRO, 8, D...  226 us
    pallas_call x1, Pallas kernels, finish(): pl.pallas_call(finish_kernel, out_shape=(jax.ShapeDtypeStruct((2, SIDE, R...  44.5 us

profile of v5, /device:TPU:1, one launch (start us, length us, event | category | flops | bytes accessed | tf_op | source)
XLA Modules:
  0.0 276.3 jit_solution(15304832315724025325)
XLA Ops:
  0.6 0.0 copy-start
  0.6 0.0 copy-start.1
  0.7 0.0 copy-start.2
  0.7 0.9 constant_dynamic-slice_fusion
  1.6 0.1 copy.27.actions_in
  1.7 0.0 copy-done
  1.7 0.2 copy.25
  2.0 0.0 copy-start.3
  2.0 1.1 copy-done.3
  3.0 0.0 copy-start.4
  3.0 1.1 copy-done.4
  4.1 0.0 copy-start.8
  4.1 0.7 copy-done.8
  4.8 0.0 copy-start.5
  4.8 0.0 copy-start.6
  4.8 0.0 copy-start.7
  4.8 0.0 copy-start.9
  4.8 0.0 copy-start.10
  4.8 0.0 copy-start.11
  4.8 0.0 copy-start.12
  4.8 0.0 copy-start.13
  4.8 225.5 %shard_map.224 = (f32[4,8,2560]{2,1,0:T(8,128)S(1)}, bf16[2560,512]{1,0:T(8,128)(2,1)}) custom-call(bf16[256,1280]{1,0:T(8,128)(2,1)} %x_ref.1, bf16[1,2560]{1,0:T(2,128)(2,1)S(1)} %copy-done.8, bf16[160,1792]{1,0:T(8,128)(2,1)S(1)} %bitcast.14, bf16[160,1792]{1,0:T(8,128)(2,1)S(1)} %bitcast.15, bf16[160,1792]{1,0:T(8,128)(2,1)} %bitcast.19, ...), custom_call_target="tpu_custom_call" | custom-call | tf_op jit(solution)/shard_map/pallas_call | solution.py:328
  230.4 0.0 copy-done.1
  230.4 0.0 copy-done.2
  230.4 0.0 copy-done.5
  230.4 0.0 copy-done.6
  230.4 0.0 copy-done.7
  230.4 0.0 copy-done.9
  230.5 0.0 copy-done.10
  230.5 0.0 copy-done.11
  230.5 0.0 copy-done.12
  230.5 0.0 copy-done.13
  230.5 44.5 %shard_map.225 = (bf16[2,4,80,128]{3,2,1,0:T(8,128)(2,1)S(1)}, bf16[2,192,128]{2,1,0:T(8,128)(2,1)S(1)}, bf16[4,4,16,1280]{3,2,1,0:T(8,128)(2,1)S(1)}, bf16[4,4,16,128]{3,2,1,0:T(8,128)(2,1)S(1)}, f32[4,1280]{1,0:T(4,128)S(1)}) custom-call(f32[4,8,2560]{2,1,0:T(8,128)S(1)} %get-tuple-element.23.cond_ref, bf16[2560,512]{1,0:T(8,128)(2,1)} %get-tuple-element.24.wcond_ref, ...), custom_call_target="tpu_custom_call" | custom-call | tf_op jit(solution)/shard_map/pallas_call | solution.py:837
  275.0 1.3 shard_map.226
  (1 shorter events, 0.0 us)
Async XLA Ops:
  0.6 1.1 copy-start
  0.6 229.7 %copy-start.1 = (bf16[1280,512]{1,0:T(8,128)(2,1)S(1)}, bf16[1280,512]{1,0:T(8,128)(2,1)}, u32[]{:S(2)}) copy-start(bf16[1280,512]{1,0:T(8,128)(2,1)} %wc_ref.3) | copy-start | bytes 3932164
  0.7 229.7 %copy-start.2 = (bf16[1280,256]{1,0:T(8,128)(2,1)S(1)}, bf16[1280,256]{1,0:T(8,128)(2,1)}, u32[]{:S(2)}) copy-start(bf16[1280,256]{1,0:T(8,128)(2,1)} %wmid_ref.1) | copy-start | bytes 1966084
  2.0 1.1 copy-start.3
  3.0 1.1 copy-start.4
  4.1 0.7 copy-start.8
  4.8 225.6 %copy-start.5 = (bf16[256,512]{1,0:T(8,128)(2,1)S(1)}, bf16[256,512]{1,0:T(8,128)(2,1)}, u32[]{:S(2)}) copy-start(bf16[256,512]{1,0:T(8,128)(2,1)} %wtime_ref.1) | copy-start | bytes 786436
  4.8 225.6 %copy-start.6 = (bf16[128,256]{1,0:T(8,128)(2,1)S(1)}, bf16[128,256]{1,0:T(8,128)(2,1)}, u32[]{:S(2)}) copy-start(bf16[128,256]{1,0:T(8,128)(2,1)} %constant.26.table_ref) | copy-start | bytes 196612
  4.8 225.6 %copy-start.7 = (bf16[70,256]{1,0:T(8,128)(2,1)S(1)}, bf16[70,256]{1,0:T(8,128)(2,1)}, u32[]{:S(2)}) copy-start(bf16[70,256]{1,0:T(8,128)(2,1)} %win_in.1) | copy-start | bytes 107524
  4.8 225.7 %copy-start.9 = (bf16[14,256]{1,0:T(8,128)(2,1)S(1)}, bf16[14,256]{1,0:T(8,128)(2,1)}, u32[]{:S(2)}) copy-start(bf16[14,256]{1,0:T(8,128)(2,1)} %wres_in.1) | copy-start | bytes 21508
  4.8 225.7 %copy-start.10 = (bf16[256,14]{0,1:T(8,128)(2,1)S(1)}, bf16[256,14]{0,1:T(8,128)(2,1)}, u32[]{:S(2)}) copy-start(bf16[256,14]{0,1:T(8,128)(2,1)} %param.27) | copy-start | bytes 21508
  4.8 225.7 %copy-start.11 = (s32[16,8]{0,1:T(8,128)S(1)}, s32[16,8]{0,1:T(8,128)}, u32[]{:S(2)}) copy-start(s32[16,8]{0,1:T(8,128)} %param.28) | copy-start | bytes 1540
  4.8 225.7 %copy-start.12 = (f32[16,8]{0,1:T(8,128)S(1)}, f32[16,8]{0,1:T(8,128)}, u32[]{:S(2)}) copy-start(f32[16,8]{0,1:T(8,128)} %param.29) | copy-start | bytes 1540
  4.8 225.7 %copy-start.13 = (f32[8,128]{1,0:T(8,128)S(1)}, f32[8,128]{1,0:T(8,128)}, u32[]{:S(2)}) copy-start(f32[8,128]{1,0:T(8,128)} %constant.20.clone.roots_ref) | copy-start | bytes 12292

commit v6 on v5

--- a/solution.py
+++ b/solution.py
@@ -158,7 +158,6 @@
     kept = pltpu.make_async_copy(wc_ref, here_rows, own_sem.at[7])
     kept.start()
     own.append(kept)
-    cond_ref[...] = jnp.zeros_like(cond_ref)
 
     for chunk in chunks:
         for number in (0, 1):
@@ -328,7 +327,7 @@
     return pl.pallas_call(
         trunk_kernel,
         out_shape=(
-            jax.ShapeDtypeStruct((MICRO, 8, D), jnp.float32),
+            jax.ShapeDtypeStruct((MICRO, 2, D), jnp.float32),
             jax.ShapeDtypeStruct((D, w_cond.shape[1]), bf16),
         ),
         in_specs=[anywhere, vmem, anywhere, anywhere, anywhere, anywhere],
@@ -543,7 +542,8 @@
     to_sibling(3, cond_ref.at[:, :, there], cond_sib)
 
     time_film = dot(time_ref[...], wtime_ref[...])
-    film_cond = dot(mish_value(cond_ref[seg]).astype(bf16), wcond_ref[...])
+    own_pair = jnp.concatenate([mish_value(cond_ref[seg]), jnp.zeros((6, D), f32)], axis=0)
+    film_cond = dot(own_pair.astype(bf16), wcond_ref[...])
     top = jnp.broadcast_to(film_cond[0:1], (8, 2 * C))
     low = jnp.broadcast_to(film_cond[1:2], (8, 2 * C))
     film[...] = jnp.concatenate([top, low], axis=0) + time_film
@@ -871,7 +871,7 @@
             pltpu.VMEM((FLATS, 2 * C), f32),
             pltpu.VMEM((FLATS, 2 * C), f32),
             small, small, small, small, small, small,
-            pltpu.VMEM((MICRO, 8, HALF), f32),
+            pltpu.VMEM((MICRO, 2, HALF), f32),
             pltpu.VMEM((8, 512), f32),
             pltpu.VMEM((8, 512), f32),
             pltpu.VMEM((SIDE, 8, 128), f32),

time: 277 us -> 272 us (0.982)
  Pallas kernels: 271 us -> 266 us
    pallas_call x1, Pallas kernels: 44.5 us -> 41.7 us  [finish(): pl.pallas_call(finish_kernel, out_shape=(jax.ShapeDtypeStruct((2, SIDE, R...]
where the time goes in v6:
time: 272 us
  Pallas kernels  266 us (98%)
  local copies, waits for them, and re-layouts  5.21 us (2%)
    pallas_call x1, Pallas kernels, trunk(): pl.pallas_call(trunk_kernel, out_shape=(jax.ShapeDtypeStruct((MICRO, 2, D...  223 us
    pallas_call x1, Pallas kernels, finish(): pl.pallas_call(finish_kernel, out_shape=(jax.ShapeDtypeStruct((2, SIDE, R...  41.7 us

profile of v6, /device:TPU:1, one launch (start us, length us, event | category | flops | bytes accessed | tf_op | source)
XLA Modules:
  0.0 271.8 jit_solution(16494354319476203001)
XLA Ops:
  0.6 0.0 copy-start
  0.6 0.0 copy-start.1
  0.7 0.0 copy-start.2
  0.7 0.9 constant_dynamic-slice_fusion
  1.6 0.1 copy.27.actions_in
  1.7 0.0 copy-done
  1.7 0.2 copy.25
  2.0 0.0 copy-start.3
  2.0 1.1 copy-done.3
  3.0 0.0 copy-start.4
  3.0 1.1 copy-done.4
  4.1 0.0 copy-start.5
  4.1 1.1 copy-done.5
  5.1 0.0 copy-start.9
  5.1 0.7 copy-done.9
  5.8 0.0 copy-start.6
  5.8 0.0 copy-start.7
  5.9 0.0 copy-start.8
  5.9 0.0 copy-start.10
  5.9 0.0 copy-start.11
  5.9 0.0 copy-start.12
  5.9 0.0 copy-start.13
  5.9 0.0 copy-start.14
  5.9 222.8 %shard_map.224 = (f32[4,2,2560]{2,1,0:T(2,128)S(1)}, bf16[2560,512]{1,0:T(8,128)(2,1)}) custom-call(bf16[256,1280]{1,0:T(8,128)(2,1)} %x_ref.1, bf16[1,2560]{1,0:T(2,128)(2,1)S(1)} %copy-done.9, bf16[160,1792]{1,0:T(8,128)(2,1)S(1)} %bitcast.14, bf16[160,1792]{1,0:T(8,128)(2,1)S(1)} %bitcast.15, bf16[160,1792]{1,0:T(8,128)(2,1)S(1)} %bitcast.16, ...), custom_call_target="tpu_custom_call" | custom-call | tf_op jit(solution)/shard_map/pallas_call | solution.py:327
  228.7 0.0 copy-done.1
  228.8 0.0 copy-done.2
  228.8 0.0 copy-done.6
  228.8 0.0 copy-done.7
  228.8 0.0 copy-done.8
  228.8 0.0 copy-done.10
  228.8 0.0 copy-done.11
  228.8 0.0 copy-done.12
  228.8 0.0 copy-done.13
  228.8 0.0 copy-done.14
  228.8 41.7 %shard_map.225 = (bf16[2,4,80,128]{3,2,1,0:T(8,128)(2,1)S(1)}, bf16[2,192,128]{2,1,0:T(8,128)(2,1)S(1)}, bf16[4,4,16,1280]{3,2,1,0:T(8,128)(2,1)S(1)}, bf16[4,4,16,128]{3,2,1,0:T(8,128)(2,1)S(1)}, f32[4,1280]{1,0:T(4,128)S(1)}) custom-call(f32[4,2,2560]{2,1,0:T(2,128)S(1)} %get-tuple-element.23.cond_ref, bf16[2560,512]{1,0:T(8,128)(2,1)} %get-tuple-element.24.wcond_ref, ...), custom_call_target="tpu_custom_call" | custom-call | tf_op jit(solution)/shard_map/pallas_call | solution.py:837
  270.5 1.3 shard_map.226
  (1 shorter events, 0.0 us)
Async XLA Ops:
  0.6 1.1 copy-start
  0.6 228.1 %copy-start.1 = (bf16[1280,512]{1,0:T(8,128)(2,1)S(1)}, bf16[1280,512]{1,0:T(8,128)(2,1)}, u32[]{:S(2)}) copy-start(bf16[1280,512]{1,0:T(8,128)(2,1)} %wc_ref.3) | copy-start | bytes 3932164
  0.7 228.1 %copy-start.2 = (bf16[1280,256]{1,0:T(8,128)(2,1)S(1)}, bf16[1280,256]{1,0:T(8,128)(2,1)}, u32[]{:S(2)}) copy-start(bf16[1280,256]{1,0:T(8,128)(2,1)} %wmid_ref.1) | copy-start | bytes 1966084
  2.0 1.1 copy-start.3
  3.0 1.1 copy-start.4
  4.1 1.1 copy-start.5
  5.1 0.7 copy-start.9
  5.8 222.9 %copy-start.6 = (bf16[256,512]{1,0:T(8,128)(2,1)S(1)}, bf16[256,512]{1,0:T(8,128)(2,1)}, u32[]{:S(2)}) copy-start(bf16[256,512]{1,0:T(8,128)(2,1)} %wtime_ref.1) | copy-start | bytes 786436
  5.8 222.9 %copy-start.7 = (bf16[128,256]{1,0:T(8,128)(2,1)S(1)}, bf16[128,256]{1,0:T(8,128)(2,1)}, u32[]{:S(2)}) copy-start(bf16[128,256]{1,0:T(8,128)(2,1)} %constant.26.table_ref) | copy-start | bytes 196612
  5.9 222.9 %copy-start.8 = (bf16[70,256]{1,0:T(8,128)(2,1)S(1)}, bf16[70,256]{1,0:T(8,128)(2,1)}, u32[]{:S(2)}) copy-start(bf16[70,256]{1,0:T(8,128)(2,1)} %win_in.1) | copy-start | bytes 107524
  5.9 222.9 %copy-start.10 = (bf16[14,256]{1,0:T(8,128)(2,1)S(1)}, bf16[14,256]{1,0:T(8,128)(2,1)}, u32[]{:S(2)}) copy-start(bf16[14,256]{1,0:T(8,128)(2,1)} %wres_in.1) | copy-start | bytes 21508
  5.9 222.9 %copy-start.11 = (bf16[256,14]{0,1:T(8,128)(2,1)S(1)}, bf16[256,14]{0,1:T(8,128)(2,1)}, u32[]{:S(2)}) copy-start(bf16[256,14]{0,1:T(8,128)(2,1)} %param.27) | copy-start | bytes 21508
  5.9 222.9 %copy-start.12 = (s32[16,8]{0,1:T(8,128)S(1)}, s32[16,8]{0,1:T(8,128)}, u32[]{:S(2)}) copy-start(s32[16,8]{0,1:T(8,128)} %param.28) | copy-start | bytes 1540
  5.9 222.9 %copy-start.13 = (f32[16,8]{0,1:T(8,128)S(1)}, f32[16,8]{0,1:T(8,128)}, u32[]{:S(2)}) copy-start(f32[16,8]{0,1:T(8,128)} %param.29) | copy-start | bytes 1540
  5.9 222.9 %copy-start.14 = (f32[8,128]{1,0:T(8,128)S(1)}, f32[8,128]{1,0:T(8,128)}, u32[]{:S(2)}) copy-start(f32[8,128]{1,0:T(8,128)} %constant.20.clone.roots_ref) | copy-start | bytes 12292

commit v7 on v6

--- a/solution.py
+++ b/solution.py
@@ -469,7 +469,7 @@
             body(f)
             return carry
 
-        lax.fori_loop(0, count, step, 0, unroll=4 if count == FLATS else 2)
+        lax.fori_loop(0, count, step, 0, unroll=8 if count == FLATS else 4)
 
     lanes = lax.broadcasted_iota(jnp.int32, (C, C), 1)
     row_ids = lax.broadcasted_iota(jnp.int32, (C, C), 0)
@@ -624,7 +624,7 @@
         d_pred[rows] = (adv_ref[one(f)] * error * (2.0 / 896.0)).astype(bf16)
         return total + error * error
 
-    err = lax.fori_loop(0, FLATS, errors, jnp.zeros((STEPS, 128), f32), unroll=4)
+    err = lax.fori_loop(0, FLATS, errors, jnp.zeros((STEPS, 128), f32), unroll=8)
     err_sum = jnp.sum(err) * (1.0 / 896.0)
 
     def from_pred(b):

time: 272 us -> 272 us (level)
  no operation moved by 1% of the time
where the time goes in v7:
time: 272 us; the launch traced here: 271 us
  Pallas kernels  265 us (97%)
  local copies, waits for them, and re-layouts  5.21 us (2%)
    pallas_call x1, Pallas kernels, trunk(): pl.pallas_call(trunk_kernel, out_shape=(jax.ShapeDtypeStruct((MICRO, 2, D...  223 us
    pallas_call x1, Pallas kernels, finish(): pl.pallas_call(finish_kernel, out_shape=(jax.ShapeDtypeStruct((2, SIDE, R...  41 us

profile of v7, /device:TPU:1, one launch (start us, length us, event | category | flops | bytes accessed | tf_op | source)
XLA Modules:
  0.0 271.2 jit_solution(16364399499930922389)
XLA Ops:
  0.6 0.0 copy-start
  0.6 0.0 copy-start.1
  0.7 0.0 copy-start.2
  0.7 0.9 constant_dynamic-slice_fusion
  1.6 0.1 copy.27.actions_in
  1.7 0.0 copy-done
  1.7 0.2 copy.25
  2.0 0.0 copy-start.3
  2.0 1.1 copy-done.3
  3.0 0.0 copy-start.4
  3.0 1.1 copy-done.4
  4.1 0.0 copy-start.5
  4.1 1.1 copy-done.5
  5.1 0.0 copy-start.9
  5.1 0.7 copy-done.9
  5.8 0.0 copy-start.6
  5.8 0.0 copy-start.7
  5.9 0.0 copy-start.8
  5.9 0.0 copy-start.10
  5.9 0.0 copy-start.11
  5.9 0.0 copy-start.12
  5.9 0.0 copy-start.13
  5.9 0.0 copy-start.14
  5.9 222.8 %shard_map.224 = (f32[4,2,2560]{2,1,0:T(2,128)S(1)}, bf16[2560,512]{1,0:T(8,128)(2,1)}) custom-call(bf16[256,1280]{1,0:T(8,128)(2,1)} %x_ref.1, bf16[1,2560]{1,0:T(2,128)(2,1)S(1)} %copy-done.9, bf16[160,1792]{1,0:T(8,128)(2,1)S(1)} %bitcast.14, bf16[160,1792]{1,0:T(8,128)(2,1)S(1)} %bitcast.15, bf16[160,1792]{1,0:T(8,128)(2,1)S(1)} %bitcast.16, ...), custom_call_target="tpu_custom_call" | custom-call | tf_op jit(solution)/shard_map/pallas_call | solution.py:327
  228.7 0.0 copy-done.1
  228.8 0.0 copy-done.2
  228.8 0.0 copy-done.6
  228.8 0.0 copy-done.7
  228.8 0.0 copy-done.8
  228.8 0.0 copy-done.10
  228.8 0.0 copy-done.11
  228.8 0.0 copy-done.12
  228.8 0.0 copy-done.13
  228.8 0.0 copy-done.14
  228.8 41.0 %shard_map.225 = (bf16[2,4,80,128]{3,2,1,0:T(8,128)(2,1)S(1)}, bf16[2,192,128]{2,1,0:T(8,128)(2,1)S(1)}, bf16[4,4,16,1280]{3,2,1,0:T(8,128)(2,1)S(1)}, bf16[4,4,16,128]{3,2,1,0:T(8,128)(2,1)S(1)}, f32[4,1280]{1,0:T(4,128)S(1)}) custom-call(f32[4,2,2560]{2,1,0:T(2,128)S(1)} %get-tuple-element.23.cond_ref, bf16[2560,512]{1,0:T(8,128)(2,1)} %get-tuple-element.24.wcond_ref, ...), custom_call_target="tpu_custom_call" | custom-call | tf_op jit(solution)/shard_map/pallas_call | solution.py:837
  269.9 1.3 shard_map.226
  (1 shorter events, 0.0 us)
Async XLA Ops:
  0.6 1.1 copy-start
  0.6 228.1 %copy-start.1 = (bf16[1280,512]{1,0:T(8,128)(2,1)S(1)}, bf16[1280,512]{1,0:T(8,128)(2,1)}, u32[]{:S(2)}) copy-start(bf16[1280,512]{1,0:T(8,128)(2,1)} %wc_ref.3) | copy-start | bytes 3932164
  0.7 228.1 %copy-start.2 = (bf16[1280,256]{1,0:T(8,128)(2,1)S(1)}, bf16[1280,256]{1,0:T(8,128)(2,1)}, u32[]{:S(2)}) copy-start(bf16[1280,256]{1,0:T(8,128)(2,1)} %wmid_ref.1) | copy-start | bytes 1966084
  2.0 1.1 copy-start.3
  3.0 1.1 copy-start.4
  4.1 1.1 copy-start.5
  5.1 0.7 copy-start.9
  5.8 222.9 %copy-start.6 = (bf16[256,512]{1,0:T(8,128)(2,1)S(1)}, bf16[256,512]{1,0:T(8,128)(2,1)}, u32[]{:S(2)}) copy-start(bf16[256,512]{1,0:T(8,128)(2,1)} %wtime_ref.1) | copy-start | bytes 786436
  5.8 222.9 %copy-start.7 = (bf16[128,256]{1,0:T(8,128)(2,1)S(1)}, bf16[128,256]{1,0:T(8,128)(2,1)}, u32[]{:S(2)}) copy-start(bf16[128,256]{1,0:T(8,128)(2,1)} %constant.26.table_ref) | copy-start | bytes 196612
  5.9 222.9 %copy-start.8 = (bf16[70,256]{1,0:T(8,128)(2,1)S(1)}, bf16[70,256]{1,0:T(8,128)(2,1)}, u32[]{:S(2)}) copy-start(bf16[70,256]{1,0:T(8,128)(2,1)} %win_in.1) | copy-start | bytes 107524
  5.9 222.9 %copy-start.10 = (bf16[14,256]{1,0:T(8,128)(2,1)S(1)}, bf16[14,256]{1,0:T(8,128)(2,1)}, u32[]{:S(2)}) copy-start(bf16[14,256]{1,0:T(8,128)(2,1)} %wres_in.1) | copy-start | bytes 21508
  5.9 222.9 %copy-start.11 = (bf16[256,14]{0,1:T(8,128)(2,1)S(1)}, bf16[256,14]{0,1:T(8,128)(2,1)}, u32[]{:S(2)}) copy-start(bf16[256,14]{0,1:T(8,128)(2,1)} %param.27) | copy-start | bytes 21508
  5.9 222.9 %copy-start.12 = (s32[16,8]{0,1:T(8,128)S(1)}, s32[16,8]{0,1:T(8,128)}, u32[]{:S(2)}) copy-start(s32[16,8]{0,1:T(8,128)} %param.28) | copy-start | bytes 1540
  5.9 222.9 %copy-start.13 = (f32[16,8]{0,1:T(8,128)S(1)}, f32[16,8]{0,1:T(8,128)}, u32[]{:S(2)}) copy-start(f32[16,8]{0,1:T(8,128)} %param.29) | copy-start | bytes 1540
  5.9 222.9 %copy-start.14 = (f32[8,128]{1,0:T(8,128)S(1)}, f32[8,128]{1,0:T(8,128)}, u32[]{:S(2)}) copy-start(f32[8,128]{1,0:T(8,128)} %constant.20.clone.roots_ref) | copy-start | bytes 12292
